TPU v7x, 512 devices: a whole 4x8x8 slice. The times are simulated.
512 devices in a mesh: tm: 16 (over z, core), space: 32 (over x, y).
Axes of the slice: x: 4, y: 8, z: 8, core: 2. Of those that a mesh axis runs over, the one named last changes fastest.
Arguments:
- right_side: float32 [1536, 8192], P('tm', 'space'), may hold values from -6 to 6
- obs_precision: float32 [1536, 8192], P('tm', 'space'), may hold values from 0.2 to 2
- mass_blocks: bfloat16 [64, 4, 128, 128], P('space')
- stiff_blocks: bfloat16 [64, 4, 128, 128], P('space')
- block_pattern: int32 [64, 4], P('space'), may hold values from 0 to 3, as said below
- send_lists: int32 [32, 2, 1], replicated, may hold values from 0 to 1, as said below
- time_bands: float32 [2, 3, 1536], replicated, as said below
Outputs:
- solution: float32 [1536, 8192], P('tm', 'space')
- residual: float32 [1536, 8192], P('tm', 'space')
Inputs may be any that keep to these rules, and one draw needn't show every extreme that they name: `block_pattern`: column 0 of block row b holds b mod 2; columns 2 and 3 hold local numbers; column 1 holds a code of a neighbour's list. The pattern is mirrored: if row b names block c in column j, row c names block b in column j. `send_lists`: the two lists of a partition together hold each of its local block numbers once. `time_bands`: per row and matrix, band 0 exceeds twice the sum of the magnitudes of bands 1 and 2.
All inputs are finite; a program needn't handle non-finite values.
Results may differ from a plain program's by a relative error of at most 0.0003.
Values sent between devices are 32-bit elements; how exact they have to be, the bound alone decides.
No kernel may reach another device: no remote copies, remote signals or barrier semaphores. Data moves between devices by JAX's collectives and lax.ppermute only.
A program may use at most 64 MiB of HBM per device.

v0:
```python
import jax
import jax.numpy as jnp
from jax import lax
from jax.sharding import PartitionSpec as P

ITERS = 4


def padded_2(array, sides, width, wrap):
    for axis, dim in sides:
        devices, length = (lax.axis_size(axis), array.shape[dim])
        up = [(i, (i + 1) % devices) for i in range(devices if wrap else devices - 1)]
        down = [(j, i) for i, j in up]
        last = lax.slice_in_dim(array, length - width, length, axis=dim)
        first = lax.slice_in_dim(array, 0, width, axis=dim)
        before = lax.ppermute(last, axis, up)
        after = lax.ppermute(first, axis, down)
        array = jnp.concatenate([before, array, after], axis=dim)
    return array


def band_apply(band_rows, padded, length):
    centre = band_rows[:, 2 : length + 2]
    result = centre[0][:, None] * padded[2 : length + 2]
    result = result + centre[1][:, None] * padded[3 : length + 3]
    result = result + band_rows[1, 1 : length + 1][:, None] * padded[1 : length + 1]
    result = result + centre[2][:, None] * padded[4 : length + 4]
    result = result + band_rows[2, 0:length][:, None] * padded[0:length]
    return result


def operate(
    vector, obs_precision, mass_blocks, stiff_blocks, block_pattern, send_lists, band_padded
):
    time_rows, node_count = vector.shape
    block_width = mass_blocks.shape[-1]
    block_rows = node_count // block_width
    half_count = send_lists.shape[2]
    node_tiles = vector.reshape(time_rows, block_rows, block_width)
    position = lax.axis_index("space")
    part_count = lax.axis_size("space")
    extended = padded_2(node_tiles, (("space", 1),), block_rows, True)
    lower_part = (position - 1) % part_count
    upper_part = (position + 1) % part_count
    lower_list = lax.dynamic_index_in_dim(send_lists, lower_part, 0, keepdims=False)[1]
    upper_list = lax.dynamic_index_in_dim(send_lists, upper_part, 0, keepdims=False)[0]
    lower_code = jnp.clip(block_pattern - block_rows, 0, half_count - 1)
    upper_code = jnp.clip(block_pattern - block_rows - half_count, 0, half_count - 1)
    inner = jnp.where(
        block_pattern < block_rows + half_count,
        lower_list[lower_code],
        2 * block_rows + upper_list[upper_code],
    )
    slot_index = jnp.where(block_pattern < block_rows, block_rows + block_pattern, inner)
    gathered = extended[:, slot_index]
    mass_part = jnp.einsum(
        "tbjc,bjrc->tbr", gathered, mass_blocks.astype(jnp.float32), precision=lax.Precision.HIGHEST
    )
    stiff_part = jnp.einsum(
        "tbjc,bjrc->tbr",
        gathered,
        stiff_blocks.astype(jnp.float32),
        precision=lax.Precision.HIGHEST,
    )
    stacked = jnp.stack(
        [mass_part.reshape(time_rows, node_count), stiff_part.reshape(time_rows, node_count)]
    )
    padded = padded_2(stacked, (("tm", 1),), 2, False)
    start = lax.axis_index("tm") * time_rows
    coeffs = lax.dynamic_slice_in_dim(band_padded, start, time_rows + 4, 2)
    result = band_apply(coeffs[0], padded[0], time_rows) + band_apply(
        coeffs[1], padded[1], time_rows
    )
    return result + obs_precision * vector


def shards(
    right_side, obs_precision, mass_blocks, stiff_blocks, block_pattern, send_lists, time_bands
):
    time_rows = right_side.shape[0]
    band_padded = jnp.pad(time_bands, ((0, 0), (0, 0), (2, 2)))
    start = lax.axis_index("tm") * time_rows
    local_main = lax.dynamic_slice_in_dim(time_bands[:, 0], start, time_rows, 1)
    mass_diag = jnp.diagonal(mass_blocks[:, 0].astype(jnp.float32), axis1=1, axis2=2).reshape(-1)
    stiff_diag = jnp.diagonal(stiff_blocks[:, 0].astype(jnp.float32), axis1=1, axis2=2).reshape(-1)
    precond = (
        local_main[0][:, None] * mass_diag[None, :]
        + local_main[1][:, None] * stiff_diag[None, :]
        + obs_precision
    )
    solution = jnp.zeros_like(right_side)
    residual = right_side
    scaled = residual / precond
    direction = scaled
    norm_now = lax.psum(jnp.sum(residual * scaled), ("tm", "space"))
    for iteration in range(ITERS):
        applied = operate(
            direction,
            obs_precision,
            mass_blocks,
            stiff_blocks,
            block_pattern,
            send_lists,
            band_padded,
        )
        step_size = norm_now / lax.psum(jnp.sum(direction * applied), ("tm", "space"))
        solution = solution + step_size * direction
        residual = residual - step_size * applied
        if iteration + 1 < ITERS:
            scaled = residual / precond
            norm_next = lax.psum(jnp.sum(residual * scaled), ("tm", "space"))
            direction = scaled + norm_next / norm_now * direction
            norm_now = norm_next
    return (solution, residual)


def solution(mesh):
    placed = (
        P("tm", "space"),
        P("tm", "space"),
        P("space", None, None, None),
        P("space", None, None, None),
        P("space", None),
        P(),
        P(),
    )
    return jax.shard_map(
        shards,
        mesh=mesh,
        in_specs=placed,
        out_specs=(P("tm", "space"), P("tm", "space")),
        check_vma=False,
    )
```

profile of v0, /device:TPU:1, one launch (start us, length us, event | category | flops | bytes accessed | tf_op | source)
XLA Modules:
  0.0 815.8 jit_solution(11793209684158471366)
XLA Ops:
  0.6 0.8 slice.457
  1.5 3.3 copy.37
  4.9 6.5 bitcast_convert_fusion
  11.3 1.8 gather_fusion.1
  13.3 3.3 copy.35
  16.6 6.5 bitcast_convert_fusion.1
  23.2 1.8 gather_fusion
  25.1 8.1 collective-permute-start.1
  33.3 1.9 collective-permute-start
  36.5 0.7 compare_select_fusion
  37.4 4.5 collective-permute-done
  43.8 6.0 collective-permute-start.3
  49.8 1.9 collective-permute-start.2
  51.8 2.9 collective-permute-done.2
  54.7 0.8 multiply_reduce_fusion.6
  55.5 99.9 %all-reduce.1 = (f32[]{:T(128)}, f32[]{:T(128)}) all-reduce(f32[]{:T(128)} %get-tuple-element.3, f32[]{:T(128)} %get-tuple-element.2), channel_id=1, replica_groups=mesh['tm'=16,'space'=32] {'tm','space'}, use_global_device_ids=true, to_apply=%region_1.2 | all-reduce | flops 2 | bytes 16 | tf_op jit(solution)/shard_map/psum | solution.py:95
  156.8 0.7 multiply_reduce_fusion.5
  157.5 94.4 %psum.58 = f32[]{:T(128)} all-reduce(f32[]{:T(128)} %get-tuple-element.16), channel_id=1, replica_groups=mesh['tm'=16,'space'=32] {'tm','space'}, use_global_device_ids=true, to_apply=%region_5.6 | all-reduce | flops 1 | bytes 8 | tf_op jit(solution)/shard_map/psum | solution.py:111
  253.4 4.0 collective-permute-start.5
  257.4 1.9 collective-permute-start.4
  259.3 6.7 collective-permute-done.4
  267.8 3.9 collective-permute-start.7
  271.7 1.9 collective-permute-start.6
  273.6 3.0 collective-permute-done.6
  276.6 0.8 multiply_reduce_fusion.4
  277.5 95.8 %psum.59 = f32[]{:T(128)} all-reduce(f32[]{:T(128)} %get-tuple-element.14), channel_id=1, replica_groups=mesh['tm'=16,'space'=32] {'tm','space'}, use_global_device_ids=true, to_apply=%region_7.8 | all-reduce | flops 1 | bytes 8 | tf_op jit(solution)/shard_map/psum | solution.py:106
  374.6 0.7 multiply_reduce_fusion.3
  375.3 95.5 %psum.60 = f32[]{:T(128)} all-reduce(f32[]{:T(128)} %get-tuple-element.12), channel_id=1, replica_groups=mesh['tm'=16,'space'=32] {'tm','space'}, use_global_device_ids=true, to_apply=%region_9.10 | all-reduce | flops 1 | bytes 8 | tf_op jit(solution)/shard_map/psum | solution.py:111
  472.3 5.0 collective-permute-start.9
  477.2 1.9 collective-permute-start.8
  479.2 6.7 collective-permute-done.8
  487.7 3.3 collective-permute-start.11
  491.0 2.0 collective-permute-start.10
  493.0 2.9 collective-permute-done.10
  495.9 0.8 multiply_reduce_fusion.2
  496.7 96.6 %psum.61 = f32[]{:T(128)} all-reduce(f32[]{:T(128)} %get-tuple-element.10), channel_id=1, replica_groups=mesh['tm'=16,'space'=32] {'tm','space'}, use_global_device_ids=true, to_apply=%region_11.12 | all-reduce | flops 1 | bytes 8 | tf_op jit(solution)/shard_map/psum | solution.py:106
  594.6 0.7 multiply_reduce_fusion.1
  595.4 95.5 %psum.62 = f32[]{:T(128)} all-reduce(f32[]{:T(128)} %get-tuple-element.8), channel_id=1, replica_groups=mesh['tm'=16,'space'=32] {'tm','space'}, use_global_device_ids=true, to_apply=%region_13.14 | all-reduce | flops 1 | bytes 8 | tf_op jit(solution)/shard_map/psum | solution.py:111
  692.3 5.0 collective-permute-start.13
  697.3 1.9 collective-permute-start.12
  699.2 6.7 collective-permute-done.12
  707.7 3.3 collective-permute-start.15
  711.0 2.0 collective-permute-start.14
  713.1 2.9 collective-permute-done.14
  715.9 0.8 multiply_reduce_fusion
  716.8 96.4 %psum.63 = f32[]{:T(128)} all-reduce(f32[]{:T(128)} %get-tuple-element.6), channel_id=1, replica_groups=mesh['tm'=16,'space'=32] {'tm','space'}, use_global_device_ids=true, to_apply=%region_15.16 | all-reduce | flops 1 | bytes 8 | tf_op jit(solution)/shard_map/psum | solution.py:106
  814.5 0.7 multiply_add_fusion
  815.2 0.7 multiply_subtract_fusion
  (90 shorter events, 8.5 us)
Async XLA Ops:
  1.5 11.6 %slice-start.1 = ((f32[2,3,1536]{2,0,1:T(2,128)}), f32[2,1,1536]{2,0,1:T(2,128)S(1)}, s32[]{:S(2)}) async-start(f32[2,3,1536]{2,0,1:T(2,128)} %param.13), calls=%async_computation.1 | async-start | bytes 24576 | tf_op jit(solution)/shard_map/slice | solution.py:83
  1.5 11.7 %slice-start = ((bf16[2,4,128,128]{3,2,1,0:T(8,128)(2,1)}), bf16[2,1,128,128]{3,2,1,0:T(8,128)(2,1)S(1)}, s32[]{:S(2)}) async-start(bf16[2,4,128,128]{3,2,1,0:T(8,128)(2,1)} %param.9), calls=%async_computation | async-start | bytes 131072 | tf_op jit(solution)/shard_map/slice | solution.py:84
  13.2 11.8 %copy-start = (f32[96,256]{1,0:T(8,128)S(1)}, f32[96,256]{1,0:T(8,128)}, u32[]{:S(2)}) copy-start(f32[96,256]{1,0:T(8,128)} %param.8) | copy-start | bytes 294916
  13.2 11.8 %copy-start.3 = (f32[96,256]{1,0:T(8,128)S(1)}, f32[96,256]{1,0:T(8,128)}, u32[]{:S(2)}) copy-start(f32[96,256]{1,0:T(8,128)} %param.7) | copy-start | bytes 294916
  13.3 22.0 %copy-start.5 = (s32[32,2,1]{0,2,1:T(1,128)S(1)}, s32[32,2,1]{0,2,1:T(1,128)}, u32[]{:S(2)}) copy-start(s32[32,2,1]{0,2,1:T(1,128)} %param.12) | copy-start | bytes 772
  13.3 23.2 %copy-start.6 = (s32[2,4]{1,0:T(2,128)S(1)}, s32[2,4]{1,0:T(2,128)}, u32[]{:S(2)}) copy-start(s32[2,4]{1,0:T(2,128)} %param.11) | copy-start | bytes 100
  13.3 24.0 %copy-start.4 = (f32[2,3,1536]{2,0,1:T(2,128)S(1)}, f32[2,3,1536]{2,0,1:T(2,128)}, u32[]{:S(2)}) copy-start(f32[2,3,1536]{2,0,1:T(2,128)} %param.13) | copy-start | bytes 110596
  16.6 25.9 %copy-start.1 = (bf16[2,4,128,128]{3,2,1,0:T(8,128)(2,1)S(1)}, bf16[2,4,128,128]{3,2,1,0:T(8,128)(2,1)}, u32[]{:S(2)}) copy-start(bf16[2,4,128,128]{3,2,1,0:T(8,128)(2,1)} %param.9) | copy-start | bytes 786436
  16.6 26.3 %copy-start.2 = (bf16[2,4,128,128]{3,2,1,0:T(8,128)(2,1)S(1)}, bf16[2,4,128,128]{3,2,1,0:T(8,128)(2,1)}, u32[]{:S(2)}) copy-start(bf16[2,4,128,128]{3,2,1,0:T(8,128)(2,1)} %param.10) | copy-start | bytes 786436
  25.1 12.3 %collective-permute-start.1 = (f32[96,2,128]{2,0,1:T(8,128)S(1)}, f32[96,2,128]{2,0,1:T(8,128)S(1)}, u32[]{:S(2)}, u32[]{:S(2)}) collective-permute-start(f32[96,2,128]{2,0,1:T(8,128)S(1)} %copy_bitcast_fusion.3), channel_id=1, source_target_pairs={{1,0},{2,1},{3,2},{4,3},{5,4},{6,5},{7,6},{8,7},{9,8},{10,9},{11,1... | collective-permute-start | bytes 294920 | tf_op jit(solution)/shard_map/ppermute | solution.py:17
  33.3 8.7 %collective-permute-start = (f32[96,2,128]{2,0,1:T(8,128)S(1)}, f32[96,2,128]{2,0,1:T(8,128)S(1)}, u32[]{:S(2)}, u32[]{:S(2)}) collective-permute-start(f32[96,2,128]{2,0,1:T(8,128)S(1)} %copy_bitcast_fusion.3), channel_id=1, source_target_pairs={{0,1},{1,2},{2,3},{3,4},{4,5},{5,6},{6,7},{7,8},{8,9},{9,10},{10,1... | collective-permute-start | bytes 294920 | tf_op jit(solution)/shard_map/ppermute | solution.py:16
  43.8 8.0 collective-permute-start.3
  49.8 4.9 collective-permute-start.2
  253.4 5.9 collective-permute-start.5
  257.4 8.7 %collective-permute-start.4 = (f32[96,2,128]{2,0,1:T(8,128)S(1)}, f32[96,2,128]{2,0,1:T(8,128)S(1)}, u32[]{:S(2)}, u32[]{:S(2)}) collective-permute-start(f32[96,2,128]{2,0,1:T(8,128)S(1)} %copy_bitcast_fusion.2), channel_id=1, source_target_pairs={{0,1},{1,2},{2,3},{3,4},{4,5},{5,6},{6,7},{7,8},{8,9},{9,10},{10,1... | collective-permute-start | bytes 294920 | tf_op jit(solution)/shard_map/ppermute | solution.py:16
  267.8 5.8 collective-permute-start.7
  271.7 4.9 collective-permute-start.6
  472.3 6.9 collective-permute-start.9
  477.2 8.7 %collective-permute-start.8 = (f32[96,2,128]{2,0,1:T(8,128)S(1)}, f32[96,2,128]{2,0,1:T(8,128)S(1)}, u32[]{:S(2)}, u32[]{:S(2)}) collective-permute-start(f32[96,2,128]{2,0,1:T(8,128)S(1)} %copy_bitcast_fusion.1), channel_id=1, source_target_pairs={{0,1},{1,2},{2,3},{3,4},{4,5},{5,6},{6,7},{7,8},{8,9},{9,10},{10,1... | collective-permute-start | bytes 294920 | tf_op jit(solution)/shard_map/ppermute | solution.py:16
  487.7 5.3 collective-permute-start.11
  491.0 4.9 collective-permute-start.10
  692.3 6.9 collective-permute-start.13
  697.3 8.7 %collective-permute-start.12 = (f32[96,2,128]{2,0,1:T(8,128)S(1)}, f32[96,2,128]{2,0,1:T(8,128)S(1)}, u32[]{:S(2)}, u32[]{:S(2)}) collective-permute-start(f32[96,2,128]{2,0,1:T(8,128)S(1)} %copy_bitcast_fusion), channel_id=1, source_target_pairs={{0,1},{1,2},{2,3},{3,4},{4,5},{5,6},{6,7},{7,8},{8,9},{9,10},{10,1... | collective-permute-start | bytes 294920 | tf_op jit(solution)/shard_map/ppermute | solution.py:16
  707.7 5.3 collective-permute-start.15
  711.0 4.9 collective-permute-start.14
where the time goes:
time: 818 us; the launch traced here: 816 us
  blocking collectives  674 us (82%)
  starting transfers between devices  54 us (7%)
  waiting for transfers between devices  36.4 us (4%)
  other arithmetic  21 us (3%)
  local copies, waits for them, and re-layouts  15.9 us (2%)
  between operations  11.3 us (1%)
    psum x3, blocking collectives, shards(): lax.psum(jnp.sum(direction * applied), ('tm', 'space'))  289 us
    psum x3, blocking collectives, shards(): norm_next = lax.psum(jnp.sum(residual * scaled), ('tm', 'space'))  285 us
    psum x1, blocking collectives, shards(): norm_now = lax.psum(jnp.sum(residual * scaled), ('tm', 'space'))  99.9 us
    ppermute x8, starting transfers between devices, padded_2(): after = lax.ppermute(first, axis, down)  29.9 us
    ppermute x8, waiting for transfers between devices, padded_2(): before = lax.ppermute(last, axis, up)  24.8 us
    ppermute x8, starting transfers between devices, padded_2(): before = lax.ppermute(last, axis, up)  24.1 us
  transfers between devices with their start and end apart: 16, of which 8 were waited for; matrix products, arithmetic and copies ran while one was open for 0% of the time, Pallas kernels for 0%

commit v1 on v0

v1 whole, which is shorter than its diff:
```python
import jax
import jax.numpy as jnp
from jax import lax
from jax.experimental import pallas as pl
from jax.experimental.pallas import tpu as pltpu
from jax.sharding import PartitionSpec as P

ITERS = 4
HALO = 2 * ITERS
BLOCK = 128
CENTRE = 1.0
WIDTH = 0.6
VMEM = pl.BlockSpec(memory_space=pltpu.VMEM)
SMEM = pl.BlockSpec(memory_space=pltpu.SMEM)
F32 = jnp.float32


def column(bands, index):
    return bands[:, index : index + 1]


def product(pieces, weights):
    return jnp.dot(
        jnp.concatenate(pieces, axis=1),
        jnp.concatenate(weights, axis=0),
        precision=lax.Precision.HIGHEST,
        preferred_element_type=F32,
    )


def moved(rows, offset):
    return pltpu.roll(rows, (-offset) % rows.shape[0], 0)


def band_apply(bands, base, rows):
    result = column(bands, base) * rows
    result = result + column(bands, base + 1) * moved(rows, 1)
    result = result + column(bands, base + 2) * moved(rows, -1)
    result = result + column(bands, base + 3) * moved(rows, 2)
    return result + column(bands, base + 4) * moved(rows, -2)


def image(bands, spatial, precision, vector):
    return (
        band_apply(bands, 0, spatial[:, :BLOCK])
        + band_apply(bands, 5, spatial[:, BLOCK:])
        + precision * vector
    )


def prepare_kernel(
    meta, right, obs, before, after, mass, stiff, bands_ref,
    scaled_ref, precond_ref, obs_ref, weights_ref, up_ref, down_ref,
):
    low = meta[0]
    high = 1 - low
    swapped = low == 1
    rows = right.shape[0]
    bands = bands_ref[...]
    valid = column(bands, 10)
    rhs = jnp.concatenate([before[:HALO], right[...], after[:HALO]], axis=0)
    precision = jnp.concatenate([before[HALO:], obs[...], after[HALO:]], axis=0)
    eye = lax.broadcasted_iota(jnp.int32, (BLOCK, BLOCK), 0) == lax.broadcasted_iota(
        jnp.int32, (BLOCK, BLOCK), 1
    )
    own = (low, high)

    def chain(array):
        first, second = array[:, :BLOCK], array[:, BLOCK:]
        return jnp.where(swapped, second, first), jnp.where(swapped, first, second)

    rhs, precision = chain(rhs), chain(precision)
    extent = rhs[0].shape[0]
    for place in range(2):
        block = own[place]
        diagonals = [
            jnp.sum(jnp.where(eye, ref[block, 0].astype(F32), 0.0), axis=0, keepdims=True)
            for ref in (mass, stiff)
        ]
        precond = column(bands, 0) * diagonals[0] + column(bands, 5) * diagonals[1]
        precond = precond + precision[place] + (1.0 - valid)
        scaled = valid * rhs[place] / precond
        lanes = slice(place * BLOCK, (place + 1) * BLOCK)
        scaled_ref[:, lanes] = scaled
        precond_ref[:, lanes] = precond
        obs_ref[:, lanes] = precision[place]
        near, far = ((down_ref, up_ref), (up_ref, down_ref))[place]
        near[:extent] = scaled
        far[extent : 2 * extent] = scaled
        near[2 * extent : 3 * extent] = precision[place]
        near[3 * extent : 3 * extent + 8] = jnp.concatenate(
            diagonals + [jnp.zeros((6, BLOCK), F32)], axis=0
        )
    start = 3 * extent + 8
    for index, ref in enumerate((mass, stiff)):
        lanes = slice(index * BLOCK, (index + 1) * BLOCK)

        def total(row, col):
            result = ref[own[row], 0].astype(F32) if row == col else jnp.zeros((BLOCK, BLOCK), F32)
            for j in (2, 3):
                named = meta[1 + own[row] * 4 + j] == own[col]
                result = result + jnp.where(named, ref[own[row], j].astype(F32), 0.0)
            return result

        first, second = total(0, 0), total(1, 1)
        first_second, second_first = total(0, 1), total(1, 0)
        cross_low = ref[low, 1].astype(F32)
        cross_high = ref[high, 1].astype(F32)
        parts = (
            first, second_first, cross_low.T,
            first_second, second, cross_high.T,
            cross_low, cross_high,
        )
        for place, part in enumerate(parts):
            weights_ref[place, :, lanes] = part
        place = start + index * BLOCK
        up_ref[place : place + BLOCK] = first_second
        up_ref[place + 2 * BLOCK : place + 3 * BLOCK] = second
        down_ref[place : place + BLOCK] = second_first
        down_ref[place + 2 * BLOCK : place + 3 * BLOCK] = first


def ghost(bands, ref):
    extent = bands.shape[0]
    near, far = ref[:extent], ref[extent : 2 * extent]
    precision = ref[2 * extent : 3 * extent]
    start = 3 * extent
    precond = column(bands, 0) * ref[start : start + 1]
    precond = precond + column(bands, 5) * ref[start + 1 : start + 2]
    precond = precond + precision + (1.0 - column(bands, 10))
    start = start + 8
    blocks = [ref[start + k * BLOCK : start + (k + 1) * BLOCK] for k in range(4)]
    weights = [
        jnp.concatenate(blocks[:2], axis=1),
        jnp.concatenate(blocks[2:], axis=1),
    ]
    return near, far, precision, precond, weights


def halves(ref):
    return ref[:, :BLOCK], ref[:, BLOCK:]


def stepped(bands, spatial, precision, precond, vector, older):
    applied = image(bands, spatial, precision, vector)
    shifted = column(bands, 10) * applied / precond - CENTRE * vector
    if older is None:
        return shifted * (1.0 / WIDTH)
    return shifted * (2.0 / WIDTH) - older


def first_kernel(
    scaled, precond_ref, obs, weights, below, above, bands_ref,
    one_ref, two_ref, near_ref,
):
    bands = bands_ref[...]
    vector, precond, precision = halves(scaled), halves(precond_ref), halves(obs)
    sides = (ghost(bands, below), ghost(bands, above))
    outer = []
    for place, (near, far, near_obs, near_precond, side) in enumerate(sides):
        spatial = product([far, near, vector[place]], side + [weights[6 + place]])
        outer.append(stepped(bands, spatial, near_obs, near_precond, near, None))
        near_ref[place] = outer[place]
    inner = []
    for place in range(2):
        spatial = product(
            list(vector) + [sides[place][0]], [weights[3 * place + k] for k in range(3)]
        )
        inner.append(stepped(bands, spatial, precision[place], precond[place], vector[place], None))
        one_ref[place] = inner[place]
    for place in range(2):
        spatial = product(inner + [outer[place]], [weights[3 * place + k] for k in range(3)])
        two_ref[place] = stepped(
            bands, spatial, precision[place], precond[place], inner[place], vector[place]
        )


def second_kernel(
    scaled, one_ref, two_ref, near_ref, precond_ref, obs, weights, below, above, bands_ref,
    below_two, above_two, three_ref, four_ref, sums_ref,
):
    bands = bands_ref[...]
    precond, precision = halves(precond_ref), halves(obs)
    extent = bands.shape[0]
    two = (two_ref[0], two_ref[1])
    nears = (below_two[1], above_two[0])
    fars = (below_two[0], above_two[1])
    outer = []
    for place, ref in enumerate((below, above)):
        _, _, near_obs, near_precond, side = ghost(bands, ref)
        spatial = product([fars[place], nears[place], two[place]], side + [weights[6 + place]])
        outer.append(
            stepped(bands, spatial, near_obs, near_precond, nears[place], near_ref[place])
        )
    three = []
    for place in range(2):
        spatial = product(list(two) + [nears[place]], [weights[3 * place + k] for k in range(3)])
        three.append(
            stepped(bands, spatial, precision[place], precond[place], two[place], one_ref[place])
        )
        three_ref[place] = three[place]
    sums = [0.0] * 14
    inside = slice(HALO, extent - HALO)
    start = halves(scaled)
    for place in range(2):
        spatial = product(three + [outer[place]], [weights[3 * place + k] for k in range(3)])
        four = stepped(bands, spatial, precision[place], precond[place], three[place], two[place])
        four_ref[place] = four
        basis = [
            rows[inside]
            for rows in (start[place], one_ref[place], two[place], three[place], four)
        ]
        index = 0
        for i in range(4):
            weighted = precond[place][inside] * basis[i]
            for j in range(i, 5):
                term = (weighted * basis[j]).reshape(-1, 8, BLOCK)
                sums[index] = sums[index] + jnp.sum(term, axis=0)
                index += 1
    rows = [jnp.sum(part, axis=0, keepdims=True) for part in sums]
    table = jnp.concatenate(rows + [jnp.zeros((2, BLOCK), F32)], axis=0)
    totals = jnp.sum(table, axis=1, keepdims=True)
    slots = lax.broadcasted_iota(jnp.int32, (16, BLOCK), 0) == lax.broadcasted_iota(
        jnp.int32, (16, BLOCK), 1
    )
    sums_ref[...] = jnp.sum(jnp.where(slots, totals, 0.0), axis=0, keepdims=True)


def operator(vector):
    result = [0.0] * 5
    for j in range(4):
        result[j] = result[j] + CENTRE * vector[j]
        if j == 0:
            result[1] = result[1] + WIDTH * vector[0]
        else:
            result[j + 1] = result[j + 1] + (0.5 * WIDTH) * vector[j]
            result[j - 1] = result[j - 1] + (0.5 * WIDTH) * vector[j]
    return result


def inner_product(table, left, right):
    total = 0.0
    for i, a in enumerate(left):
        for j, b in enumerate(right):
            if a is not None and b is not None:
                total = total + table[(min(i, j), max(i, j))] * (a * b)
    return total


def final_kernel(meta, parts, scaled, one_ref, two_ref, three_ref, four_ref, precond_ref,
                 solution_ref, residual_ref):
    rows = jnp.sum(parts[...], axis=0, keepdims=True)
    lane = lax.broadcasted_iota(jnp.int32, (1, BLOCK), 1)
    table = {}
    index = 0
    for i in range(4):
        for j in range(i, 5):
            table[(i, j)] = jnp.sum(jnp.where(lane == index, rows, 0.0), axis=1, keepdims=True)
            index += 1
    one = jnp.ones((1, 1), F32)
    zero = jnp.zeros((1, 1), F32)
    state = [one, zero, zero, zero, zero]
    direction = list(state)
    answer = [zero] * 5
    norm_now = table[(0, 0)]

    def cut(vector, degree):
        return [v if k <= degree else None for k, v in enumerate(vector)]

    for iteration in range(ITERS):
        applied = operator(direction)
        step = norm_now / inner_product(
            table, cut(direction, iteration), cut(applied, iteration + 1)
        )
        answer = [a + step * d for a, d in zip(answer, direction)]
        state = [s - step * w for s, w in zip(state, applied)]
        if iteration + 1 < ITERS:
            kept = cut(state, iteration + 1)
            norm_next = inner_product(table, kept, kept)
            direction = [s + norm_next / norm_now * d for s, d in zip(state, direction)]
            norm_now = norm_next
    swapped = meta[0] == 1
    precond = halves(precond_ref)
    start = halves(scaled)
    extent = start[0].shape[0]
    inside = slice(HALO, extent - HALO)
    solutions, residuals = [], []
    for place in range(2):
        basis = [
            rows[inside]
            for rows in (
                start[place], one_ref[place], two_ref[place], three_ref[place], four_ref[place]
            )
        ]
        total = answer[0] * basis[0]
        left = state[0] * basis[0]
        for k in range(1, 5):
            if k < 4:
                total = total + answer[k] * basis[k]
            left = left + state[k] * basis[k]
        solutions.append(total)
        residuals.append(left * precond[place][inside])
    for ref, pair in ((solution_ref, solutions), (residual_ref, residuals)):
        ref[:, :BLOCK] = jnp.where(swapped, pair[1], pair[0])
        ref[:, BLOCK:] = jnp.where(swapped, pair[0], pair[1])


def call(kernel, shapes, *operands, scalars=0):
    return pl.pallas_call(
        kernel,
        out_shape=[jax.ShapeDtypeStruct(shape, F32) for shape in shapes],
        in_specs=[SMEM] * scalars + [VMEM] * (len(operands) - scalars),
        out_specs=[VMEM] * len(shapes),
        compiler_params=pltpu.CompilerParams(vmem_limit_bytes=32 * 1024 * 1024),
    )(*operands)


def ring(array, axis, wrap):
    devices = lax.axis_size(axis)
    up = [(i, (i + 1) % devices) for i in range(devices if wrap else devices - 1)]
    return up, [(j, i) for i, j in up]


def shards(
    right_side, obs_precision, mass_blocks, stiff_blocks, block_pattern, send_lists, time_bands
):
    time_rows, nodes = right_side.shape
    extent = time_rows + 2 * HALO
    part = lax.axis_index("space")
    low = lax.dynamic_index_in_dim(send_lists, part, 0, keepdims=False)[0]
    meta = jnp.concatenate([low, block_pattern.reshape(-1)])

    up, down = ring(right_side, "tm", False)
    last = jnp.concatenate([right_side[-HALO:], obs_precision[-HALO:]], axis=0)
    first = jnp.concatenate([right_side[:HALO], obs_precision[:HALO]], axis=0)
    before = lax.ppermute(last, "tm", up)
    after = lax.ppermute(first, "tm", down)

    start = lax.axis_index("tm") * time_rows
    margin = HALO + 2
    known = jnp.ones((1, time_bands.shape[2]), F32)
    padded = jnp.concatenate([time_bands.reshape(6, -1), known], axis=0)
    padded = jnp.pad(padded, ((0, 0), (margin, margin)))
    local = lax.dynamic_slice_in_dim(padded, start, extent + 4, 1)
    lines = []
    for matrix in range(2):
        for band, offset in ((0, 0), (1, 0), (1, -1), (2, 0), (2, -2)):
            row = 3 * matrix + band
            lines.append(local[row, 2 + offset : 2 + offset + extent])
    lines.append(local[6, 2 : 2 + extent])
    bands = jnp.pad(jnp.stack(lines, axis=1), ((0, 0), (0, 16 - len(lines))))

    full = (extent, nodes)
    pair = (2, extent, BLOCK)
    buffer = (3 * extent + 8 + 4 * BLOCK, BLOCK)
    scaled, precond, precision, weights, to_up, to_down = call(
        prepare_kernel,
        [full, full, full, (8, BLOCK, 2 * BLOCK), buffer, buffer],
        meta, right_side, obs_precision, before, after, mass_blocks, stiff_blocks, bands,
        scalars=1,
    )
    up, down = ring(right_side, "space", True)
    below = lax.ppermute(to_up, "space", up)
    above = lax.ppermute(to_down, "space", down)
    one, two, near = call(
        first_kernel, [pair, pair, pair], scaled, precond, precision, weights, below, above, bands
    )
    below_two = lax.ppermute(two, "space", up)
    above_two = lax.ppermute(two, "space", down)
    three, four, sums = call(
        second_kernel,
        [pair, pair, (1, BLOCK)],
        scaled, one, two, near, precond, precision, weights, below, above, bands,
        below_two, above_two,
    )
    for axis in ("space", "tm"):
        devices = lax.axis_size(axis)
        sent = jnp.broadcast_to(sums[None], (devices, 1, BLOCK))
        parts = lax.all_to_all(sent, axis, 0, 0)
        sums = jnp.sum(parts, axis=0)
    return tuple(
        call(
            final_kernel,
            [right_side.shape, right_side.shape],
            meta, sums, scaled, one, two, three, four, precond,
            scalars=1,
        )
    )


def solution(mesh):
    placed = (
        P("tm", "space"),
        P("tm", "space"),
        P("space", None, None, None),
        P("space", None, None, None),
        P("space", None),
        P(),
        P(),
    )
    return jax.shard_map(
        shards,
        mesh=mesh,
        in_specs=placed,
        out_specs=(P("tm", "space"), P("tm", "space")),
        check_vma=False,
    )
```

time: 818 us -> 86.6 us (0.11)
  blocking collectives: 674 us -> 29.3 us
  starting transfers between devices: 54 us -> 28.2 us
  other arithmetic: 21 us -> 0.85 us
  waiting for transfers between devices: 36.4 us -> 16.7 us
  local copies, waits for them, and re-layouts: 15.9 us -> 3.44 us
  between operations: 11.3 us -> 0.83 us
    psum x7 -> x0, blocking collectives: 674 us -> none  [the longest x3 289 us: shards(): lax.psum(jnp.sum(direction * applied), ('tm', 'space'))]
    all_to_all x0 -> x2, blocking collectives: none -> 29.3 us  [shards(): parts = lax.all_to_all(sent, axis, 0, 0)]
    ppermute x16 -> x6, starting transfers between devices: 54 us -> 28.2 us  [the longest x1 7.43 us: shards(): above_two = lax.ppermute(two, 'space', down)]
    ppermute x16 -> x6, waiting for transfers between devices: 36.4 us -> 16.7 us  [the longest x1 8.38 us: shards(): below = lax.ppermute(to_up, 'space', up)]
    convert_element_type x2 -> x0, other arithmetic: 13 us -> none  [the longest x1 6.53 us: shards(): mass_blocks[:, 0].astype(jnp.float32)]
  transfers between devices with their start and end apart: 16 -> 6, of which waited for: 8 -> 3; matrix products, arithmetic and copies ran while one was open for 0% -> 3% of each run, Pallas kernels for 0% -> 0%
where the time goes in v1:
time: 86.6 us; the launch traced here: 86.2 us
  blocking collectives  29.3 us (34%)
  starting transfers between devices  28.2 us (33%)
  waiting for transfers between devices  16.7 us (19%)
  Pallas kernels  6.9 us (8%)
  local copies, waits for them, and re-layouts  3.44 us (4%)
    all_to_all x2, blocking collectives, shards(): parts = lax.all_to_all(sent, axis, 0, 0)  29.3 us
    ppermute x1, waiting for transfers between devices, shards(): below = lax.ppermute(to_up, 'space', up)  8.38 us
    ppermute x1, starting transfers between devices, shards(): above_two = lax.ppermute(two, 'space', down)  7.43 us
    pallas_call x4, Pallas kernels, call(): pl.pallas_call(kernel, out_shape=[jax.ShapeDtypeStruct(shape, F32) for sh...  6.9 us
    ppermute x1, waiting for transfers between devices, shards(): below_two = lax.ppermute(two, 'space', up)  6.89 us
    ppermute x1, starting transfers between devices, shards(): above = lax.ppermute(to_down, 'space', down)  6.68 us
    ppermute x1, starting transfers between devices, shards(): before = lax.ppermute(last, 'tm', up)  5.38 us
    ppermute x1, starting transfers between devices, shards(): after = lax.ppermute(first, 'tm', down)  4.82 us
  transfers between devices with their start and end apart: 6, of which 3 were waited for; matrix products, arithmetic and copies ran while one was open for 3% of the time, Pallas kernels for 0%

profile of v1, /device:TPU:1, one launch (start us, length us, event | category | flops | bytes accessed | tf_op | source)
XLA Modules:
  0.0 86.2 jit_solution(3702968047157670899)
XLA Ops:
  0.6 0.0 copy-start
  0.6 0.0 copy-start.3
  0.7 0.8 fusion.4
  1.4 5.4 %collective-permute-start = (f32[16,256]{1,0:T(8,128)S(1)}, f32[16,256]{1,0:T(8,128)S(1)}, u32[]{:S(2)}, u32[]{:S(2)}) collective-permute-start(f32[16,256]{1,0:T(8,128)S(1)} %pad_maximum_fusion), channel_id=1, source_target_pairs={{0,32},{32,64},{64,96},{96,128},{128,160},{160,192},{192,224},{224... | collective-permute-start | bytes 49160 | tf_op jit(solution)/shard_map/ppermute | solution.py:336
  6.8 0.0 copy-start.5
  6.8 0.0 copy-start.1
  6.9 0.0 copy-start.2
  6.9 4.8 %collective-permute-start.1 = (f32[16,256]{1,0:T(8,128)S(1)}, f32[16,256]{1,0:T(8,128)S(1)}, u32[]{:S(2)}, u32[]{:S(2)}) collective-permute-start(f32[16,256]{1,0:T(8,128)S(1)} %pad_maximum_fusion.1), channel_id=1, source_target_pairs={{32,0},{64,32},{96,64},{128,96},{160,128},{192,160},{224,192},{256... | collective-permute-start | bytes 49160 | tf_op jit(solution)/shard_map/ppermute | solution.py:337
  11.7 0.0 copy-done.5
  11.7 0.1 reshape.21
  11.8 0.8 copy.36
  12.6 0.1 fusion
  12.7 0.1 slice_bitcast_fusion
  12.8 0.0 copy-done
  12.8 0.6 constant_dynamic-slice_fusion
  13.4 0.7 pad_add_fusion.meta
  14.1 0.1 copy.37
  14.3 0.0 collective-permute-done.before
  14.3 0.0 collective-permute-done.1.after
  14.3 0.0 copy-done.3
  14.3 0.0 copy-done.1
  14.3 0.0 copy-done.2
  14.3 0.0 copy-start.4
  14.3 0.9 %copy-done.4 = f32[96,256]{1,0:T(8,128)S(1)} copy-done((f32[96,256]{1,0:T(8,128)S(1)}, f32[96,256]{1,0:T(8,128)}, u32[]{:S(2)}) %copy-start.4) | copy-done | bytes 98328
  15.2 0.8 shard_map.86
  16.0 1.9 %collective-permute-start.2 = (f32[856,128]{1,0:T(8,128)S(1)}, f32[856,128]{1,0:T(8,128)S(1)}, u32[]{:S(2)}, u32[]{:S(2)}) collective-permute-start(f32[856,128]{1,0:T(8,128)S(1)} %get-tuple-element.18), channel_id=1, source_target_pairs={{0,1},{1,2},{2,3},{3,4},{4,5},{5,6},{6,7},{7,8},{8,9},{9,10},{10,1... | collective-permute-start | bytes 1314824 | tf_op jit(solution)/shard_map/ppermute | solution.py:363
  18.0 6.7 %collective-permute-start.3 = (f32[856,128]{1,0:T(8,128)S(1)}, f32[856,128]{1,0:T(8,128)S(1)}, u32[]{:S(2)}, u32[]{:S(2)}) collective-permute-start(f32[856,128]{1,0:T(8,128)S(1)} %get-tuple-element.19), channel_id=1, source_target_pairs={{1,0},{2,1},{3,2},{4,3},{5,4},{6,5},{7,6},{8,7},{9,8},{10,9},{11,1... | collective-permute-start | bytes 1314824 | tf_op jit(solution)/shard_map/ppermute | solution.py:364
  24.6 8.4 %collective-permute-done.2.below = f32[856,128]{1,0:T(8,128)S(1)} collective-permute-done((f32[856,128]{1,0:T(8,128)S(1)}, f32[856,128]{1,0:T(8,128)S(1)}, u32[]{:S(2)}, u32[]{:S(2)}) %collective-permute-start.2) | collective-permute-done | bytes 438304 | tf_op jit(solution)/shard_map/ppermute | solution.py:363
  33.0 1.4 %collective-permute-done.3.above = f32[856,128]{1,0:T(8,128)S(1)} collective-permute-done((f32[856,128]{1,0:T(8,128)S(1)}, f32[856,128]{1,0:T(8,128)S(1)}, u32[]{:S(2)}, u32[]{:S(2)}) %collective-permute-start.3) | collective-permute-done | bytes 438304 | tf_op jit(solution)/shard_map/ppermute | solution.py:364
  34.4 2.2 %shard_map.87 = (f32[2,112,128]{2,1,0:T(8,128)S(1)}, f32[2,112,128]{2,1,0:T(8,128)S(1)}, f32[2,112,128]{2,1,0:T(8,128)S(1)}) custom-call(f32[112,256]{1,0:T(8,128)S(1)} %get-tuple-element.14.scaled, f32[112,256]{1,0:T(8,128)S(1)} %get-tuple-element.15.precond_ref, f32[112,256]{1,0:T(8,128)S(1)} %get-tuple-element.16.obs, ...), custom_call_target="tpu_custom_call" | custom-call | tf_op jit(solution)/shard_map/pallas_call | solution.py:309
  36.6 7.4 %collective-permute-start.5 = (f32[2,112,128]{2,1,0:T(8,128)S(1)}, f32[2,112,128]{2,1,0:T(8,128)S(1)}, u32[]{:S(2)}, u32[]{:S(2)}) collective-permute-start(f32[2,112,128]{2,1,0:T(8,128)S(1)} %get-tuple-element.21.two_ref), channel_id=1, source_target_pairs={{1,0},{2,1},{3,2},{4,3},{5,4},{6,5},{7,6},{8,7},{9,8},{10,9},{11,1... | collective-permute-start | bytes 344072 | tf_op jit(solution)/shard_map/ppermute | solution.py:369
  44.1 1.9 %collective-permute-start.4 = (f32[2,112,128]{2,1,0:T(8,128)S(1)}, f32[2,112,128]{2,1,0:T(8,128)S(1)}, u32[]{:S(2)}, u32[]{:S(2)}) collective-permute-start(f32[2,112,128]{2,1,0:T(8,128)S(1)} %get-tuple-element.21.two_ref), channel_id=1, source_target_pairs={{0,1},{1,2},{2,3},{3,4},{4,5},{5,6},{6,7},{7,8},{8,9},{9,10},{10,1... | collective-permute-start | bytes 344072 | tf_op jit(solution)/shard_map/ppermute | solution.py:368
  46.0 0.0 collective-permute-done.5.above_two
  46.0 6.9 %collective-permute-done.4.below_two = f32[2,112,128]{2,1,0:T(8,128)S(1)} collective-permute-done((f32[2,112,128]{2,1,0:T(8,128)S(1)}, f32[2,112,128]{2,1,0:T(8,128)S(1)}, u32[]{:S(2)}, u32[]{:S(2)}) %collective-permute-start.4) | collective-permute-done | bytes 114720 | tf_op jit(solution)/shard_map/ppermute | solution.py:368
  52.9 2.4 %shard_map.88 = (f32[2,112,128]{2,1,0:T(8,128)S(1)}, f32[2,112,128]{2,1,0:T(8,128)S(1)}, f32[1,128]{1,0:T(1,128)S(1)}) custom-call(f32[112,256]{1,0:T(8,128)S(1)} %get-tuple-element.14.scaled, f32[2,112,128]{2,1,0:T(8,128)S(1)} %get-tuple-element.20.one_ref, f32[2,112,128]{2,1,0:T(8,128)S(1)} %get-tuple-element.21.two_ref, ...), custom_call_target="tpu_custom_call" | custom-call | tf_op jit(solution)/shard_map/pallas_call | solution.py:309
  55.3 11.6 %all_to_all.10 = f32[32,1,128]{2,1,0:T(1,128)S(1)} all-to-all(f32[32,1,128]{2,1,0:T(1,128)S(1)} %broadcast_in_dim.7), channel_id=1, replica_groups=mesh['tm'=16,'space'=32] {'space'}, dimensions={0} | all-to-all | bytes 32768 | tf_op jit(solution)/shard_map/all_to_all | solution.py:379
  67.0 17.7 %all_to_all.11 = f32[16,1,128]{2,1,0:T(1,128)S(1)} all-to-all(f32[16,1,128]{2,1,0:T(1,128)S(1)} %broadcast_in_dim.8), channel_id=1, replica_groups=mesh['tm'=16,'space'=32] {'tm'}, dimensions={0} | all-to-all | bytes 16384 | tf_op jit(solution)/shard_map/all_to_all | solution.py:379
  84.7 1.5 %shard_map.89 = (f32[96,256]{1,0:T(8,128)}, f32[96,256]{1,0:T(8,128)}) custom-call(s32[9]{0:T(128)S(1)} %pad_add_fusion.meta, f32[1,128]{1,0:T(1,128)S(1)} %bitcast.27, f32[112,256]{1,0:T(8,128)S(1)} %get-tuple-element.14.scaled, f32[2,112,128]{2,1,0:T(8,128)S(1)} %get-tuple-element.20.one_ref, f32[2,112,128]{2,1,0:T(8,128)S(1)} %get-tuple-element.21.two_ref, ...), custom_call_target="tpu_custom_call" | custom-call | tf_op jit(solution)/shard_map/pallas_call | solution.py:309
  (9 shorter events, 0.1 us)
Async XLA Ops:
  0.6 12.2 %copy-start = (s32[32,2,1]{0,2,1:T(1,128)S(1)}, s32[32,2,1]{0,2,1:T(1,128)}, u32[]{:S(2)}) copy-start(s32[32,2,1]{0,2,1:T(1,128)} %param.12) | copy-start | bytes 772
  0.6 13.6 %copy-start.3 = (f32[96,256]{1,0:T(8,128)S(1)}, f32[96,256]{1,0:T(8,128)}, u32[]{:S(2)}) copy-start(f32[96,256]{1,0:T(8,128)} %right.1) | copy-start | bytes 294916
  1.4 12.8 %collective-permute-start = (f32[16,256]{1,0:T(8,128)S(1)}, f32[16,256]{1,0:T(8,128)S(1)}, u32[]{:S(2)}, u32[]{:S(2)}) collective-permute-start(f32[16,256]{1,0:T(8,128)S(1)} %pad_maximum_fusion), channel_id=1, source_target_pairs={{0,32},{32,64},{64,96},{96,128},{128,160},{160,192},{192,224},{224... | collective-permute-start | bytes 49160 | tf_op jit(solution)/shard_map/ppermute | solution.py:336
  6.8 4.9 %copy-start.5 = (s32[2,4]{1,0:T(2,128)S(1)}, s32[2,4]{1,0:T(2,128)}, u32[]{:S(2)}) copy-start(s32[2,4]{1,0:T(2,128)} %param.11) | copy-start | bytes 100
  6.8 7.4 %copy-start.1 = (bf16[2,4,128,128]{3,2,1,0:T(8,128)(2,1)S(1)}, bf16[2,4,128,128]{3,2,1,0:T(8,128)(2,1)}, u32[]{:S(2)}) copy-start(bf16[2,4,128,128]{3,2,1,0:T(8,128)(2,1)} %mass.1) | copy-start | bytes 786436
  6.9 7.4 %copy-start.2 = (bf16[2,4,128,128]{3,2,1,0:T(8,128)(2,1)S(1)}, bf16[2,4,128,128]{3,2,1,0:T(8,128)(2,1)}, u32[]{:S(2)}) copy-start(bf16[2,4,128,128]{3,2,1,0:T(8,128)(2,1)} %stiff.1) | copy-start | bytes 786436
  6.9 7.4 %collective-permute-start.1 = (f32[16,256]{1,0:T(8,128)S(1)}, f32[16,256]{1,0:T(8,128)S(1)}, u32[]{:S(2)}, u32[]{:S(2)}) collective-permute-start(f32[16,256]{1,0:T(8,128)S(1)} %pad_maximum_fusion.1), channel_id=1, source_target_pairs={{32,0},{64,32},{96,64},{128,96},{160,128},{192,160},{224,192},{256... | collective-permute-start | bytes 49160 | tf_op jit(solution)/shard_map/ppermute | solution.py:337
  14.3 0.9 %copy-start.4 = (f32[96,256]{1,0:T(8,128)S(1)}, f32[96,256]{1,0:T(8,128)}, u32[]{:S(2)}) copy-start(f32[96,256]{1,0:T(8,128)} %obs.1) | copy-start | bytes 294916
  16.0 17.0 %collective-permute-start.2 = (f32[856,128]{1,0:T(8,128)S(1)}, f32[856,128]{1,0:T(8,128)S(1)}, u32[]{:S(2)}, u32[]{:S(2)}) collective-permute-start(f32[856,128]{1,0:T(8,128)S(1)} %get-tuple-element.18), channel_id=1, source_target_pairs={{0,1},{1,2},{2,3},{3,4},{4,5},{5,6},{6,7},{7,8},{8,9},{9,10},{10,1... | collective-permute-start | bytes 1314824 | tf_op jit(solution)/shard_map/ppermute | solution.py:363
  18.0 16.4 %collective-permute-start.3 = (f32[856,128]{1,0:T(8,128)S(1)}, f32[856,128]{1,0:T(8,128)S(1)}, u32[]{:S(2)}, u32[]{:S(2)}) collective-permute-start(f32[856,128]{1,0:T(8,128)S(1)} %get-tuple-element.19), channel_id=1, source_target_pairs={{1,0},{2,1},{3,2},{4,3},{5,4},{6,5},{7,6},{8,7},{9,8},{10,9},{11,1... | collective-permute-start | bytes 1314824 | tf_op jit(solution)/shard_map/ppermute | solution.py:364
  36.6 9.4 %collective-permute-start.5 = (f32[2,112,128]{2,1,0:T(8,128)S(1)}, f32[2,112,128]{2,1,0:T(8,128)S(1)}, u32[]{:S(2)}, u32[]{:S(2)}) collective-permute-start(f32[2,112,128]{2,1,0:T(8,128)S(1)} %get-tuple-element.21.two_ref), channel_id=1, source_target_pairs={{1,0},{2,1},{3,2},{4,3},{5,4},{6,5},{7,6},{8,7},{9,8},{10,9},{11,1... | collective-permute-start | bytes 344072 | tf_op jit(solution)/shard_map/ppermute | solution.py:369
  44.1 8.9 %collective-permute-start.4 = (f32[2,112,128]{2,1,0:T(8,128)S(1)}, f32[2,112,128]{2,1,0:T(8,128)S(1)}, u32[]{:S(2)}, u32[]{:S(2)}) collective-permute-start(f32[2,112,128]{2,1,0:T(8,128)S(1)} %get-tuple-element.21.two_ref), channel_id=1, source_target_pairs={{0,1},{1,2},{2,3},{3,4},{4,5},{5,6},{6,7},{7,8},{8,9},{9,10},{10,1... | collective-permute-start | bytes 344072 | tf_op jit(solution)/shard_map/ppermute | solution.py:368

commit v2 on v0

v2 whole, which is shorter than its diff:
```python
import jax
import jax.numpy as jnp
from jax import lax
from jax.experimental import pallas as pl
from jax.experimental.pallas import tpu as pltpu
from jax.sharding import PartitionSpec as P

ITERS = 4
HALO = 2 * ITERS
BLOCK = 128
CENTRE = 1.0
WIDTH = 0.6
VMEM = pl.BlockSpec(memory_space=pltpu.VMEM)
SMEM = pl.BlockSpec(memory_space=pltpu.SMEM)
F32 = jnp.float32
BF16 = jnp.bfloat16
TERMS = ((0, 0), (1, 0), (1, -1), (2, 0), (2, -2))


def parts_of(array, count):
    parts = []
    for _ in range(count):
        part = array.astype(BF16)
        parts.append(part)
        array = array - part.astype(F32)
    return parts


def dot(left, right):
    return jnp.dot(left, right, preferred_element_type=F32)


def local_product(vectors, weights):
    first, second, third = parts_of(jnp.concatenate(vectors, axis=1), 3)
    return dot(
        jnp.concatenate([first, second, third, first, second], axis=1), weights[...]
    )


def cross_product(vector, block):
    return dot(
        jnp.concatenate(parts_of(vector, 3), axis=1), jnp.concatenate([block] * 3, axis=0)
    )


def moved(rows, offset):
    return pltpu.roll(rows, (-offset) % rows.shape[0], 0)


def band_apply(bands, spatial):
    result = None
    for matrix in range(2):
        rows = spatial[:, matrix * BLOCK : (matrix + 1) * BLOCK]
        for index, offset in enumerate((0, 1, -1, 2, -2)):
            term = bands[5 * matrix + index] * (moved(rows, offset) if offset else rows)
            result = term if result is None else result + term
    return result


def weights_kernel(
    lists, pattern, bands_row, mass, stiff,
    bands_ref, flag_ref, diagonal_ref, local_ref, into_ref, out_ref,
    *, time_rows, time_total,
):
    part = lax.axis_index("space")
    low = lists[0, 0, part]
    high = 1 - low
    own = (low, high)
    flag_ref[...] = jnp.full((8, BLOCK), low.astype(F32))
    extent = time_rows + 2 * HALO
    lines = []
    for matrix in range(2):
        for band, offset in TERMS:
            line = bands_row[band, matrix : matrix + 1, :]
            lines.append(pltpu.roll(line, (-(2 + offset)) % BLOCK, 1))
    lines.append(jnp.zeros((BLOCK - len(lines), BLOCK), F32))
    columns = jnp.concatenate(lines, axis=0).T
    for index in range(10):
        bands_ref[index] = jnp.broadcast_to(
            columns[:extent, index : index + 1], (extent, BLOCK)
        )
    time = lax.broadcasted_iota(jnp.int32, (extent, BLOCK), 0) - HALO
    time = time + lax.axis_index("tm") * time_rows
    bands_ref[10] = jnp.where((time >= 0) & (time < time_total), 1.0, 0.0)
    eye = lax.broadcasted_iota(jnp.int32, (BLOCK, BLOCK), 0) == lax.broadcasted_iota(
        jnp.int32, (BLOCK, BLOCK), 1
    )
    for place in range(2):
        for matrix, ref in enumerate((mass, stiff)):
            row = 2 * place + matrix
            diagonal_ref[row : row + 1] = jnp.sum(
                jnp.where(eye, ref[own[place], 0].astype(F32), 0.0), axis=0, keepdims=True
            )
    diagonal_ref[4:] = jnp.zeros((4, BLOCK), F32)
    for matrix, ref in enumerate((mass, stiff)):
        for col in range(2):
            lanes = slice((2 * col + matrix) * BLOCK, (2 * col + matrix + 1) * BLOCK)
            for row in range(2):
                if row == col:
                    total = ref[own[row], 0].astype(F32)
                else:
                    total = jnp.zeros((BLOCK, BLOCK), F32)
                for j in (2, 3):
                    named = pattern[own[row], j] == own[col]
                    total = total + jnp.where(named, ref[own[row], j].astype(F32), 0.0)
                lead, rest = parts_of(total, 2)
                for k, value in enumerate((lead, lead, lead, rest, rest)):
                    start = (2 * k + row) * BLOCK
                    local_ref[start : start + BLOCK, lanes] = value
        lanes = slice(matrix * BLOCK, (matrix + 1) * BLOCK)
        for place in range(2):
            block = ref[own[place], 1]
            out_ref[place, :, lanes] = block
            into_ref[place, :, lanes] = block.astype(F32).T.astype(BF16)


def stepped(scale, applied, inverse, vector, older):
    result = scale * (inverse * applied - CENTRE * vector)
    return result if older is None else result - older


def prepare_kernel(
    right, obs, before, after, bands, flag, diagonal, local,
    precond_ref, obs_ref, down_ref, up_ref,
):
    swapped = flag[0:1] > 0.5
    rhs = jnp.concatenate([before[:HALO], right[...], after[:HALO]], axis=0)
    precision = jnp.concatenate([before[HALO:], obs[...], after[HALO:]], axis=0)

    def chain(array):
        first, second = array[:, :BLOCK], array[:, BLOCK:]
        return jnp.where(swapped, second, first), jnp.where(swapped, first, second)

    rhs, precision = chain(rhs), chain(precision)
    valid = bands[10]
    scaled, inverses = [], []
    for place in range(2):
        precond = bands[0] * diagonal[2 * place : 2 * place + 1]
        precond = precond + bands[5] * diagonal[2 * place + 1 : 2 * place + 2]
        precond = precond + precision[place] + (1.0 - valid)
        precond_ref[place] = precond
        obs_ref[place] = precision[place]
        inverses.append(valid / precond)
        scaled.append(rhs[place] * inverses[place])
    spatial = local_product(scaled, local)
    for place, ref in enumerate((down_ref, up_ref)):
        applied = band_apply(bands, spatial[:, 2 * place * BLOCK : 2 * (place + 1) * BLOCK])
        applied = applied + precision[place] * scaled[place]
        ref[0] = scaled[place]
        ref[1] = stepped(1.0 / WIDTH, applied, inverses[place], scaled[place], None)
        ref[2] = inverses[place]


def completed(scale, bands, block, vector, partial, inverse):
    return partial + scale * (inverse * band_apply(bands, cross_product(vector, block)))


def full_step(bands, local, into, vectors, nears, precision, inverses, olders):
    spatial = local_product(vectors, local)
    results = []
    for place in range(2):
        mine = spatial[:, 2 * place * BLOCK : 2 * (place + 1) * BLOCK]
        mine = mine + cross_product(nears[place], into[place])
        applied = band_apply(bands, mine) + precision[place] * vectors[place]
        results.append(
            stepped(2.0 / WIDTH, applied, inverses[place], vectors[place], olders[place])
        )
    return results


def first_kernel(
    down, up, below, above, obs, bands, local, into, out,
    one_ref, down_two_ref, up_two_ref,
):
    own, sides = (down, up), (below, above)
    scale = 1.0 / WIDTH
    inverses = [ref[2] for ref in own]
    vectors = [
        completed(scale, bands, into[k], sides[k][0], own[k][1], inverses[k]) for k in range(2)
    ]
    nears = [
        completed(scale, bands, out[k], own[k][0], sides[k][1], sides[k][2]) for k in range(2)
    ]
    olders = [ref[0] for ref in own]
    two = full_step(bands, local, into, vectors, nears, obs, inverses, olders)
    spatial = local_product(two, local)
    for place, ref in enumerate((down_two_ref, up_two_ref)):
        one_ref[place] = vectors[place]
        applied = band_apply(bands, spatial[:, 2 * place * BLOCK : 2 * (place + 1) * BLOCK])
        applied = applied + obs[place] * two[place]
        ref[0] = two[place]
        ref[1] = stepped(2.0 / WIDTH, applied, inverses[place], two[place], vectors[place])


def second_kernel(
    down, up, below, above, one, down_two, up_two, below_two, above_two, precond, obs,
    bands, local, into, out,
    three_ref, four_ref, sums_ref,
):
    own, sides = (down, up), (below, above)
    own_two, sides_two = (down_two, up_two), (below_two, above_two)
    scale = 2.0 / WIDTH
    inverses = [ref[2] for ref in own]
    vectors = [
        completed(scale, bands, into[k], sides_two[k][0], own_two[k][1], inverses[k])
        for k in range(2)
    ]
    nears = [
        completed(scale, bands, out[k], own_two[k][0], sides_two[k][1], sides[k][2])
        for k in range(2)
    ]
    olders = [ref[0] for ref in own_two]
    four = full_step(bands, local, into, vectors, nears, obs, inverses, olders)
    extent = bands.shape[1]
    inside = slice(HALO, extent - HALO)
    sums = [0.0] * 14
    for place in range(2):
        three_ref[place] = vectors[place]
        four_ref[place] = four[place]
        basis = (own[place][0], one[place], olders[place], vectors[place], four[place])
        basis = [rows[inside] for rows in basis]
        index = 0
        for i in range(4):
            weighted = precond[place][inside] * basis[i]
            for j in range(i, 5):
                term = (weighted * basis[j]).reshape(-1, 8, BLOCK)
                sums[index] = sums[index] + jnp.sum(term, axis=0)
                index += 1
    rows = [jnp.sum(part, axis=0, keepdims=True) for part in sums]
    table = jnp.concatenate(rows + [jnp.zeros((2, BLOCK), F32)], axis=0)
    totals = jnp.sum(table, axis=1, keepdims=True)
    slots = lax.broadcasted_iota(jnp.int32, (16, BLOCK), 0) == lax.broadcasted_iota(
        jnp.int32, (16, BLOCK), 1
    )
    sums_ref[...] = jnp.sum(jnp.where(slots, totals, 0.0), axis=0, keepdims=True)


def added(terms):
    while len(terms) > 1:
        terms = [
            terms[k] + terms[k + 1] if k + 1 < len(terms) else terms[k]
            for k in range(0, len(terms), 2)
        ]
    return terms[0]


def operator(vector, degree):
    result = [[] for _ in range(5)]
    for j in range(degree + 1):
        result[j].append(CENTRE * vector[j])
        if j == 0:
            result[1].append(WIDTH * vector[0])
        else:
            result[j + 1].append((0.5 * WIDTH) * vector[j])
            result[j - 1].append((0.5 * WIDTH) * vector[j])
    return [added(terms) if terms else None for terms in result]


def inner_product(table, left, right):
    terms = []
    for i, a in enumerate(left):
        if a is not None:
            row = [
                table[(min(i, j), max(i, j))] * b for j, b in enumerate(right) if b is not None
            ]
            terms.append(a * added(row))
    return added(terms)


def combined(first, factor, second):
    result = []
    for a, b in zip(first, second):
        if b is None:
            result.append(a)
        else:
            result.append(factor * b if a is None else a + factor * b)
    return result


def final_kernel(
    flag, parts, down, up, one, down_two, up_two, three, four, precond,
    solution_ref, residual_ref,
):
    rows = jnp.sum(parts[...], axis=0, keepdims=True)
    lane = lax.broadcasted_iota(jnp.int32, (1, BLOCK), 1)
    table = {}
    index = 0
    for i in range(4):
        for j in range(i, 5):
            table[(i, j)] = jnp.sum(jnp.where(lane == index, rows, 0.0), axis=1, keepdims=True)
            index += 1
    state = [jnp.ones((1, 1), F32)] + [None] * 4
    direction = list(state)
    answer = [None] * 5
    norm_now = table[(0, 0)]
    for iteration in range(ITERS):
        applied = operator(direction, iteration)
        step = norm_now / inner_product(table, direction, applied)
        answer = combined(answer, step, direction)
        state = combined(state, -step, applied)
        if iteration + 1 < ITERS:
            norm_next = inner_product(table, state, state)
            direction = combined(state, norm_next / norm_now, direction)
            norm_now = norm_next
    swapped = flag[0:1] > 0.5
    inside = slice(HALO, HALO + solution_ref.shape[0])
    solutions, residuals = [], []
    for place, (ref, ref_two) in enumerate(((down, down_two), (up, up_two))):
        basis = (ref[0], one[place], ref_two[0], three[place], four[place])
        basis = [rows[inside] for rows in basis]
        solutions.append(added([answer[k] * basis[k] for k in range(4)]))
        left = added([state[k] * basis[k] for k in range(5)])
        residuals.append(left * precond[place][inside])
    for ref, pair in ((solution_ref, solutions), (residual_ref, residuals)):
        ref[:, :BLOCK] = jnp.where(swapped, pair[1], pair[0])
        ref[:, BLOCK:] = jnp.where(swapped, pair[0], pair[1])


def call(kernel, shapes, *operands, scalars=0, flops=0):
    return pl.pallas_call(
        kernel,
        out_shape=[
            shape if isinstance(shape, jax.ShapeDtypeStruct) else jax.ShapeDtypeStruct(shape, F32)
            for shape in shapes
        ],
        in_specs=[SMEM] * scalars + [VMEM] * (len(operands) - scalars),
        out_specs=[VMEM] * len(shapes),
        compiler_params=pltpu.CompilerParams(vmem_limit_bytes=32 * 1024 * 1024),
        cost_estimate=pl.CostEstimate(flops=flops, bytes_accessed=1 << 20, transcendentals=0),
    )(*operands)


def ring(axis, wrap):
    devices = lax.axis_size(axis)
    up = [(i, (i + 1) % devices) for i in range(devices if wrap else devices - 1)]
    return up, [(j, i) for i, j in up]


def shards(
    right_side, obs_precision, mass_blocks, stiff_blocks, block_pattern, send_lists, time_bands
):
    time_rows = right_side.shape[0]
    time_total = time_bands.shape[2]
    extent = time_rows + 2 * HALO

    up, down = ring("tm", False)
    last = jnp.concatenate([right_side[-HALO:], obs_precision[-HALO:]], axis=0)
    first = jnp.concatenate([right_side[:HALO], obs_precision[:HALO]], axis=0)
    before = lax.ppermute(last, "tm", up)
    after = lax.ppermute(first, "tm", down)

    margin = HALO + 2
    padded = jnp.pad(time_bands.transpose(1, 0, 2), ((0, 0), (0, 0), (margin, BLOCK)))
    bands_row = lax.dynamic_slice_in_dim(
        padded, lax.axis_index("tm") * time_rows, BLOCK, 2
    )
    wide = 2 * BLOCK
    bands, flag, diagonal, local, into, out = call(
        lambda *refs: weights_kernel(*refs, time_rows=time_rows, time_total=time_total),
        [
            (11, extent, BLOCK),
            (8, BLOCK),
            (8, BLOCK),
            jax.ShapeDtypeStruct((5 * wide, 2 * wide), BF16),
            jax.ShapeDtypeStruct((2, BLOCK, wide), BF16),
            jax.ShapeDtypeStruct((2, BLOCK, wide), BF16),
        ],
        send_lists.transpose(1, 2, 0), block_pattern, bands_row, mass_blocks, stiff_blocks,
        scalars=2, flops=1 << 21,
    )

    pair = (2, extent, BLOCK)
    triple = (3, extent, BLOCK)
    precond, precision, to_down, to_up = call(
        prepare_kernel, [pair, pair, triple, triple],
        right_side, obs_precision, before, after, bands, flag, diagonal, local,
    )
    up, down = ring("space", True)
    below = lax.ppermute(to_up, "space", up)
    above = lax.ppermute(to_down, "space", down)
    one, down_two, up_two = call(
        first_kernel, [pair, pair, pair],
        to_down, to_up, below, above, precision, bands, local, into, out,
    )
    below_two = lax.ppermute(up_two, "space", up)
    above_two = lax.ppermute(down_two, "space", down)
    three, four, sums = call(
        second_kernel, [pair, pair, (1, BLOCK)],
        to_down, to_up, below, above, one, down_two, up_two, below_two, above_two,
        precond, precision, bands, local, into, out,
    )
    for axis in ("space", "tm"):
        devices = lax.axis_size(axis)
        sent = jnp.broadcast_to(sums[None], (devices, 1, BLOCK))
        gathered = lax.all_to_all(sent, axis, 0, 0)
        sums = jnp.sum(gathered, axis=0)
    return tuple(
        call(
            final_kernel, [right_side.shape, right_side.shape],
            flag, sums, to_down, to_up, one, down_two, up_two, three, four, precond,
        )
    )


def solution(mesh):
    placed = (
        P("tm", "space"),
        P("tm", "space"),
        P("space", None, None, None),
        P("space", None, None, None),
        P("space", None),
        P(),
        P(),
    )
    return jax.shard_map(
        shards,
        mesh=mesh,
        in_specs=placed,
        out_specs=(P("tm", "space"), P("tm", "space")),
        check_vma=False,
    )
```

time: 818 us -> 81.6 us (0.10)
  blocking collectives: 674 us -> 33.1 us
  starting transfers between devices: 54 us -> 21.8 us
  waiting for transfers between devices: 36.4 us -> 13.4 us
  other arithmetic: 21 us -> 0.04 us
  between operations: 11.3 us -> 0.75 us
  local copies, waits for them, and re-layouts: 15.9 us -> 6.6 us
    psum x7 -> x0, blocking collectives: 674 us -> none  [the longest x3 289 us: shards(): lax.psum(jnp.sum(direction * applied), ('tm', 'space'))]
    all_to_all x0 -> x2, blocking collectives: none -> 33.1 us  [shards(): gathered = lax.all_to_all(sent, axis, 0, 0)]
    ppermute x16 -> x6, starting transfers between devices: 54 us -> 21.8 us  [the longest x1 5.38 us: shards(): before = lax.ppermute(last, 'tm', up)]
    ppermute x16 -> x6, waiting for transfers between devices: 36.4 us -> 13.4 us  [the longest x1 6.04 us: shards(): below = lax.ppermute(to_up, 'space', up)]
    convert_element_type x2 -> x0, other arithmetic: 13 us -> none  [the longest x1 6.53 us: shards(): mass_blocks[:, 0].astype(jnp.float32)]
  transfers between devices with their start and end apart: 16 -> 6, of which waited for: 8 -> 4; matrix products, arithmetic and copies ran while one was open for 0% -> 1% of each run, Pallas kernels for 0% -> 2%
where the time goes in v2:
time: 81.6 us; the launch traced here: 81.1 us
  blocking collectives  33.1 us (41%)
  starting transfers between devices  21.8 us (27%)
  waiting for transfers between devices  13.4 us (16%)
  local copies, waits for them, and re-layouts  6.6 us (8%)
  Pallas kernels  5.47 us (7%)
    all_to_all x2, blocking collectives, shards(): gathered = lax.all_to_all(sent, axis, 0, 0)  33.1 us
    ppermute x1, waiting for transfers between devices, shards(): below = lax.ppermute(to_up, 'space', up)  6.04 us
    pallas_call x5, Pallas kernels, call(): pl.pallas_call(kernel, out_shape=[shape if isinstance(shape, jax.ShapeDty...  5.47 us
    ppermute x1, starting transfers between devices, shards(): before = lax.ppermute(last, 'tm', up)  5.38 us
    ppermute x1, waiting for transfers between devices, shards(): below_two = lax.ppermute(up_two, 'space', up)  5.25 us
    unnamed x12, local copies, waits for them, and re-layouts  5.04 us
    ppermute x1, starting transfers between devices, shards(): after = lax.ppermute(first, 'tm', down)  4.69 us
    ppermute x1, starting transfers between devices, shards(): above = lax.ppermute(to_down, 'space', down)  4.52 us
  transfers between devices with their start and end apart: 6, of which 4 were waited for; matrix products, arithmetic and copies ran while one was open for 1% of the time, Pallas kernels for 2%

profile of v2, /device:TPU:1, one launch (start us, length us, event | category | flops | bytes accessed | tf_op | source)
XLA Modules:
  0.0 81.1 jit_solution(16322002673509921894)
XLA Ops:
  0.6 0.8 fusion
  1.4 5.4 %collective-permute-start = (f32[16,256]{1,0:T(8,128)S(1)}, f32[16,256]{1,0:T(8,128)S(1)}, u32[]{:S(2)}, u32[]{:S(2)}) collective-permute-start(f32[16,256]{1,0:T(8,128)S(1)} %pad_maximum_fusion), channel_id=1, source_target_pairs={{0,32},{32,64},{64,96},{96,128},{128,160},{160,192},{192,224},{224... | collective-permute-start | bytes 49160 | tf_op jit(solution)/shard_map/ppermute | solution.py:349
  6.8 4.7 %collective-permute-start.1 = (f32[16,256]{1,0:T(8,128)S(1)}, f32[16,256]{1,0:T(8,128)S(1)}, u32[]{:S(2)}, u32[]{:S(2)}) collective-permute-start(f32[16,256]{1,0:T(8,128)S(1)} %pad_maximum_fusion.1), channel_id=1, source_target_pairs={{32,0},{64,32},{96,64},{128,96},{160,128},{192,160},{224,192},{256... | collective-permute-start | bytes 49160 | tf_op jit(solution)/shard_map/ppermute | solution.py:350
  11.5 0.8 pad_dynamic-slice_fusion.refs_2_
  12.3 0.0 copy-start
  12.3 0.9 %copy-done = bf16[2,4,128,128]{3,2,1,0:T(8,128)(2,1)S(1)} copy-done((bf16[2,4,128,128]{3,2,1,0:T(8,128)(2,1)S(1)}, bf16[2,4,128,128]{3,2,1,0:T(8,128)(2,1)}, u32[]{:S(2)}) %copy-start) | copy-done | bytes 262168
  13.2 0.0 copy-start.1
  13.2 0.9 %copy-done.1 = bf16[2,4,128,128]{3,2,1,0:T(8,128)(2,1)S(1)} copy-done((bf16[2,4,128,128]{3,2,1,0:T(8,128)(2,1)S(1)}, bf16[2,4,128,128]{3,2,1,0:T(8,128)(2,1)}, u32[]{:S(2)}) %copy-start.1) | copy-done | bytes 262168
  14.2 0.0 copy-start.4
  14.2 0.7 copy-done.4
  14.9 0.0 copy-start.5
  14.9 0.7 copy-done.5
  15.5 1.3 %shard_map.86 = (f32[11,112,128]{2,1,0:T(8,128)S(1)}, f32[8,128]{1,0:T(8,128)S(1)}, f32[8,128]{1,0:T(8,128)S(1)}, bf16[1280,512]{1,0:T(8,128)(2,1)S(1)}, bf16[2,...) custom-call(s32[2,1,32]{2,1,0:T(1,128)S(1)} %bitcast.7, s32[2,4]{1,0:T(2,128)S(1)} %copy-done.5, ...), custom_call_target="tpu_custom_call" | custom-call | flops 2097152 | bytes 1048576 | tf_op jit(solution)/shard_map/pallas_call | solution.py:320
  16.8 0.0 collective-permute-done.before
  16.8 0.0 collective-permute-done.1.after
  16.9 0.0 copy-start.2
  16.9 0.9 %copy-done.2 = f32[96,256]{1,0:T(8,128)S(1)} copy-done((f32[96,256]{1,0:T(8,128)S(1)}, f32[96,256]{1,0:T(8,128)}, u32[]{:S(2)}) %copy-start.2) | copy-done | bytes 98328
  17.8 0.0 copy-start.3
  17.8 0.9 %copy-done.3 = f32[96,256]{1,0:T(8,128)S(1)} copy-done((f32[96,256]{1,0:T(8,128)S(1)}, f32[96,256]{1,0:T(8,128)}, u32[]{:S(2)}) %copy-start.3) | copy-done | bytes 98328
  18.6 0.5 shard_map.87
  19.1 4.5 %collective-permute-start.3 = (f32[3,112,128]{2,1,0:T(8,128)S(1)}, f32[3,112,128]{2,1,0:T(8,128)S(1)}, u32[]{:S(2)}, u32[]{:S(2)}) collective-permute-start(f32[3,112,128]{2,1,0:T(8,128)S(1)} %get-tuple-element.22.down), channel_id=1, source_target_pairs={{1,0},{2,1},{3,2},{4,3},{5,4},{6,5},{7,6},{8,7},{9,8},{10,9},{11,1... | collective-permute-start | bytes 516104 | tf_op jit(solution)/shard_map/ppermute | solution.py:380
  23.7 1.9 %collective-permute-start.2 = (f32[3,112,128]{2,1,0:T(8,128)S(1)}, f32[3,112,128]{2,1,0:T(8,128)S(1)}, u32[]{:S(2)}, u32[]{:S(2)}) collective-permute-start(f32[3,112,128]{2,1,0:T(8,128)S(1)} %get-tuple-element.23.up), channel_id=1, source_target_pairs={{0,1},{1,2},{2,3},{3,4},{4,5},{5,6},{6,7},{7,8},{8,9},{9,10},{10,1... | collective-permute-start | bytes 516104 | tf_op jit(solution)/shard_map/ppermute | solution.py:379
  25.6 1.5 %collective-permute-done.3.above = f32[3,112,128]{2,1,0:T(8,128)S(1)} collective-permute-done((f32[3,112,128]{2,1,0:T(8,128)S(1)}, f32[3,112,128]{2,1,0:T(8,128)S(1)}, u32[]{:S(2)}, u32[]{:S(2)}) %collective-permute-start.3) | collective-permute-done | bytes 172064 | tf_op jit(solution)/shard_map/ppermute | solution.py:380
  27.1 6.0 %collective-permute-done.2.below = f32[3,112,128]{2,1,0:T(8,128)S(1)} collective-permute-done((f32[3,112,128]{2,1,0:T(8,128)S(1)}, f32[3,112,128]{2,1,0:T(8,128)S(1)}, u32[]{:S(2)}, u32[]{:S(2)}) %collective-permute-start.2) | collective-permute-done | bytes 172064 | tf_op jit(solution)/shard_map/ppermute | solution.py:379
  33.1 1.5 %shard_map.88 = (f32[2,112,128]{2,1,0:T(8,128)S(1)}, f32[2,112,128]{2,1,0:T(8,128)S(1)}, f32[2,112,128]{2,1,0:T(8,128)S(1)}) custom-call(f32[3,112,128]{2,1,0:T(8,128)S(1)} %get-tuple-element.22.down, f32[3,112,128]{2,1,0:T(8,128)S(1)} %get-tuple-element.23.up, f32[3,112,128]{2,1,0:T(8,128)S(1)} %collective-permute-done.2.below, ...), custom_call_target="tpu_custom_call" | custom-call | bytes 1048576 | tf_op jit(solution)/shard_map/pallas_call | solution.py:320
  34.7 1.9 %collective-permute-start.5 = (f32[2,112,128]{2,1,0:T(8,128)S(1)}, f32[2,112,128]{2,1,0:T(8,128)S(1)}, u32[]{:S(2)}, u32[]{:S(2)}) collective-permute-start(f32[2,112,128]{2,1,0:T(8,128)S(1)} %get-tuple-element.28.down_two), channel_id=1, source_target_pairs={{1,0},{2,1},{3,2},{4,3},{5,4},{6,5},{7,6},{8,7},{9,8},{10,9},{11,1... | collective-permute-start | bytes 344072 | tf_op jit(solution)/shard_map/ppermute | solution.py:386
  36.6 3.4 %collective-permute-start.4 = (f32[2,112,128]{2,1,0:T(8,128)S(1)}, f32[2,112,128]{2,1,0:T(8,128)S(1)}, u32[]{:S(2)}, u32[]{:S(2)}) collective-permute-start(f32[2,112,128]{2,1,0:T(8,128)S(1)} %get-tuple-element.29.up_two), channel_id=1, source_target_pairs={{0,1},{1,2},{2,3},{3,4},{4,5},{5,6},{6,7},{7,8},{8,9},{9,10},{10,1... | collective-permute-start | bytes 344072 | tf_op jit(solution)/shard_map/ppermute | solution.py:385
  40.0 0.6 collective-permute-done.5.above_two
  40.6 5.2 %collective-permute-done.4.below_two = f32[2,112,128]{2,1,0:T(8,128)S(1)} collective-permute-done((f32[2,112,128]{2,1,0:T(8,128)S(1)}, f32[2,112,128]{2,1,0:T(8,128)S(1)}, u32[]{:S(2)}, u32[]{:S(2)}) %collective-permute-start.4) | collective-permute-done | bytes 114720 | tf_op jit(solution)/shard_map/ppermute | solution.py:385
  45.8 1.2 %shard_map.89 = (f32[2,112,128]{2,1,0:T(8,128)S(1)}, f32[2,112,128]{2,1,0:T(8,128)S(1)}, f32[1,128]{1,0:T(1,128)S(1)}) custom-call(f32[3,112,128]{2,1,0:T(8,128)S(1)} %get-tuple-element.22.down, f32[3,112,128]{2,1,0:T(8,128)S(1)} %get-tuple-element.23.up, f32[3,112,128]{2,1,0:T(8,128)S(1)} %collective-permute-done.2.below, ...), custom_call_target="tpu_custom_call" | custom-call | bytes 1048576 | tf_op jit(solution)/shard_map/pallas_call | solution.py:320
  47.1 11.6 %all_to_all.10 = f32[32,1,128]{2,1,0:T(1,128)S(1)} all-to-all(f32[32,1,128]{2,1,0:T(1,128)S(1)} %broadcast_in_dim.7), channel_id=1, replica_groups=mesh['tm'=16,'space'=32] {'space'}, dimensions={0} | all-to-all | bytes 32768 | tf_op jit(solution)/shard_map/all_to_all | solution.py:395
  58.7 21.5 %all_to_all.11 = f32[16,1,128]{2,1,0:T(1,128)S(1)} all-to-all(f32[16,1,128]{2,1,0:T(1,128)S(1)} %broadcast_in_dim.16), channel_id=1, replica_groups=mesh['tm'=16,'space'=32] {'tm'}, dimensions={0} | all-to-all | bytes 16384 | tf_op jit(solution)/shard_map/all_to_all | solution.py:395
  80.2 0.9 %shard_map.90 = (f32[96,256]{1,0:T(8,128)}, f32[96,256]{1,0:T(8,128)}) custom-call(f32[8,128]{1,0:T(8,128)S(1)} %get-tuple-element.18.flag, f32[1,128]{1,0:T(1,128)S(1)} %bitcast.6, f32[3,112,128]{2,1,0:T(8,128)S(1)} %get-tuple-element.22.down, f32[3,112,128]{2,1,0:T(8,128)S(1)} %get-tuple-element.23.up, f32[2,112,128]{2,1,0:T(8,128)S(1)} %get-tuple-element.27.one, ...), custom_call_target="tpu_custom_call" | custom-call | bytes 1048576 | tf_op jit(solution)/shard_map/pallas_call | solution.py:320
  (6 shorter events, 0.1 us)
Async XLA Ops:
  1.4 15.5 %collective-permute-start = (f32[16,256]{1,0:T(8,128)S(1)}, f32[16,256]{1,0:T(8,128)S(1)}, u32[]{:S(2)}, u32[]{:S(2)}) collective-permute-start(f32[16,256]{1,0:T(8,128)S(1)} %pad_maximum_fusion), channel_id=1, source_target_pairs={{0,32},{32,64},{64,96},{96,128},{128,160},{160,192},{192,224},{224... | collective-permute-start | bytes 49160 | tf_op jit(solution)/shard_map/ppermute | solution.py:349
  6.8 10.1 %collective-permute-start.1 = (f32[16,256]{1,0:T(8,128)S(1)}, f32[16,256]{1,0:T(8,128)S(1)}, u32[]{:S(2)}, u32[]{:S(2)}) collective-permute-start(f32[16,256]{1,0:T(8,128)S(1)} %pad_maximum_fusion.1), channel_id=1, source_target_pairs={{32,0},{64,32},{96,64},{128,96},{160,128},{192,160},{224,192},{256... | collective-permute-start | bytes 49160 | tf_op jit(solution)/shard_map/ppermute | solution.py:350
  12.3 1.0 %copy-start = (bf16[2,4,128,128]{3,2,1,0:T(8,128)(2,1)S(1)}, bf16[2,4,128,128]{3,2,1,0:T(8,128)(2,1)}, u32[]{:S(2)}) copy-start(bf16[2,4,128,128]{3,2,1,0:T(8,128)(2,1)} %refs_3_.1) | copy-start | bytes 786436
  13.2 0.9 %copy-start.1 = (bf16[2,4,128,128]{3,2,1,0:T(8,128)(2,1)S(1)}, bf16[2,4,128,128]{3,2,1,0:T(8,128)(2,1)}, u32[]{:S(2)}) copy-start(bf16[2,4,128,128]{3,2,1,0:T(8,128)(2,1)} %refs_4_.1) | copy-start | bytes 786436
  14.2 0.7 copy-start.4
  14.9 0.7 copy-start.5
  16.9 0.9 %copy-start.2 = (f32[96,256]{1,0:T(8,128)S(1)}, f32[96,256]{1,0:T(8,128)}, u32[]{:S(2)}) copy-start(f32[96,256]{1,0:T(8,128)} %right.1) | copy-start | bytes 294916
  17.8 0.9 %copy-start.3 = (f32[96,256]{1,0:T(8,128)S(1)}, f32[96,256]{1,0:T(8,128)}, u32[]{:S(2)}) copy-start(f32[96,256]{1,0:T(8,128)} %obs.1) | copy-start | bytes 294916
  19.1 8.0 %collective-permute-start.3 = (f32[3,112,128]{2,1,0:T(8,128)S(1)}, f32[3,112,128]{2,1,0:T(8,128)S(1)}, u32[]{:S(2)}, u32[]{:S(2)}) collective-permute-start(f32[3,112,128]{2,1,0:T(8,128)S(1)} %get-tuple-element.22.down), channel_id=1, source_target_pairs={{1,0},{2,1},{3,2},{4,3},{5,4},{6,5},{7,6},{8,7},{9,8},{10,9},{11,1... | collective-permute-start | bytes 516104 | tf_op jit(solution)/shard_map/ppermute | solution.py:380
  23.7 9.5 %collective-permute-start.2 = (f32[3,112,128]{2,1,0:T(8,128)S(1)}, f32[3,112,128]{2,1,0:T(8,128)S(1)}, u32[]{:S(2)}, u32[]{:S(2)}) collective-permute-start(f32[3,112,128]{2,1,0:T(8,128)S(1)} %get-tuple-element.23.up), channel_id=1, source_target_pairs={{0,1},{1,2},{2,3},{3,4},{4,5},{5,6},{6,7},{7,8},{8,9},{9,10},{10,1... | collective-permute-start | bytes 516104 | tf_op jit(solution)/shard_map/ppermute | solution.py:379
  34.7 5.9 %collective-permute-start.5 = (f32[2,112,128]{2,1,0:T(8,128)S(1)}, f32[2,112,128]{2,1,0:T(8,128)S(1)}, u32[]{:S(2)}, u32[]{:S(2)}) collective-permute-start(f32[2,112,128]{2,1,0:T(8,128)S(1)} %get-tuple-element.28.down_two), channel_id=1, source_target_pairs={{1,0},{2,1},{3,2},{4,3},{5,4},{6,5},{7,6},{8,7},{9,8},{10,9},{11,1... | collective-permute-start | bytes 344072 | tf_op jit(solution)/shard_map/ppermute | solution.py:386
  36.6 9.2 %collective-permute-start.4 = (f32[2,112,128]{2,1,0:T(8,128)S(1)}, f32[2,112,128]{2,1,0:T(8,128)S(1)}, u32[]{:S(2)}, u32[]{:S(2)}) collective-permute-start(f32[2,112,128]{2,1,0:T(8,128)S(1)} %get-tuple-element.29.up_two), channel_id=1, source_target_pairs={{0,1},{1,2},{2,3},{3,4},{4,5},{5,6},{6,7},{7,8},{8,9},{9,10},{10,1... | collective-permute-start | bytes 344072 | tf_op jit(solution)/shard_map/ppermute | solution.py:385

commit v3 on v2

--- a/solution.py
+++ b/solution.py
@@ -11,7 +11,6 @@
 CENTRE = 1.0
 WIDTH = 0.6
 VMEM = pl.BlockSpec(memory_space=pltpu.VMEM)
-SMEM = pl.BlockSpec(memory_space=pltpu.SMEM)
 F32 = jnp.float32
 BF16 = jnp.bfloat16
 TERMS = ((0, 0), (1, 0), (1, -1), (2, 0), (2, -2))
@@ -58,60 +57,107 @@
 
 
 def weights_kernel(
-    lists, pattern, bands_row, mass, stiff,
-    bands_ref, flag_ref, diagonal_ref, local_ref, into_ref, out_ref,
-    *, time_rows, time_total,
-):
-    part = lax.axis_index("space")
-    low = lists[0, 0, part]
-    high = 1 - low
-    own = (low, high)
-    flag_ref[...] = jnp.full((8, BLOCK), low.astype(F32))
+    lists_hbm, pattern_hbm, bands_hbm, right_hbm, obs_hbm, mass_hbm, stiff_hbm,
+    bands_ref, flag_ref, diagonal_ref, local_ref, into_ref, out_ref, right_ref, obs_ref,
+    lists, pattern, band_rows, right, obs, mass, stiff, arrived,
+):
+    sources = (lists_hbm, pattern_hbm, bands_hbm, right_hbm, obs_hbm, mass_hbm, stiff_hbm)
+    targets = (lists, pattern, band_rows, right, obs, mass, stiff)
+    copies = [
+        pltpu.make_async_copy(source, target, arrived.at[index])
+        for index, (source, target) in enumerate(zip(sources, targets))
+    ]
+    for copy in copies:
+        copy.start()
+    for copy in copies[:5]:
+        copy.wait()
+    time_rows, time_total = right.shape[0], band_rows.shape[2]
     extent = time_rows + 2 * HALO
+
+    first = lax.axis_index("tm") * time_rows - HALO - 2
+    tile = (first + time_total) // BLOCK - time_total // BLOCK
+    shift = first - tile * BLOCK
+    last_tile = time_total // BLOCK - 1
+    lane = lax.broadcasted_iota(jnp.int32, (1, BLOCK), 1)
+    time = first + lane
+    inside = (time >= 0) & (time < time_total)
+
+    def window(band, matrix):
+        halves = []
+        for index in (tile, tile + 1):
+            index = jnp.clip(index, 0, last_tile)
+            start = pl.multiple_of(index * BLOCK, BLOCK)
+            row = band_rows[band, :, pl.ds(start, BLOCK)][matrix : matrix + 1]
+            halves.append(pltpu.roll(row, (BLOCK - shift) % BLOCK, 1))
+        line = jnp.where(lane + shift < BLOCK, halves[0], halves[1])
+        return jnp.where(inside, line, 0.0)
+
     lines = []
     for matrix in range(2):
+        rows = [window(band, matrix) for band in range(3)]
         for band, offset in TERMS:
-            line = bands_row[band, matrix : matrix + 1, :]
-            lines.append(pltpu.roll(line, (-(2 + offset)) % BLOCK, 1))
-    lines.append(jnp.zeros((BLOCK - len(lines), BLOCK), F32))
+            lines.append(pltpu.roll(rows[band], (-(2 + offset)) % BLOCK, 1))
+    valid = jnp.where(inside, 1.0, 0.0)
+    lines.append(pltpu.roll(valid, BLOCK - 2, 1))
+    count = len(lines)
+    lines.append(jnp.zeros((BLOCK - count, BLOCK), F32))
     columns = jnp.concatenate(lines, axis=0).T
-    for index in range(10):
+    for index in range(count):
         bands_ref[index] = jnp.broadcast_to(
             columns[:extent, index : index + 1], (extent, BLOCK)
         )
-    time = lax.broadcasted_iota(jnp.int32, (extent, BLOCK), 0) - HALO
-    time = time + lax.axis_index("tm") * time_rows
-    bands_ref[10] = jnp.where((time >= 0) & (time < time_total), 1.0, 0.0)
+
+    entries = lists[0].astype(F32)
+    here = lax.broadcasted_iota(jnp.int32, entries.shape, 1) == lax.axis_index("space")
+    low = jnp.sum(jnp.where(here, entries, 0.0), axis=1, keepdims=True)
+    flag = jnp.broadcast_to(low, (8, BLOCK))
+    flag_ref[...] = flag
+    swapped = jnp.broadcast_to(low, (BLOCK, BLOCK)) > 0.5
+    for ref, source in ((right_ref, right), (obs_ref, obs)):
+        one, two = source[:, :BLOCK], source[:, BLOCK:]
+        turned = jnp.broadcast_to(low, one.shape) > 0.5
+        ref[0] = jnp.where(turned, two, one)
+        ref[1] = jnp.where(turned, one, two)
+    codes = pattern[...].astype(F32)
+    codes = (
+        low * codes[1:2] + (1.0 - low) * codes[0:1],
+        low * codes[0:1] + (1.0 - low) * codes[1:2],
+    )
+    own = (low, 1.0 - low)
+
+    for copy in copies[5:]:
+        copy.wait()
     eye = lax.broadcasted_iota(jnp.int32, (BLOCK, BLOCK), 0) == lax.broadcasted_iota(
         jnp.int32, (BLOCK, BLOCK), 1
     )
-    for place in range(2):
-        for matrix, ref in enumerate((mass, stiff)):
-            row = 2 * place + matrix
-            diagonal_ref[row : row + 1] = jnp.sum(
-                jnp.where(eye, ref[own[place], 0].astype(F32), 0.0), axis=0, keepdims=True
+    diagonals = [None] * 4
+    for matrix, ref in enumerate((mass, stiff)):
+
+        def block(place, j):
+            one, two = ref[place, j].astype(F32), ref[1 - place, j].astype(F32)
+            return jnp.where(swapped, two, one)
+
+        stored = [[block(place, j) for j in range(4)] for place in range(2)]
+        for place in range(2):
+            diagonals[2 * place + matrix] = jnp.sum(
+                jnp.where(eye, stored[place][0], 0.0), axis=0, keepdims=True
             )
-    diagonal_ref[4:] = jnp.zeros((4, BLOCK), F32)
-    for matrix, ref in enumerate((mass, stiff)):
         for col in range(2):
             lanes = slice((2 * col + matrix) * BLOCK, (2 * col + matrix + 1) * BLOCK)
             for row in range(2):
-                if row == col:
-                    total = ref[own[row], 0].astype(F32)
-                else:
-                    total = jnp.zeros((BLOCK, BLOCK), F32)
+                total = stored[row][0] if row == col else jnp.zeros((BLOCK, BLOCK), F32)
                 for j in (2, 3):
-                    named = pattern[own[row], j] == own[col]
-                    total = total + jnp.where(named, ref[own[row], j].astype(F32), 0.0)
+                    named = codes[row][:, j : j + 1] == own[col]
+                    total = total + jnp.where(named, 1.0, 0.0) * stored[row][j]
                 lead, rest = parts_of(total, 2)
                 for k, value in enumerate((lead, lead, lead, rest, rest)):
                     start = (2 * k + row) * BLOCK
                     local_ref[start : start + BLOCK, lanes] = value
         lanes = slice(matrix * BLOCK, (matrix + 1) * BLOCK)
         for place in range(2):
-            block = ref[own[place], 1]
-            out_ref[place, :, lanes] = block
-            into_ref[place, :, lanes] = block.astype(F32).T.astype(BF16)
+            out_ref[place, :, lanes] = stored[place][1].astype(BF16)
+            into_ref[place, :, lanes] = stored[place][1].T.astype(BF16)
+    diagonal_ref[...] = jnp.concatenate(diagonals + [jnp.zeros((4, BLOCK), F32)], axis=0)
 
 
 def stepped(scale, applied, inverse, vector, older):
@@ -123,15 +169,19 @@
     right, obs, before, after, bands, flag, diagonal, local,
     precond_ref, obs_ref, down_ref, up_ref,
 ):
-    swapped = flag[0:1] > 0.5
-    rhs = jnp.concatenate([before[:HALO], right[...], after[:HALO]], axis=0)
-    precision = jnp.concatenate([before[HALO:], obs[...], after[HALO:]], axis=0)
-
-    def chain(array):
-        first, second = array[:, :BLOCK], array[:, BLOCK:]
-        return jnp.where(swapped, second, first), jnp.where(swapped, first, second)
-
-    rhs, precision = chain(rhs), chain(precision)
+    swapped = flag[...] > 0.5
+
+    def extended(middle, start):
+        ends = []
+        for ref in (before, after):
+            rows = ref[start : start + HALO]
+            one, two = rows[:, :BLOCK], rows[:, BLOCK:]
+            ends.append((jnp.where(swapped, two, one), jnp.where(swapped, one, two)))
+        return [
+            jnp.concatenate([ends[0][k], middle[k], ends[1][k]], axis=0) for k in range(2)
+        ]
+
+    rhs, precision = extended(right, 0), extended(obs, HALO)
     valid = bands[10]
     scaled, inverses = [], []
     for place in range(2):
@@ -316,15 +366,16 @@
         ref[:, BLOCK:] = jnp.where(swapped, pair[0], pair[1])
 
 
-def call(kernel, shapes, *operands, scalars=0, flops=0):
+def call(kernel, shapes, *operands, space=VMEM, scratch=(), flops=0):
     return pl.pallas_call(
         kernel,
         out_shape=[
             shape if isinstance(shape, jax.ShapeDtypeStruct) else jax.ShapeDtypeStruct(shape, F32)
             for shape in shapes
         ],
-        in_specs=[SMEM] * scalars + [VMEM] * (len(operands) - scalars),
+        in_specs=[space] * len(operands),
         out_specs=[VMEM] * len(shapes),
+        scratch_shapes=scratch,
         compiler_params=pltpu.CompilerParams(vmem_limit_bytes=32 * 1024 * 1024),
         cost_estimate=pl.CostEstimate(flops=flops, bytes_accessed=1 << 20, transcendentals=0),
     )(*operands)
@@ -340,7 +391,6 @@
     right_side, obs_precision, mass_blocks, stiff_blocks, block_pattern, send_lists, time_bands
 ):
     time_rows = right_side.shape[0]
-    time_total = time_bands.shape[2]
     extent = time_rows + 2 * HALO
 
     up, down = ring("tm", False)
@@ -349,14 +399,14 @@
     before = lax.ppermute(last, "tm", up)
     after = lax.ppermute(first, "tm", down)
 
-    margin = HALO + 2
-    padded = jnp.pad(time_bands.transpose(1, 0, 2), ((0, 0), (0, 0), (margin, BLOCK)))
-    bands_row = lax.dynamic_slice_in_dim(
-        padded, lax.axis_index("tm") * time_rows, BLOCK, 2
-    )
     wide = 2 * BLOCK
-    bands, flag, diagonal, local, into, out = call(
-        lambda *refs: weights_kernel(*refs, time_rows=time_rows, time_total=time_total),
+    stored = (
+        send_lists.transpose(1, 2, 0), block_pattern, time_bands.transpose(1, 0, 2),
+        right_side, obs_precision, mass_blocks, stiff_blocks,
+    )
+    half = (2, time_rows, BLOCK)
+    bands, flag, diagonal, local, into, out, right, obs = call(
+        weights_kernel,
         [
             (11, extent, BLOCK),
             (8, BLOCK),
@@ -364,16 +414,21 @@
             jax.ShapeDtypeStruct((5 * wide, 2 * wide), BF16),
             jax.ShapeDtypeStruct((2, BLOCK, wide), BF16),
             jax.ShapeDtypeStruct((2, BLOCK, wide), BF16),
+            half,
+            half,
         ],
-        send_lists.transpose(1, 2, 0), block_pattern, bands_row, mass_blocks, stiff_blocks,
-        scalars=2, flops=1 << 21,
+        *[pltpu.with_memory_space_constraint(array, pltpu.HBM) for array in stored],
+        space=pl.BlockSpec(memory_space=pltpu.HBM),
+        scratch=[pltpu.VMEM(array.shape, array.dtype) for array in stored]
+        + [pltpu.SemaphoreType.DMA((len(stored),))],
+        flops=1 << 21,
     )
 
     pair = (2, extent, BLOCK)
     triple = (3, extent, BLOCK)
     precond, precision, to_down, to_up = call(
         prepare_kernel, [pair, pair, triple, triple],
-        right_side, obs_precision, before, after, bands, flag, diagonal, local,
+        right, obs, before, after, bands, flag, diagonal, local,
     )
     up, down = ring("space", True)
     below = lax.ppermute(to_up, "space", up)

time: 81.6 us -> 76.8 us (0.941)
  local copies, waits for them, and re-layouts: 6.6 us -> 0.78 us
  blocking collectives: 33.1 us -> 30.8 us
  waiting for transfers between devices: 13.4 us -> 15 us
  starting transfers between devices: 21.8 us -> 22.9 us
    unnamed x12 -> x0, local copies, waits for them, and re-layouts: 5.04 us -> none
    all_to_all x2, blocking collectives: 33.1 us -> 30.8 us  [shards(): gathered = lax.all_to_all(sent, axis, 0, 0)]
    ppermute x1, waiting for transfers between devices: 6.04 us -> 7.42 us  [shards(): below = lax.ppermute(to_up, 'space', up)]
    ppermute x1, starting transfers between devices: 4.52 us -> 5.63 us  [shards(): above = lax.ppermute(to_down, 'space', down)]
    ppermute x1, waiting for transfers between devices: 0.57 us -> 1.55 us  [shards(): above_two = lax.ppermute(down_two, 'space', down)]
  transfers between devices with their start and end apart: 6 -> 6, of which waited for: 4 -> 4; matrix products, arithmetic and copies ran while one was open for 1% -> 0% of each run, Pallas kernels for 2% -> 3%
where the time goes in v3:
time: 76.8 us; the launch traced here: 76.4 us
  blocking collectives  30.8 us (40%)
  starting transfers between devices  22.9 us (30%)
  waiting for transfers between devices  15 us (20%)
  Pallas kernels  6.2 us (8%)
  local copies, waits for them, and re-layouts  0.78 us (1%)
    all_to_all x2, blocking collectives, shards(): gathered = lax.all_to_all(sent, axis, 0, 0)  30.8 us
    ppermute x1, waiting for transfers between devices, shards(): below = lax.ppermute(to_up, 'space', up)  7.42 us
    pallas_call x5, Pallas kernels, call(): pl.pallas_call(kernel, out_shape=[shape if isinstance(shape, jax.ShapeDty...  6.2 us
    ppermute x1, starting transfers between devices, shards(): above = lax.ppermute(to_down, 'space', down)  5.63 us
    ppermute x1, starting transfers between devices, shards(): before = lax.ppermute(last, 'tm', up)  5.38 us
    ppermute x1, waiting for transfers between devices, shards(): below_two = lax.ppermute(up_two, 'space', up)  5.25 us
    ppermute x1, starting transfers between devices, shards(): after = lax.ppermute(first, 'tm', down)  4.69 us
    ppermute x1, starting transfers between devices, shards(): below_two = lax.ppermute(up_two, 'space', up)  3.36 us
  transfers between devices with their start and end apart: 6, of which 4 were waited for; matrix products, arithmetic and copies ran while one was open for 0% of the time, Pallas kernels for 3%

profile of v3, /device:TPU:1, one launch (start us, length us, event | category | flops | bytes accessed | tf_op | source)
XLA Modules:
  0.0 76.4 jit_solution(9069060524887044542)
XLA Ops:
  0.6 0.8 fusion
  1.4 5.4 %collective-permute-start = (f32[16,256]{1,0:T(8,128)S(1)}, f32[16,256]{1,0:T(8,128)S(1)}, u32[]{:S(2)}, u32[]{:S(2)}) collective-permute-start(f32[16,256]{1,0:T(8,128)S(1)} %pad_maximum_fusion), channel_id=1, source_target_pairs={{0,32},{32,64},{64,96},{96,128},{128,160},{160,192},{192,224},{224... | collective-permute-start | bytes 49160 | tf_op jit(solution)/shard_map/ppermute | solution.py:399
  6.8 4.7 %collective-permute-start.1 = (f32[16,256]{1,0:T(8,128)S(1)}, f32[16,256]{1,0:T(8,128)S(1)}, u32[]{:S(2)}, u32[]{:S(2)}) collective-permute-start(f32[16,256]{1,0:T(8,128)S(1)} %pad_maximum_fusion.1), channel_id=1, source_target_pairs={{32,0},{64,32},{96,64},{128,96},{160,128},{192,160},{224,192},{256... | collective-permute-start | bytes 49160 | tf_op jit(solution)/shard_map/ppermute | solution.py:400
  11.5 2.0 %shard_map.86 = (f32[11,112,128]{2,1,0:T(8,128)S(1)}, f32[8,128]{1,0:T(8,128)S(1)}, f32[8,128]{1,0:T(8,128)S(1)}, bf16[1280,512]{1,0:T(8,128)(2,1)S(1)}, bf16[2,...) custom-call(s32[2,1,32]{2,1,0:T(1,128)} %bitcast.11, ...), custom_call_target="tpu_custom_call" | custom-call | flops 2097152 | bytes 1048576 | tf_op jit(solution)/shard_map/pallas_call | solution.py:370
  13.5 0.0 collective-permute-done.before
  13.5 0.0 collective-permute-done.1.after
  13.5 0.5 shard_map.87
  14.0 5.6 %collective-permute-start.3 = (f32[3,112,128]{2,1,0:T(8,128)S(1)}, f32[3,112,128]{2,1,0:T(8,128)S(1)}, u32[]{:S(2)}, u32[]{:S(2)}) collective-permute-start(f32[3,112,128]{2,1,0:T(8,128)S(1)} %get-tuple-element.26.down), channel_id=1, source_target_pairs={{1,0},{2,1},{3,2},{4,3},{5,4},{6,5},{7,6},{8,7},{9,8},{10,9},{11,1... | collective-permute-start | bytes 516104 | tf_op jit(solution)/shard_map/ppermute | solution.py:435
  19.6 1.9 %collective-permute-start.2 = (f32[3,112,128]{2,1,0:T(8,128)S(1)}, f32[3,112,128]{2,1,0:T(8,128)S(1)}, u32[]{:S(2)}, u32[]{:S(2)}) collective-permute-start(f32[3,112,128]{2,1,0:T(8,128)S(1)} %get-tuple-element.27.up), channel_id=1, source_target_pairs={{0,1},{1,2},{2,3},{3,4},{4,5},{5,6},{6,7},{7,8},{8,9},{9,10},{10,1... | collective-permute-start | bytes 516104 | tf_op jit(solution)/shard_map/ppermute | solution.py:434
  21.6 0.7 collective-permute-done.3.above
  22.3 7.4 %collective-permute-done.2.below = f32[3,112,128]{2,1,0:T(8,128)S(1)} collective-permute-done((f32[3,112,128]{2,1,0:T(8,128)S(1)}, f32[3,112,128]{2,1,0:T(8,128)S(1)}, u32[]{:S(2)}, u32[]{:S(2)}) %collective-permute-start.2) | collective-permute-done | bytes 172064 | tf_op jit(solution)/shard_map/ppermute | solution.py:434
  29.7 1.5 %shard_map.88 = (f32[2,112,128]{2,1,0:T(8,128)S(1)}, f32[2,112,128]{2,1,0:T(8,128)S(1)}, f32[2,112,128]{2,1,0:T(8,128)S(1)}) custom-call(f32[3,112,128]{2,1,0:T(8,128)S(1)} %get-tuple-element.26.down, f32[3,112,128]{2,1,0:T(8,128)S(1)} %get-tuple-element.27.up, f32[3,112,128]{2,1,0:T(8,128)S(1)} %collective-permute-done.2.below, ...), custom_call_target="tpu_custom_call" | custom-call | bytes 1048576 | tf_op jit(solution)/shard_map/pallas_call | solution.py:370
  31.3 1.9 %collective-permute-start.5 = (f32[2,112,128]{2,1,0:T(8,128)S(1)}, f32[2,112,128]{2,1,0:T(8,128)S(1)}, u32[]{:S(2)}, u32[]{:S(2)}) collective-permute-start(f32[2,112,128]{2,1,0:T(8,128)S(1)} %get-tuple-element.32.down_two), channel_id=1, source_target_pairs={{1,0},{2,1},{3,2},{4,3},{5,4},{6,5},{7,6},{8,7},{9,8},{10,9},{11,1... | collective-permute-start | bytes 344072 | tf_op jit(solution)/shard_map/ppermute | solution.py:441
  33.2 3.4 %collective-permute-start.4 = (f32[2,112,128]{2,1,0:T(8,128)S(1)}, f32[2,112,128]{2,1,0:T(8,128)S(1)}, u32[]{:S(2)}, u32[]{:S(2)}) collective-permute-start(f32[2,112,128]{2,1,0:T(8,128)S(1)} %get-tuple-element.33.up_two), channel_id=1, source_target_pairs={{0,1},{1,2},{2,3},{3,4},{4,5},{5,6},{6,7},{7,8},{8,9},{9,10},{10,1... | collective-permute-start | bytes 344072 | tf_op jit(solution)/shard_map/ppermute | solution.py:440
  36.6 1.5 %collective-permute-done.5.above_two = f32[2,112,128]{2,1,0:T(8,128)S(1)} collective-permute-done((f32[2,112,128]{2,1,0:T(8,128)S(1)}, f32[2,112,128]{2,1,0:T(8,128)S(1)}, u32[]{:S(2)}, u32[]{:S(2)}) %collective-permute-start.5) | collective-permute-done | bytes 114720 | tf_op jit(solution)/shard_map/ppermute | solution.py:441
  38.1 5.2 %collective-permute-done.4.below_two = f32[2,112,128]{2,1,0:T(8,128)S(1)} collective-permute-done((f32[2,112,128]{2,1,0:T(8,128)S(1)}, f32[2,112,128]{2,1,0:T(8,128)S(1)}, u32[]{:S(2)}, u32[]{:S(2)}) %collective-permute-start.4) | collective-permute-done | bytes 114720 | tf_op jit(solution)/shard_map/ppermute | solution.py:440
  43.4 1.2 %shard_map.89 = (f32[2,112,128]{2,1,0:T(8,128)S(1)}, f32[2,112,128]{2,1,0:T(8,128)S(1)}, f32[1,128]{1,0:T(1,128)S(1)}) custom-call(f32[3,112,128]{2,1,0:T(8,128)S(1)} %get-tuple-element.26.down, f32[3,112,128]{2,1,0:T(8,128)S(1)} %get-tuple-element.27.up, f32[3,112,128]{2,1,0:T(8,128)S(1)} %collective-permute-done.2.below, ...), custom_call_target="tpu_custom_call" | custom-call | bytes 1048576 | tf_op jit(solution)/shard_map/pallas_call | solution.py:370
  44.6 11.6 %all_to_all.10 = f32[32,1,128]{2,1,0:T(1,128)S(1)} all-to-all(f32[32,1,128]{2,1,0:T(1,128)S(1)} %broadcast_in_dim.7), channel_id=1, replica_groups=mesh['tm'=16,'space'=32] {'space'}, dimensions={0} | all-to-all | bytes 32768 | tf_op jit(solution)/shard_map/all_to_all | solution.py:450
  56.3 19.2 %all_to_all.11 = f32[16,1,128]{2,1,0:T(1,128)S(1)} all-to-all(f32[16,1,128]{2,1,0:T(1,128)S(1)} %broadcast_in_dim.16), channel_id=1, replica_groups=mesh['tm'=16,'space'=32] {'tm'}, dimensions={0} | all-to-all | bytes 16384 | tf_op jit(solution)/shard_map/all_to_all | solution.py:450
  75.5 0.9 %shard_map.90 = (f32[96,256]{1,0:T(8,128)}, f32[96,256]{1,0:T(8,128)}) custom-call(f32[8,128]{1,0:T(8,128)S(1)} %get-tuple-element.20.flag, f32[1,128]{1,0:T(1,128)S(1)} %bitcast.6, f32[3,112,128]{2,1,0:T(8,128)S(1)} %get-tuple-element.26.down, f32[3,112,128]{2,1,0:T(8,128)S(1)} %get-tuple-element.27.up, f32[2,112,128]{2,1,0:T(8,128)S(1)} %get-tuple-element.31.one, ...), custom_call_target="tpu_custom_call" | custom-call | bytes 1048576 | tf_op jit(solution)/shard_map/pallas_call | solution.py:370
  (6 shorter events, 0.1 us)
Async XLA Ops:
  1.4 12.1 %collective-permute-start = (f32[16,256]{1,0:T(8,128)S(1)}, f32[16,256]{1,0:T(8,128)S(1)}, u32[]{:S(2)}, u32[]{:S(2)}) collective-permute-start(f32[16,256]{1,0:T(8,128)S(1)} %pad_maximum_fusion), channel_id=1, source_target_pairs={{0,32},{32,64},{64,96},{96,128},{128,160},{160,192},{192,224},{224... | collective-permute-start | bytes 49160 | tf_op jit(solution)/shard_map/ppermute | solution.py:399
  6.8 6.7 %collective-permute-start.1 = (f32[16,256]{1,0:T(8,128)S(1)}, f32[16,256]{1,0:T(8,128)S(1)}, u32[]{:S(2)}, u32[]{:S(2)}) collective-permute-start(f32[16,256]{1,0:T(8,128)S(1)} %pad_maximum_fusion.1), channel_id=1, source_target_pairs={{32,0},{64,32},{96,64},{128,96},{160,128},{192,160},{224,192},{256... | collective-permute-start | bytes 49160 | tf_op jit(solution)/shard_map/ppermute | solution.py:400
  14.0 8.3 %collective-permute-start.3 = (f32[3,112,128]{2,1,0:T(8,128)S(1)}, f32[3,112,128]{2,1,0:T(8,128)S(1)}, u32[]{:S(2)}, u32[]{:S(2)}) collective-permute-start(f32[3,112,128]{2,1,0:T(8,128)S(1)} %get-tuple-element.26.down), channel_id=1, source_target_pairs={{1,0},{2,1},{3,2},{4,3},{5,4},{6,5},{7,6},{8,7},{9,8},{10,9},{11,1... | collective-permute-start | bytes 516104 | tf_op jit(solution)/shard_map/ppermute | solution.py:435
  19.6 10.1 %collective-permute-start.2 = (f32[3,112,128]{2,1,0:T(8,128)S(1)}, f32[3,112,128]{2,1,0:T(8,128)S(1)}, u32[]{:S(2)}, u32[]{:S(2)}) collective-permute-start(f32[3,112,128]{2,1,0:T(8,128)S(1)} %get-tuple-element.27.up), channel_id=1, source_target_pairs={{0,1},{1,2},{2,3},{3,4},{4,5},{5,6},{6,7},{7,8},{8,9},{9,10},{10,1... | collective-permute-start | bytes 516104 | tf_op jit(solution)/shard_map/ppermute | solution.py:434
  31.3 6.8 %collective-permute-start.5 = (f32[2,112,128]{2,1,0:T(8,128)S(1)}, f32[2,112,128]{2,1,0:T(8,128)S(1)}, u32[]{:S(2)}, u32[]{:S(2)}) collective-permute-start(f32[2,112,128]{2,1,0:T(8,128)S(1)} %get-tuple-element.32.down_two), channel_id=1, source_target_pairs={{1,0},{2,1},{3,2},{4,3},{5,4},{6,5},{7,6},{8,7},{9,8},{10,9},{11,1... | collective-permute-start | bytes 344072 | tf_op jit(solution)/shard_map/ppermute | solution.py:441
  33.2 10.2 %collective-permute-start.4 = (f32[2,112,128]{2,1,0:T(8,128)S(1)}, f32[2,112,128]{2,1,0:T(8,128)S(1)}, u32[]{:S(2)}, u32[]{:S(2)}) collective-permute-start(f32[2,112,128]{2,1,0:T(8,128)S(1)} %get-tuple-element.33.up_two), channel_id=1, source_target_pairs={{0,1},{1,2},{2,3},{3,4},{4,5},{5,6},{6,7},{7,8},{8,9},{9,10},{10,1... | collective-permute-start | bytes 344072 | tf_op jit(solution)/shard_map/ppermute | solution.py:440

commit v4 on v3

--- a/solution.py
+++ b/solution.py
@@ -7,13 +7,14 @@
 
 ITERS = 4
 HALO = 2 * ITERS
+FRONT = 2 * HALO
 BLOCK = 128
 CENTRE = 1.0
 WIDTH = 0.6
 VMEM = pl.BlockSpec(memory_space=pltpu.VMEM)
 F32 = jnp.float32
 BF16 = jnp.bfloat16
-TERMS = ((0, 0), (1, 0), (1, -1), (2, 0), (2, -2))
+TERMS = ((0, 0, 0), (1, 1, -1), (-1, 1, 0), (2, 2, -2), (-2, 2, 0))
 
 
 def parts_of(array, count):
@@ -31,9 +32,7 @@
 
 def local_product(vectors, weights):
     first, second, third = parts_of(jnp.concatenate(vectors, axis=1), 3)
-    return dot(
-        jnp.concatenate([first, second, third, first, second], axis=1), weights[...]
-    )
+    return dot(jnp.concatenate([first, second, third, first], axis=1), weights[...])
 
 
 def cross_product(vector, block):
@@ -47,12 +46,13 @@
 
 
 def band_apply(bands, spatial):
+    first, second = spatial[:, :BLOCK], spatial[:, BLOCK:]
     result = None
-    for matrix in range(2):
-        rows = spatial[:, matrix * BLOCK : (matrix + 1) * BLOCK]
-        for index, offset in enumerate((0, 1, -1, 2, -2)):
-            term = bands[5 * matrix + index] * (moved(rows, offset) if offset else rows)
-            result = term if result is None else result + term
+    for index, (offset, _, _) in enumerate(TERMS):
+        term = bands[index] * first + bands[5 + index] * second
+        if offset:
+            term = moved(term, offset)
+        result = term if result is None else result + term
     return result
 
 
@@ -72,9 +72,9 @@
     for copy in copies[:5]:
         copy.wait()
     time_rows, time_total = right.shape[0], band_rows.shape[2]
-    extent = time_rows + 2 * HALO
-
-    first = lax.axis_index("tm") * time_rows - HALO - 2
+    extent = time_rows + FRONT
+
+    first = lax.axis_index("tm") * time_rows - FRONT - 2
     tile = (first + time_total) // BLOCK - time_total // BLOCK
     shift = first - tile * BLOCK
     last_tile = time_total // BLOCK - 1
@@ -95,8 +95,9 @@
     lines = []
     for matrix in range(2):
         rows = [window(band, matrix) for band in range(3)]
-        for band, offset in TERMS:
-            lines.append(pltpu.roll(rows[band], (-(2 + offset)) % BLOCK, 1))
+        for offset, band, shifted in TERMS:
+            line = pltpu.roll(rows[band], (-(2 + shifted)) % BLOCK, 1)
+            lines.append(jnp.where(lane >= offset, line, 0.0) if offset > 0 else line)
     valid = jnp.where(inside, 1.0, 0.0)
     lines.append(pltpu.roll(valid, BLOCK - 2, 1))
     count = len(lines)
@@ -150,7 +151,7 @@
                     named = codes[row][:, j : j + 1] == own[col]
                     total = total + jnp.where(named, 1.0, 0.0) * stored[row][j]
                 lead, rest = parts_of(total, 2)
-                for k, value in enumerate((lead, lead, lead, rest, rest)):
+                for k, value in enumerate((lead, lead, lead, rest)):
                     start = (2 * k + row) * BLOCK
                     local_ref[start : start + BLOCK, lanes] = value
         lanes = slice(matrix * BLOCK, (matrix + 1) * BLOCK)
@@ -166,22 +167,19 @@
 
 
 def prepare_kernel(
-    right, obs, before, after, bands, flag, diagonal, local,
+    right, obs, before, bands, flag, diagonal, local,
     precond_ref, obs_ref, down_ref, up_ref,
 ):
     swapped = flag[...] > 0.5
 
     def extended(middle, start):
-        ends = []
-        for ref in (before, after):
-            rows = ref[start : start + HALO]
-            one, two = rows[:, :BLOCK], rows[:, BLOCK:]
-            ends.append((jnp.where(swapped, two, one), jnp.where(swapped, one, two)))
-        return [
-            jnp.concatenate([ends[0][k], middle[k], ends[1][k]], axis=0) for k in range(2)
-        ]
-
-    rhs, precision = extended(right, 0), extended(obs, HALO)
+        rows = before[start : start + FRONT]
+        one, two = rows[:, :BLOCK], rows[:, BLOCK:]
+        turned = jnp.concatenate([swapped] * (FRONT // 8), axis=0)
+        ends = (jnp.where(turned, two, one), jnp.where(turned, one, two))
+        return [jnp.concatenate([ends[k], middle[k]], axis=0) for k in range(2)]
+
+    rhs, precision = extended(right, 0), extended(obs, FRONT)
     valid = bands[10]
     scaled, inverses = [], []
     for place in range(2):
@@ -245,7 +243,7 @@
 def second_kernel(
     down, up, below, above, one, down_two, up_two, below_two, above_two, precond, obs,
     bands, local, into, out,
-    three_ref, four_ref, sums_ref,
+    three_ref, four_ref, back_ref, sums_ref,
 ):
     own, sides = (down, up), (below, above)
     own_two, sides_two = (down_two, up_two), (below_two, above_two)
@@ -262,16 +260,21 @@
     olders = [ref[0] for ref in own_two]
     four = full_step(bands, local, into, vectors, nears, obs, inverses, olders)
     extent = bands.shape[1]
-    inside = slice(HALO, extent - HALO)
+    final = lax.axis_index("tm") == lax.axis_size("tm") - 1
+    counted = lax.broadcasted_iota(jnp.int32, (extent - HALO, BLOCK), 0) < extent - FRONT
+    counted = jnp.where(counted | final, 1.0, 0.0)
     sums = [0.0] * 14
     for place in range(2):
         three_ref[place] = vectors[place]
         four_ref[place] = four[place]
         basis = (own[place][0], one[place], olders[place], vectors[place], four[place])
-        basis = [rows[inside] for rows in basis]
+        for k in range(4):
+            back_ref[place, k] = basis[k + 1][HALO:FRONT]
+        basis = [rows[HALO:] for rows in basis]
+        weight = counted * precond[place][HALO:]
         index = 0
         for i in range(4):
-            weighted = precond[place][inside] * basis[i]
+            weighted = weight * basis[i]
             for j in range(i, 5):
                 term = (weighted * basis[j]).reshape(-1, 8, BLOCK)
                 sums[index] = sums[index] + jnp.sum(term, axis=0)
@@ -328,7 +331,7 @@
 
 
 def final_kernel(
-    flag, parts, down, up, one, down_two, up_two, three, four, precond,
+    flag, parts, down, up, one, down_two, up_two, three, four, precond, back,
     solution_ref, residual_ref,
 ):
     rows = jnp.sum(parts[...], axis=0, keepdims=True)
@@ -353,14 +356,26 @@
             direction = combined(state, norm_next / norm_now, direction)
             norm_now = norm_next
     swapped = flag[0:1] > 0.5
-    inside = slice(HALO, HALO + solution_ref.shape[0])
+    final = lax.axis_index("tm") == lax.axis_size("tm") - 1
     solutions, residuals = [], []
     for place, (ref, ref_two) in enumerate(((down, down_two), (up, up_two))):
         basis = (ref[0], one[place], ref_two[0], three[place], four[place])
-        basis = [rows[inside] for rows in basis]
+        extent = precond.shape[1]
+        start = basis[0][FRONT:]
+        basis = [
+            jnp.concatenate(
+                [
+                    rows[FRONT : extent - HALO],
+                    jnp.where(final, rows[extent - HALO :], back[place, k]),
+                ],
+                axis=0,
+            )
+            for k, rows in enumerate(basis[1:])
+        ]
+        basis.insert(0, start)
         solutions.append(added([answer[k] * basis[k] for k in range(4)]))
         left = added([state[k] * basis[k] for k in range(5)])
-        residuals.append(left * precond[place][inside])
+        residuals.append(left * precond[place][FRONT:])
     for ref, pair in ((solution_ref, solutions), (residual_ref, residuals)):
         ref[:, :BLOCK] = jnp.where(swapped, pair[1], pair[0])
         ref[:, BLOCK:] = jnp.where(swapped, pair[0], pair[1])
@@ -391,13 +406,11 @@
     right_side, obs_precision, mass_blocks, stiff_blocks, block_pattern, send_lists, time_bands
 ):
     time_rows = right_side.shape[0]
-    extent = time_rows + 2 * HALO
-
-    up, down = ring("tm", False)
-    last = jnp.concatenate([right_side[-HALO:], obs_precision[-HALO:]], axis=0)
-    first = jnp.concatenate([right_side[:HALO], obs_precision[:HALO]], axis=0)
-    before = lax.ppermute(last, "tm", up)
-    after = lax.ppermute(first, "tm", down)
+    extent = time_rows + FRONT
+
+    later, earlier = ring("tm", False)
+    last = jnp.concatenate([right_side[-FRONT:], obs_precision[-FRONT:]], axis=0)
+    before = lax.ppermute(last, "tm", later)
 
     wide = 2 * BLOCK
     stored = (
@@ -411,7 +424,7 @@
             (11, extent, BLOCK),
             (8, BLOCK),
             (8, BLOCK),
-            jax.ShapeDtypeStruct((5 * wide, 2 * wide), BF16),
+            jax.ShapeDtypeStruct((4 * wide, 2 * wide), BF16),
             jax.ShapeDtypeStruct((2, BLOCK, wide), BF16),
             jax.ShapeDtypeStruct((2, BLOCK, wide), BF16),
             half,
@@ -428,7 +441,7 @@
     triple = (3, extent, BLOCK)
     precond, precision, to_down, to_up = call(
         prepare_kernel, [pair, pair, triple, triple],
-        right, obs, before, after, bands, flag, diagonal, local,
+        right, obs, before, bands, flag, diagonal, local,
     )
     up, down = ring("space", True)
     below = lax.ppermute(to_up, "space", up)
@@ -439,11 +452,12 @@
     )
     below_two = lax.ppermute(up_two, "space", up)
     above_two = lax.ppermute(down_two, "space", down)
-    three, four, sums = call(
-        second_kernel, [pair, pair, (1, BLOCK)],
+    three, four, back, sums = call(
+        second_kernel, [pair, pair, (2, 4, HALO, BLOCK), (1, BLOCK)],
         to_down, to_up, below, above, one, down_two, up_two, below_two, above_two,
         precond, precision, bands, local, into, out,
     )
+    back = lax.ppermute(back, "tm", earlier)
     for axis in ("space", "tm"):
         devices = lax.axis_size(axis)
         sent = jnp.broadcast_to(sums[None], (devices, 1, BLOCK))
@@ -452,7 +466,7 @@
     return tuple(
         call(
             final_kernel, [right_side.shape, right_side.shape],
-            flag, sums, to_down, to_up, one, down_two, up_two, three, four, precond,
+            flag, sums, to_down, to_up, one, down_two, up_two, three, four, precond, back,
         )
     )
 

time: 76.8 us -> 75.1 us (0.978)
  blocking collectives: 30.8 us -> 20 us
  waiting for transfers between devices: 15 us -> 22.1 us
  starting transfers between devices: 22.9 us -> 24.5 us
    all_to_all x2 -> x1, blocking collectives: 30.8 us -> 20 us  [shards(): gathered = lax.all_to_all(sent, axis, 0, 0)]
    all_to_all x0 -> x1, waiting for transfers between devices: none -> 6.28 us  [shards(): gathered = lax.all_to_all(sent, axis, 0, 0)]
    all_to_all x0 -> x1, starting transfers between devices: none -> 3.83 us  [shards(): gathered = lax.all_to_all(sent, axis, 0, 0)]
    ppermute x2, starting transfers between devices: 10.1 us -> 7.65 us  [the longest x1 5.38 us: shards(): before = lax.ppermute(last, 'tm', later)]
    ppermute x2, waiting for transfers between devices: 0.01 us -> 1.48 us  [the longest x1 1.48 us: shards(): before = lax.ppermute(last, 'tm', later)]
  transfers between devices with their start and end apart: 6 -> 7, of which waited for: 4 -> 6; matrix products, arithmetic and copies ran while one was open for 0% -> 0% of each run, Pallas kernels for 3% -> 3%
where the time goes in v4:
time: 75.1 us; the launch traced here: 74.5 us
  starting transfers between devices  24.5 us (33%)
  waiting for transfers between devices  22.1 us (29%)
  blocking collectives  20 us (27%)
  Pallas kernels  5.7 us (8%)
  local copies, waits for them, and re-layouts  1.35 us (2%)
    all_to_all x1, blocking collectives, shards(): gathered = lax.all_to_all(sent, axis, 0, 0)  20 us
    ppermute x1, waiting for transfers between devices, shards(): below = lax.ppermute(to_up, 'space', up)  7.42 us
    all_to_all x1, waiting for transfers between devices, shards(): gathered = lax.all_to_all(sent, axis, 0, 0)  6.28 us
    ppermute x1, starting transfers between devices, shards(): above = lax.ppermute(to_down, 'space', down)  5.83 us
    pallas_call x5, Pallas kernels, call(): pl.pallas_call(kernel, out_shape=[shape if isinstance(shape, jax.ShapeDty...  5.7 us
    ppermute x1, starting transfers between devices, shards(): before = lax.ppermute(last, 'tm', later)  5.38 us
    ppermute x1, waiting for transfers between devices, shards(): below_two = lax.ppermute(up_two, 'space', up)  5.25 us
    all_to_all x1, starting transfers between devices, shards(): gathered = lax.all_to_all(sent, axis, 0, 0)  3.83 us
  transfers between devices with their start and end apart: 7, of which 6 were waited for; matrix products, arithmetic and copies ran while one was open for 0% of the time, Pallas kernels for 3%

profile of v4, /device:TPU:1, one launch (start us, length us, event | category | flops | bytes accessed | tf_op | source)
XLA Modules:
  0.0 74.5 jit_solution(4552233059029004369)
XLA Ops:
  0.6 0.0 slice-start
  0.6 0.0 slice-start.1
  0.7 0.7 slice-done
  1.4 0.0 slice-done.1
  1.4 5.4 %collective-permute-start = (f32[32,256]{1,0:T(8,128)S(1)}, f32[32,256]{1,0:T(8,128)S(1)}, u32[]{:S(2)}, u32[]{:S(2)}) collective-permute-start(f32[32,256]{1,0:T(8,128)S(1)} %pad_maximum_fusion), channel_id=1, source_target_pairs={{0,32},{32,64},{64,96},{96,128},{128,160},{160,192},{192,224},{224... | collective-permute-start | bytes 98312 | tf_op jit(solution)/shard_map/ppermute | solution.py:413
  6.8 2.0 %shard_map.86 = (f32[11,112,128]{2,1,0:T(8,128)S(1)}, f32[8,128]{1,0:T(8,128)S(1)}, f32[8,128]{1,0:T(8,128)S(1)}, bf16[1024,512]{1,0:T(8,128)(2,1)S(1)}, bf16[2,...) custom-call(s32[2,1,32]{2,1,0:T(1,128)} %bitcast.11, ...), custom_call_target="tpu_custom_call" | custom-call | flops 2097152 | bytes 1048576 | tf_op jit(solution)/shard_map/pallas_call | solution.py:385
  8.7 1.5 %collective-permute-done.before = f32[32,256]{1,0:T(8,128)S(1)} collective-permute-done((f32[32,256]{1,0:T(8,128)S(1)}, f32[32,256]{1,0:T(8,128)S(1)}, u32[]{:S(2)}, u32[]{:S(2)}) %collective-permute-start) | collective-permute-done | bytes 32800 | tf_op jit(solution)/shard_map/ppermute | solution.py:413
  10.2 0.4 shard_map.87
  10.6 5.8 %collective-permute-start.2 = (f32[3,112,128]{2,1,0:T(8,128)S(1)}, f32[3,112,128]{2,1,0:T(8,128)S(1)}, u32[]{:S(2)}, u32[]{:S(2)}) collective-permute-start(f32[3,112,128]{2,1,0:T(8,128)S(1)} %get-tuple-element.27.down), channel_id=1, source_target_pairs={{1,0},{2,1},{3,2},{4,3},{5,4},{6,5},{7,6},{8,7},{9,8},{10,9},{11,1... | collective-permute-start | bytes 516104 | tf_op jit(solution)/shard_map/ppermute | solution.py:448
  16.5 1.9 %collective-permute-start.1 = (f32[3,112,128]{2,1,0:T(8,128)S(1)}, f32[3,112,128]{2,1,0:T(8,128)S(1)}, u32[]{:S(2)}, u32[]{:S(2)}) collective-permute-start(f32[3,112,128]{2,1,0:T(8,128)S(1)} %get-tuple-element.28.up), channel_id=1, source_target_pairs={{0,1},{1,2},{2,3},{3,4},{4,5},{5,6},{6,7},{7,8},{8,9},{9,10},{10,1... | collective-permute-start | bytes 516104 | tf_op jit(solution)/shard_map/ppermute | solution.py:447
  18.4 0.6 collective-permute-done.2.above
  19.0 7.4 %collective-permute-done.1.below = f32[3,112,128]{2,1,0:T(8,128)S(1)} collective-permute-done((f32[3,112,128]{2,1,0:T(8,128)S(1)}, f32[3,112,128]{2,1,0:T(8,128)S(1)}, u32[]{:S(2)}, u32[]{:S(2)}) %collective-permute-start.1) | collective-permute-done | bytes 172064 | tf_op jit(solution)/shard_map/ppermute | solution.py:447
  26.4 1.3 %shard_map.88 = (f32[2,112,128]{2,1,0:T(8,128)S(1)}, f32[2,112,128]{2,1,0:T(8,128)S(1)}, f32[2,112,128]{2,1,0:T(8,128)S(1)}) custom-call(f32[3,112,128]{2,1,0:T(8,128)S(1)} %get-tuple-element.27.down, f32[3,112,128]{2,1,0:T(8,128)S(1)} %get-tuple-element.28.up, f32[3,112,128]{2,1,0:T(8,128)S(1)} %collective-permute-done.1.below, ...), custom_call_target="tpu_custom_call" | custom-call | bytes 1048576 | tf_op jit(solution)/shard_map/pallas_call | solution.py:385
  27.7 1.9 %collective-permute-start.4 = (f32[2,112,128]{2,1,0:T(8,128)S(1)}, f32[2,112,128]{2,1,0:T(8,128)S(1)}, u32[]{:S(2)}, u32[]{:S(2)}) collective-permute-start(f32[2,112,128]{2,1,0:T(8,128)S(1)} %get-tuple-element.33.down_two), channel_id=1, source_target_pairs={{1,0},{2,1},{3,2},{4,3},{5,4},{6,5},{7,6},{8,7},{9,8},{10,9},{11,1... | collective-permute-start | bytes 344072 | tf_op jit(solution)/shard_map/ppermute | solution.py:454
  29.6 3.4 %collective-permute-start.3 = (f32[2,112,128]{2,1,0:T(8,128)S(1)}, f32[2,112,128]{2,1,0:T(8,128)S(1)}, u32[]{:S(2)}, u32[]{:S(2)}) collective-permute-start(f32[2,112,128]{2,1,0:T(8,128)S(1)} %get-tuple-element.34.up_two), channel_id=1, source_target_pairs={{0,1},{1,2},{2,3},{3,4},{4,5},{5,6},{6,7},{7,8},{8,9},{9,10},{10,1... | collective-permute-start | bytes 344072 | tf_op jit(solution)/shard_map/ppermute | solution.py:453
  33.0 1.2 %collective-permute-done.4.above_two = f32[2,112,128]{2,1,0:T(8,128)S(1)} collective-permute-done((f32[2,112,128]{2,1,0:T(8,128)S(1)}, f32[2,112,128]{2,1,0:T(8,128)S(1)}, u32[]{:S(2)}, u32[]{:S(2)}) %collective-permute-start.4) | collective-permute-done | bytes 114720 | tf_op jit(solution)/shard_map/ppermute | solution.py:454
  34.2 5.2 %collective-permute-done.3.below_two = f32[2,112,128]{2,1,0:T(8,128)S(1)} collective-permute-done((f32[2,112,128]{2,1,0:T(8,128)S(1)}, f32[2,112,128]{2,1,0:T(8,128)S(1)}, u32[]{:S(2)}, u32[]{:S(2)}) %collective-permute-start.3) | collective-permute-done | bytes 114720 | tf_op jit(solution)/shard_map/ppermute | solution.py:453
  39.4 1.1 %shard_map.89 = (f32[2,112,128]{2,1,0:T(8,128)S(1)}, f32[2,112,128]{2,1,0:T(8,128)S(1)}, f32[2,4,8,128]{3,2,1,0:T(8,128)S(1)}, f32[1,128]{1,0:T(1,128)S(1)}) custom-call(f32[3,112,128]{2,1,0:T(8,128)S(1)} %get-tuple-element.27.down, f32[3,112,128]{2,1,0:T(8,128)S(1)} %get-tuple-element.28.up, f32[3,112,128]{2,1,0:T(8,128)S(1)} %collective-permute-done.1.below, ...), custom_call_target="tpu_custom_call" | custom-call | bytes 1048576 | tf_op jit(solution)/shard_map/pallas_call | solution.py:385
  40.5 0.6 broadcast_in_dim.7
  41.1 3.8 %all-to-all-start = ((f32[32,1,128]{2,1,0:T(1,128)}), f32[32,1,128]{2,1,0:T(1,128)S(1)}, u32[]{:S(2)}, u32[]{:S(2)}) async-start(f32[32,1,128]{2,1,0:T(1,128)} %broadcast_in_dim.7), calls=%async_computation | async-start | bytes 32768 | tf_op jit(solution)/shard_map/all_to_all | solution.py:464
  44.9 2.3 %collective-permute-start.5 = (f32[2,4,8,128]{3,2,1,0:T(8,128)S(1)}, f32[2,4,8,128]{3,2,1,0:T(8,128)S(1)}, u32[]{:S(2)}, u32[]{:S(2)}) collective-permute-start(f32[2,4,8,128]{3,2,1,0:T(8,128)S(1)} %get-tuple-element.39), channel_id=1, source_target_pairs={{32,0},{64,32},{96,64},{128,96},{160,128},{192,160},{224,192},{256... | collective-permute-start | bytes 98312 | tf_op jit(solution)/shard_map/ppermute | solution.py:460
  47.2 6.3 %all-to-all-done = f32[32,1,128]{2,1,0:T(1,128)S(1)} async-done(((f32[32,1,128]{2,1,0:T(1,128)}), f32[32,1,128]{2,1,0:T(1,128)S(1)}, u32[]{:S(2)}, u32[]{:S(2)}) %all-to-all-start) | async-done | bytes 16416 | tf_op jit(solution)/shard_map/all_to_all | solution.py:464
  53.5 20.0 %all_to_all.10 = f32[16,1,128]{2,1,0:T(1,128)S(1)} all-to-all(f32[16,1,128]{2,1,0:T(1,128)S(1)} %broadcast_in_dim.16), channel_id=1, replica_groups=mesh['tm'=16,'space'=32] {'tm'}, dimensions={0} | all-to-all | bytes 16384 | tf_op jit(solution)/shard_map/all_to_all | solution.py:464
  73.6 0.0 collective-permute-done.5.back
  73.6 0.9 %shard_map.90 = (f32[96,256]{1,0:T(8,128)}, f32[96,256]{1,0:T(8,128)}) custom-call(f32[8,128]{1,0:T(8,128)S(1)} %get-tuple-element.21.flag, f32[1,128]{1,0:T(1,128)S(1)} %bitcast.6, f32[3,112,128]{2,1,0:T(8,128)S(1)} %get-tuple-element.27.down, f32[3,112,128]{2,1,0:T(8,128)S(1)} %get-tuple-element.28.up, f32[2,112,128]{2,1,0:T(8,128)S(1)} %get-tuple-element.32.one, ...), custom_call_target="tpu_custom_call" | custom-call | bytes 1048576 | tf_op jit(solution)/shard_map/pallas_call | solution.py:385
  (4 shorter events, 0.0 us)
Async XLA Ops:
  0.6 0.7 slice-start
  0.6 0.7 slice-start.1
  1.4 8.8 %collective-permute-start = (f32[32,256]{1,0:T(8,128)S(1)}, f32[32,256]{1,0:T(8,128)S(1)}, u32[]{:S(2)}, u32[]{:S(2)}) collective-permute-start(f32[32,256]{1,0:T(8,128)S(1)} %pad_maximum_fusion), channel_id=1, source_target_pairs={{0,32},{32,64},{64,96},{96,128},{128,160},{160,192},{192,224},{224... | collective-permute-start | bytes 98312 | tf_op jit(solution)/shard_map/ppermute | solution.py:413
  10.6 8.3 %collective-permute-start.2 = (f32[3,112,128]{2,1,0:T(8,128)S(1)}, f32[3,112,128]{2,1,0:T(8,128)S(1)}, u32[]{:S(2)}, u32[]{:S(2)}) collective-permute-start(f32[3,112,128]{2,1,0:T(8,128)S(1)} %get-tuple-element.27.down), channel_id=1, source_target_pairs={{1,0},{2,1},{3,2},{4,3},{5,4},{6,5},{7,6},{8,7},{9,8},{10,9},{11,1... | collective-permute-start | bytes 516104 | tf_op jit(solution)/shard_map/ppermute | solution.py:448
  16.5 9.9 %collective-permute-start.1 = (f32[3,112,128]{2,1,0:T(8,128)S(1)}, f32[3,112,128]{2,1,0:T(8,128)S(1)}, u32[]{:S(2)}, u32[]{:S(2)}) collective-permute-start(f32[3,112,128]{2,1,0:T(8,128)S(1)} %get-tuple-element.28.up), channel_id=1, source_target_pairs={{0,1},{1,2},{2,3},{3,4},{4,5},{5,6},{6,7},{7,8},{8,9},{9,10},{10,1... | collective-permute-start | bytes 516104 | tf_op jit(solution)/shard_map/ppermute | solution.py:447
  27.7 6.5 %collective-permute-start.4 = (f32[2,112,128]{2,1,0:T(8,128)S(1)}, f32[2,112,128]{2,1,0:T(8,128)S(1)}, u32[]{:S(2)}, u32[]{:S(2)}) collective-permute-start(f32[2,112,128]{2,1,0:T(8,128)S(1)} %get-tuple-element.33.down_two), channel_id=1, source_target_pairs={{1,0},{2,1},{3,2},{4,3},{5,4},{6,5},{7,6},{8,7},{9,8},{10,9},{11,1... | collective-permute-start | bytes 344072 | tf_op jit(solution)/shard_map/ppermute | solution.py:454
  29.6 9.8 %collective-permute-start.3 = (f32[2,112,128]{2,1,0:T(8,128)S(1)}, f32[2,112,128]{2,1,0:T(8,128)S(1)}, u32[]{:S(2)}, u32[]{:S(2)}) collective-permute-start(f32[2,112,128]{2,1,0:T(8,128)S(1)} %get-tuple-element.34.up_two), channel_id=1, source_target_pairs={{0,1},{1,2},{2,3},{3,4},{4,5},{5,6},{6,7},{7,8},{8,9},{9,10},{10,1... | collective-permute-start | bytes 344072 | tf_op jit(solution)/shard_map/ppermute | solution.py:453
  41.1 12.4 %all-to-all-start = ((f32[32,1,128]{2,1,0:T(1,128)}), f32[32,1,128]{2,1,0:T(1,128)S(1)}, u32[]{:S(2)}, u32[]{:S(2)}) async-start(f32[32,1,128]{2,1,0:T(1,128)} %broadcast_in_dim.7), calls=%async_computation | async-start | bytes 32768 | tf_op jit(solution)/shard_map/all_to_all | solution.py:464
  44.9 28.6 %collective-permute-start.5 = (f32[2,4,8,128]{3,2,1,0:T(8,128)S(1)}, f32[2,4,8,128]{3,2,1,0:T(8,128)S(1)}, u32[]{:S(2)}, u32[]{:S(2)}) collective-permute-start(f32[2,4,8,128]{3,2,1,0:T(8,128)S(1)} %get-tuple-element.39), channel_id=1, source_target_pairs={{32,0},{64,32},{96,64},{128,96},{160,128},{192,160},{224,192},{256... | collective-permute-start | bytes 98312 | tf_op jit(solution)/shard_map/ppermute | solution.py:460

commit v5 on v4

--- a/solution.py
+++ b/solution.py
@@ -30,15 +30,22 @@
     return jnp.dot(left, right, preferred_element_type=F32)
 
 
+def stacked_product(parts, block):
+    rows = parts[0].shape[0]
+    product = dot(jnp.concatenate(parts, axis=0), block)
+    result = product[:rows]
+    for k in range(1, len(parts)):
+        result = result + product[k * rows : (k + 1) * rows]
+    return result
+
+
 def local_product(vectors, weights):
-    first, second, third = parts_of(jnp.concatenate(vectors, axis=1), 3)
-    return dot(jnp.concatenate([first, second, third, first], axis=1), weights[...])
+    parts = parts_of(jnp.concatenate(vectors, axis=1), 3)
+    return stacked_product(parts, weights[0]) + dot(parts[0], weights[1])
 
 
 def cross_product(vector, block):
-    return dot(
-        jnp.concatenate(parts_of(vector, 3), axis=1), jnp.concatenate([block] * 3, axis=0)
-    )
+    return stacked_product(parts_of(vector, 3), block)
 
 
 def moved(rows, offset):
@@ -151,9 +158,8 @@
                     named = codes[row][:, j : j + 1] == own[col]
                     total = total + jnp.where(named, 1.0, 0.0) * stored[row][j]
                 lead, rest = parts_of(total, 2)
-                for k, value in enumerate((lead, lead, lead, rest)):
-                    start = (2 * k + row) * BLOCK
-                    local_ref[start : start + BLOCK, lanes] = value
+                for k, value in enumerate((lead, rest)):
+                    local_ref[k, row * BLOCK : (row + 1) * BLOCK, lanes] = value
         lanes = slice(matrix * BLOCK, (matrix + 1) * BLOCK)
         for place in range(2):
             out_ref[place, :, lanes] = stored[place][1].astype(BF16)
@@ -285,7 +291,8 @@
     slots = lax.broadcasted_iota(jnp.int32, (16, BLOCK), 0) == lax.broadcasted_iota(
         jnp.int32, (16, BLOCK), 1
     )
-    sums_ref[...] = jnp.sum(jnp.where(slots, totals, 0.0), axis=0, keepdims=True)
+    line = jnp.sum(jnp.where(slots, totals, 0.0), axis=0, keepdims=True)
+    sums_ref[...] = jnp.broadcast_to(line[None], sums_ref.shape)
 
 
 def added(terms):
@@ -424,7 +431,7 @@
             (11, extent, BLOCK),
             (8, BLOCK),
             (8, BLOCK),
-            jax.ShapeDtypeStruct((4 * wide, 2 * wide), BF16),
+            jax.ShapeDtypeStruct((2, wide, 2 * wide), BF16),
             jax.ShapeDtypeStruct((2, BLOCK, wide), BF16),
             jax.ShapeDtypeStruct((2, BLOCK, wide), BF16),
             half,
@@ -453,16 +460,16 @@
     below_two = lax.ppermute(up_two, "space", up)
     above_two = lax.ppermute(down_two, "space", down)
     three, four, back, sums = call(
-        second_kernel, [pair, pair, (2, 4, HALO, BLOCK), (1, BLOCK)],
+        second_kernel, [pair, pair, (2, 4, HALO, BLOCK), (lax.axis_size("tm"), 1, BLOCK)],
         to_down, to_up, below, above, one, down_two, up_two, below_two, above_two,
         precond, precision, bands, local, into, out,
     )
     back = lax.ppermute(back, "tm", earlier)
-    for axis in ("space", "tm"):
-        devices = lax.axis_size(axis)
-        sent = jnp.broadcast_to(sums[None], (devices, 1, BLOCK))
-        gathered = lax.all_to_all(sent, axis, 0, 0)
-        sums = jnp.sum(gathered, axis=0)
+    gathered = lax.all_to_all(sums, "tm", 0, 0)
+    sums = jnp.sum(gathered, axis=0)
+    sent = jnp.broadcast_to(sums[None], (lax.axis_size("space"), 1, BLOCK))
+    gathered = lax.all_to_all(sent, "space", 0, 0)
+    sums = jnp.sum(gathered, axis=0)
     return tuple(
         call(
             final_kernel, [right_side.shape, right_side.shape],

time: 75.1 us -> 73.1 us (0.973)
  blocking collectives: 20 us -> 11.6 us
  starting transfers between devices: 24.5 us -> 32.5 us
  waiting for transfers between devices: 22.1 us -> 20.8 us
    all_to_all x1, blocking collectives: 20 us -> 11.6 us  [shards(): gathered = lax.all_to_all(sent, 'space', 0, 0)]
    all_to_all x1, starting transfers between devices: 3.83 us -> 12.1 us  [shards(): gathered = lax.all_to_all(sums, 'tm', 0, 0)]
    all_to_all x1, waiting for transfers between devices: 6.28 us -> 4.93 us  [shards(): gathered = lax.all_to_all(sums, 'tm', 0, 0)]
where the time goes in v5:
time: 73.1 us; the launch traced here: 72.5 us
  starting transfers between devices  32.5 us (44%)
  waiting for transfers between devices  20.8 us (28%)
  blocking collectives  11.6 us (16%)
  Pallas kernels  6.06 us (8%)
  local copies, waits for them, and re-layouts  0.74 us (1%)
    all_to_all x1, starting transfers between devices, shards(): gathered = lax.all_to_all(sums, 'tm', 0, 0)  12.1 us
    all_to_all x1, blocking collectives, shards(): gathered = lax.all_to_all(sent, 'space', 0, 0)  11.6 us
    ppermute x1, waiting for transfers between devices, shards(): below = lax.ppermute(to_up, 'space', up)  7.42 us
    pallas_call x5, Pallas kernels, call(): pl.pallas_call(kernel, out_shape=[shape if isinstance(shape, jax.ShapeDty...  6.06 us
    ppermute x1, starting transfers between devices, shards(): above = lax.ppermute(to_down, 'space', down)  5.77 us
    ppermute x1, starting transfers between devices, shards(): before = lax.ppermute(last, 'tm', later)  5.38 us
    ppermute x1, waiting for transfers between devices, shards(): below_two = lax.ppermute(up_two, 'space', up)  5.25 us
    all_to_all x1, waiting for transfers between devices, shards(): gathered = lax.all_to_all(sums, 'tm', 0, 0)  4.93 us
  transfers between devices with their start and end apart: 7, of which 6 were waited for; matrix products, arithmetic and copies ran while one was open for 0% of the time, Pallas kernels for 3%

profile of v5, /device:TPU:1, one launch (start us, length us, event | category | flops | bytes accessed | tf_op | source)
XLA Modules:
  0.0 72.5 jit_solution(17328138483557191588)
XLA Ops:
  0.6 0.0 slice-start
  0.6 0.0 slice-start.1
  0.7 0.7 slice-done
  1.4 0.0 slice-done.1
  1.4 5.4 %collective-permute-start = (f32[32,256]{1,0:T(8,128)S(1)}, f32[32,256]{1,0:T(8,128)S(1)}, u32[]{:S(2)}, u32[]{:S(2)}) collective-permute-start(f32[32,256]{1,0:T(8,128)S(1)} %pad_maximum_fusion), channel_id=1, source_target_pairs={{0,32},{32,64},{64,96},{96,128},{128,160},{160,192},{192,224},{224... | collective-permute-start | bytes 98312 | tf_op jit(solution)/shard_map/ppermute | solution.py:420
  6.8 1.9 %shard_map.86 = (f32[11,112,128]{2,1,0:T(8,128)S(1)}, f32[8,128]{1,0:T(8,128)S(1)}, f32[8,128]{1,0:T(8,128)S(1)}, bf16[2,256,512]{2,1,0:T(8,128)(2,1)S(1)}, bf16...) custom-call(s32[2,1,32]{2,1,0:T(1,128)} %bitcast.7, ...), custom_call_target="tpu_custom_call" | custom-call | flops 2097152 | bytes 1048576 | tf_op jit(solution)/shard_map/pallas_call | solution.py:392
  8.7 1.5 %collective-permute-done.before = f32[32,256]{1,0:T(8,128)S(1)} collective-permute-done((f32[32,256]{1,0:T(8,128)S(1)}, f32[32,256]{1,0:T(8,128)S(1)}, u32[]{:S(2)}, u32[]{:S(2)}) %collective-permute-start) | collective-permute-done | bytes 32800 | tf_op jit(solution)/shard_map/ppermute | solution.py:420
  10.2 0.4 shard_map.87
  10.6 5.8 %collective-permute-start.2 = (f32[3,112,128]{2,1,0:T(8,128)S(1)}, f32[3,112,128]{2,1,0:T(8,128)S(1)}, u32[]{:S(2)}, u32[]{:S(2)}) collective-permute-start(f32[3,112,128]{2,1,0:T(8,128)S(1)} %get-tuple-element.27.down), channel_id=1, source_target_pairs={{1,0},{2,1},{3,2},{4,3},{5,4},{6,5},{7,6},{8,7},{9,8},{10,9},{11,1... | collective-permute-start | bytes 516104 | tf_op jit(solution)/shard_map/ppermute | solution.py:455
  16.4 1.9 %collective-permute-start.1 = (f32[3,112,128]{2,1,0:T(8,128)S(1)}, f32[3,112,128]{2,1,0:T(8,128)S(1)}, u32[]{:S(2)}, u32[]{:S(2)}) collective-permute-start(f32[3,112,128]{2,1,0:T(8,128)S(1)} %get-tuple-element.28.up), channel_id=1, source_target_pairs={{0,1},{1,2},{2,3},{3,4},{4,5},{5,6},{6,7},{7,8},{8,9},{9,10},{10,1... | collective-permute-start | bytes 516104 | tf_op jit(solution)/shard_map/ppermute | solution.py:454
  18.3 0.6 collective-permute-done.2.above
  18.9 7.4 %collective-permute-done.1.below = f32[3,112,128]{2,1,0:T(8,128)S(1)} collective-permute-done((f32[3,112,128]{2,1,0:T(8,128)S(1)}, f32[3,112,128]{2,1,0:T(8,128)S(1)}, u32[]{:S(2)}, u32[]{:S(2)}) %collective-permute-start.1) | collective-permute-done | bytes 172064 | tf_op jit(solution)/shard_map/ppermute | solution.py:454
  26.3 1.2 %shard_map.88 = (f32[2,112,128]{2,1,0:T(8,128)S(1)}, f32[2,112,128]{2,1,0:T(8,128)S(1)}, f32[2,112,128]{2,1,0:T(8,128)S(1)}) custom-call(f32[3,112,128]{2,1,0:T(8,128)S(1)} %get-tuple-element.27.down, f32[3,112,128]{2,1,0:T(8,128)S(1)} %get-tuple-element.28.up, f32[3,112,128]{2,1,0:T(8,128)S(1)} %collective-permute-done.1.below, ...), custom_call_target="tpu_custom_call" | custom-call | bytes 1048576 | tf_op jit(solution)/shard_map/pallas_call | solution.py:392
  27.5 1.9 %collective-permute-start.4 = (f32[2,112,128]{2,1,0:T(8,128)S(1)}, f32[2,112,128]{2,1,0:T(8,128)S(1)}, u32[]{:S(2)}, u32[]{:S(2)}) collective-permute-start(f32[2,112,128]{2,1,0:T(8,128)S(1)} %get-tuple-element.33.down_two), channel_id=1, source_target_pairs={{1,0},{2,1},{3,2},{4,3},{5,4},{6,5},{7,6},{8,7},{9,8},{10,9},{11,1... | collective-permute-start | bytes 344072 | tf_op jit(solution)/shard_map/ppermute | solution.py:461
  29.5 3.4 %collective-permute-start.3 = (f32[2,112,128]{2,1,0:T(8,128)S(1)}, f32[2,112,128]{2,1,0:T(8,128)S(1)}, u32[]{:S(2)}, u32[]{:S(2)}) collective-permute-start(f32[2,112,128]{2,1,0:T(8,128)S(1)} %get-tuple-element.34.up_two), channel_id=1, source_target_pairs={{0,1},{1,2},{2,3},{3,4},{4,5},{5,6},{6,7},{7,8},{8,9},{9,10},{10,1... | collective-permute-start | bytes 344072 | tf_op jit(solution)/shard_map/ppermute | solution.py:460
  32.8 1.2 %collective-permute-done.4.above_two = f32[2,112,128]{2,1,0:T(8,128)S(1)} collective-permute-done((f32[2,112,128]{2,1,0:T(8,128)S(1)}, f32[2,112,128]{2,1,0:T(8,128)S(1)}, u32[]{:S(2)}, u32[]{:S(2)}) %collective-permute-start.4) | collective-permute-done | bytes 114720 | tf_op jit(solution)/shard_map/ppermute | solution.py:461
  34.0 5.2 %collective-permute-done.3.below_two = f32[2,112,128]{2,1,0:T(8,128)S(1)} collective-permute-done((f32[2,112,128]{2,1,0:T(8,128)S(1)}, f32[2,112,128]{2,1,0:T(8,128)S(1)}, u32[]{:S(2)}, u32[]{:S(2)}) %collective-permute-start.3) | collective-permute-done | bytes 114720 | tf_op jit(solution)/shard_map/ppermute | solution.py:460
  39.2 1.6 %shard_map.89 = (f32[2,112,128]{2,1,0:T(8,128)S(1)}, f32[2,112,128]{2,1,0:T(8,128)S(1)}, f32[2,4,8,128]{3,2,1,0:T(8,128)S(1)}, f32[16,1,128]{2,1,0:T(1,128)}) custom-call(f32[3,112,128]{2,1,0:T(8,128)S(1)} %get-tuple-element.27.down, f32[3,112,128]{2,1,0:T(8,128)S(1)} %get-tuple-element.28.up, f32[3,112,128]{2,1,0:T(8,128)S(1)} %collective-permute-done.1.below, ...), custom_call_target="tpu_custom_call" | custom-call | bytes 1048576 | tf_op jit(solution)/shard_map/pallas_call | solution.py:392
  40.8 12.1 %all-to-all-start = ((f32[16,1,128]{2,1,0:T(1,128)}), f32[16,1,128]{2,1,0:T(1,128)S(1)}, u32[]{:S(2)}, u32[]{:S(2)}) async-start(f32[16,1,128]{2,1,0:T(1,128)} %get-tuple-element.36), calls=%async_computation | async-start | bytes 16384 | tf_op jit(solution)/shard_map/all_to_all | solution.py:468
  53.0 2.0 %collective-permute-start.5 = (f32[2,4,8,128]{3,2,1,0:T(8,128)S(1)}, f32[2,4,8,128]{3,2,1,0:T(8,128)S(1)}, u32[]{:S(2)}, u32[]{:S(2)}) collective-permute-start(f32[2,4,8,128]{3,2,1,0:T(8,128)S(1)} %get-tuple-element.39), channel_id=1, source_target_pairs={{32,0},{64,32},{96,64},{128,96},{160,128},{192,160},{224,192},{256... | collective-permute-start | bytes 98312 | tf_op jit(solution)/shard_map/ppermute | solution.py:467
  55.0 4.9 %all-to-all-done = f32[16,1,128]{2,1,0:T(1,128)S(1)} async-done(((f32[16,1,128]{2,1,0:T(1,128)}), f32[16,1,128]{2,1,0:T(1,128)S(1)}, u32[]{:S(2)}, u32[]{:S(2)}) %all-to-all-start) | async-done | bytes 8224 | tf_op jit(solution)/shard_map/all_to_all | solution.py:468
  60.0 11.6 %all_to_all.10 = f32[32,1,128]{2,1,0:T(1,128)S(1)} all-to-all(f32[32,1,128]{2,1,0:T(1,128)S(1)} %broadcast_in_dim.2), channel_id=1, replica_groups=mesh['tm'=16,'space'=32] {'space'}, dimensions={0} | all-to-all | bytes 32768 | tf_op jit(solution)/shard_map/all_to_all | solution.py:471
  71.6 0.0 collective-permute-done.5.back
  71.6 0.9 %shard_map.90 = (f32[96,256]{1,0:T(8,128)}, f32[96,256]{1,0:T(8,128)}) custom-call(f32[8,128]{1,0:T(8,128)S(1)} %get-tuple-element.21.flag, f32[1,128]{1,0:T(1,128)S(1)} %bitcast.4, f32[3,112,128]{2,1,0:T(8,128)S(1)} %get-tuple-element.27.down, f32[3,112,128]{2,1,0:T(8,128)S(1)} %get-tuple-element.28.up, f32[2,112,128]{2,1,0:T(8,128)S(1)} %get-tuple-element.32.one, ...), custom_call_target="tpu_custom_call" | custom-call | bytes 1048576 | tf_op jit(solution)/shard_map/pallas_call | solution.py:392
  (4 shorter events, 0.1 us)
Async XLA Ops:
  0.6 0.7 slice-start
  0.6 0.7 %slice-start.1 = ((f32[96,256]{1,0:T(8,128)}), f32[16,256]{1,0:T(8,128)S(1)}, s32[]{:S(2)}) async-start(f32[96,256]{1,0:T(8,128)} %obs_hbm.1), calls=%async_computation.3 | async-start | bytes 32768 | tf_op jit(solution)/shard_map/slice | solution.py:419
  1.4 8.8 %collective-permute-start = (f32[32,256]{1,0:T(8,128)S(1)}, f32[32,256]{1,0:T(8,128)S(1)}, u32[]{:S(2)}, u32[]{:S(2)}) collective-permute-start(f32[32,256]{1,0:T(8,128)S(1)} %pad_maximum_fusion), channel_id=1, source_target_pairs={{0,32},{32,64},{64,96},{96,128},{128,160},{160,192},{192,224},{224... | collective-permute-start | bytes 98312 | tf_op jit(solution)/shard_map/ppermute | solution.py:420
  10.6 8.3 %collective-permute-start.2 = (f32[3,112,128]{2,1,0:T(8,128)S(1)}, f32[3,112,128]{2,1,0:T(8,128)S(1)}, u32[]{:S(2)}, u32[]{:S(2)}) collective-permute-start(f32[3,112,128]{2,1,0:T(8,128)S(1)} %get-tuple-element.27.down), channel_id=1, source_target_pairs={{1,0},{2,1},{3,2},{4,3},{5,4},{6,5},{7,6},{8,7},{9,8},{10,9},{11,1... | collective-permute-start | bytes 516104 | tf_op jit(solution)/shard_map/ppermute | solution.py:455
  16.4 9.9 %collective-permute-start.1 = (f32[3,112,128]{2,1,0:T(8,128)S(1)}, f32[3,112,128]{2,1,0:T(8,128)S(1)}, u32[]{:S(2)}, u32[]{:S(2)}) collective-permute-start(f32[3,112,128]{2,1,0:T(8,128)S(1)} %get-tuple-element.28.up), channel_id=1, source_target_pairs={{0,1},{1,2},{2,3},{3,4},{4,5},{5,6},{6,7},{7,8},{8,9},{9,10},{10,1... | collective-permute-start | bytes 516104 | tf_op jit(solution)/shard_map/ppermute | solution.py:454
  27.5 6.5 %collective-permute-start.4 = (f32[2,112,128]{2,1,0:T(8,128)S(1)}, f32[2,112,128]{2,1,0:T(8,128)S(1)}, u32[]{:S(2)}, u32[]{:S(2)}) collective-permute-start(f32[2,112,128]{2,1,0:T(8,128)S(1)} %get-tuple-element.33.down_two), channel_id=1, source_target_pairs={{1,0},{2,1},{3,2},{4,3},{5,4},{6,5},{7,6},{8,7},{9,8},{10,9},{11,1... | collective-permute-start | bytes 344072 | tf_op jit(solution)/shard_map/ppermute | solution.py:461
  29.5 9.8 %collective-permute-start.3 = (f32[2,112,128]{2,1,0:T(8,128)S(1)}, f32[2,112,128]{2,1,0:T(8,128)S(1)}, u32[]{:S(2)}, u32[]{:S(2)}) collective-permute-start(f32[2,112,128]{2,1,0:T(8,128)S(1)} %get-tuple-element.34.up_two), channel_id=1, source_target_pairs={{0,1},{1,2},{2,3},{3,4},{4,5},{5,6},{6,7},{7,8},{8,9},{9,10},{10,1... | collective-permute-start | bytes 344072 | tf_op jit(solution)/shard_map/ppermute | solution.py:460
  40.8 19.1 %all-to-all-start = ((f32[16,1,128]{2,1,0:T(1,128)}), f32[16,1,128]{2,1,0:T(1,128)S(1)}, u32[]{:S(2)}, u32[]{:S(2)}) async-start(f32[16,1,128]{2,1,0:T(1,128)} %get-tuple-element.36), calls=%async_computation | async-start | bytes 16384 | tf_op jit(solution)/shard_map/all_to_all | solution.py:468
  53.0 18.6 %collective-permute-start.5 = (f32[2,4,8,128]{3,2,1,0:T(8,128)S(1)}, f32[2,4,8,128]{3,2,1,0:T(8,128)S(1)}, u32[]{:S(2)}, u32[]{:S(2)}) collective-permute-start(f32[2,4,8,128]{3,2,1,0:T(8,128)S(1)} %get-tuple-element.39), channel_id=1, source_target_pairs={{32,0},{64,32},{96,64},{128,96},{160,128},{192,160},{224,192},{256... | collective-permute-start | bytes 98312 | tf_op jit(solution)/shard_map/ppermute | solution.py:467

commit v6 on v5

--- a/solution.py
+++ b/solution.py
@@ -118,6 +118,7 @@
     entries = lists[0].astype(F32)
     here = lax.broadcasted_iota(jnp.int32, entries.shape, 1) == lax.axis_index("space")
     low = jnp.sum(jnp.where(here, entries, 0.0), axis=1, keepdims=True)
+    low = jnp.where(lax.axis_index("space") % 2 == 0, low, 1.0 - low)
     flag = jnp.broadcast_to(low, (8, BLOCK))
     flag_ref[...] = flag
     swapped = jnp.broadcast_to(low, (BLOCK, BLOCK)) > 0.5
@@ -450,15 +451,19 @@
         prepare_kernel, [pair, pair, triple, triple],
         right, obs, before, bands, flag, diagonal, local,
     )
-    up, down = ring("space", True)
-    below = lax.ppermute(to_up, "space", up)
-    above = lax.ppermute(to_down, "space", down)
+    parts = lax.axis_size("space")
+    inner = [(i, i ^ 1) for i in range(parts)]
+    outer = [(i, ((i + 1) ^ 1) - 1) for i in range(parts)]
+    outer = [(i, j % parts) for i, j in outer]
+    first, second = outer, inner
+    below = lax.ppermute(to_down, "space", first)
+    above = lax.ppermute(to_up, "space", second)
     one, down_two, up_two = call(
         first_kernel, [pair, pair, pair],
         to_down, to_up, below, above, precision, bands, local, into, out,
     )
-    below_two = lax.ppermute(up_two, "space", up)
-    above_two = lax.ppermute(down_two, "space", down)
+    below_two = lax.ppermute(down_two, "space", first)
+    above_two = lax.ppermute(up_two, "space", second)
     three, four, back, sums = call(
         second_kernel, [pair, pair, (2, 4, HALO, BLOCK), (lax.axis_size("tm"), 1, BLOCK)],
         to_down, to_up, below, above, one, down_two, up_two, below_two, above_two,

time: 73.1 us -> 70.5 us (0.964)
  waiting for transfers between devices: 20.8 us -> 16.4 us
  blocking collectives: 11.6 us -> 14.3 us
  starting transfers between devices: 32.5 us -> 31.7 us
    ppermute x4, waiting for transfers between devices: 14.4 us -> 9.9 us  [the longest x1 5.24 us: shards(): below_two = lax.ppermute(down_two, 'space', first)]
    all_to_all x1, blocking collectives: 11.6 us -> 14.3 us  [shards(): gathered = lax.all_to_all(sent, 'space', 0, 0)]
  transfers between devices with their start and end apart: 7 -> 7, of which waited for: 6 -> 5; matrix products, arithmetic and copies ran while one was open for 0% -> 0% of each run, Pallas kernels for 3% -> 3%
where the time goes in v6:
time: 70.5 us; the launch traced here: 70 us
  starting transfers between devices  31.7 us (45%)
  waiting for transfers between devices  16.4 us (23%)
  blocking collectives  14.3 us (20%)
  Pallas kernels  6.07 us (9%)
  local copies, waits for them, and re-layouts  0.74 us (1%)
  between operations  0.72 us (1%)
    all_to_all x1, blocking collectives, shards(): gathered = lax.all_to_all(sent, 'space', 0, 0)  14.3 us
    all_to_all x1, starting transfers between devices, shards(): gathered = lax.all_to_all(sums, 'tm', 0, 0)  11.6 us
    pallas_call x5, Pallas kernels, call(): pl.pallas_call(kernel, out_shape=[shape if isinstance(shape, jax.ShapeDty...  6.07 us
    ppermute x1, starting transfers between devices, shards(): below = lax.ppermute(to_down, 'space', first)  5.78 us
    ppermute x1, starting transfers between devices, shards(): before = lax.ppermute(last, 'tm', later)  5.38 us
    ppermute x1, waiting for transfers between devices, shards(): below_two = lax.ppermute(down_two, 'space', first)  5.24 us
    all_to_all x1, waiting for transfers between devices, shards(): gathered = lax.all_to_all(sums, 'tm', 0, 0)  4.93 us
    ppermute x1, starting transfers between devices, shards(): below_two = lax.ppermute(down_two, 'space', first)  3.1 us
  transfers between devices with their start and end apart: 7, of which 5 were waited for; matrix products, arithmetic and copies ran while one was open for 0% of the time, Pallas kernels for 3%

profile of v6, /device:TPU:1, one launch (start us, length us, event | category | flops | bytes accessed | tf_op | source)
XLA Modules:
  0.0 70.0 jit_solution(10224385345673353410)
XLA Ops:
  0.6 0.0 slice-start
  0.6 0.0 slice-start.1
  0.7 0.7 slice-done
  1.4 0.0 slice-done.1
  1.4 5.4 %collective-permute-start = (f32[32,256]{1,0:T(8,128)S(1)}, f32[32,256]{1,0:T(8,128)S(1)}, u32[]{:S(2)}, u32[]{:S(2)}) collective-permute-start(f32[32,256]{1,0:T(8,128)S(1)} %pad_maximum_fusion), channel_id=1, source_target_pairs={{0,32},{32,64},{64,96},{96,128},{128,160},{160,192},{192,224},{224... | collective-permute-start | bytes 98312 | tf_op jit(solution)/shard_map/ppermute | solution.py:421
  6.8 1.9 %shard_map.86 = (f32[11,112,128]{2,1,0:T(8,128)S(1)}, f32[8,128]{1,0:T(8,128)S(1)}, f32[8,128]{1,0:T(8,128)S(1)}, bf16[2,256,512]{2,1,0:T(8,128)(2,1)S(1)}, bf16...) custom-call(s32[2,1,32]{2,1,0:T(1,128)} %bitcast.7, ...), custom_call_target="tpu_custom_call" | custom-call | flops 2097152 | bytes 1048576 | tf_op jit(solution)/shard_map/pallas_call | solution.py:393
  8.7 1.5 %collective-permute-done.before = f32[32,256]{1,0:T(8,128)S(1)} collective-permute-done((f32[32,256]{1,0:T(8,128)S(1)}, f32[32,256]{1,0:T(8,128)S(1)}, u32[]{:S(2)}, u32[]{:S(2)}) %collective-permute-start) | collective-permute-done | bytes 32800 | tf_op jit(solution)/shard_map/ppermute | solution.py:421
  10.2 0.4 shard_map.87
  10.6 5.8 %collective-permute-start.1 = (f32[3,112,128]{2,1,0:T(8,128)S(1)}, f32[3,112,128]{2,1,0:T(8,128)S(1)}, u32[]{:S(2)}, u32[]{:S(2)}) collective-permute-start(f32[3,112,128]{2,1,0:T(8,128)S(1)} %get-tuple-element.27.down), channel_id=1, source_target_pairs={{0,31},{1,2},{2,1},{3,4},{4,3},{5,6},{6,5},{7,8},{8,7},{9,10},{10,... | collective-permute-start | bytes 516104 | tf_op jit(solution)/shard_map/ppermute | solution.py:459
  16.4 1.9 %collective-permute-start.2 = (f32[3,112,128]{2,1,0:T(8,128)S(1)}, f32[3,112,128]{2,1,0:T(8,128)S(1)}, u32[]{:S(2)}, u32[]{:S(2)}) collective-permute-start(f32[3,112,128]{2,1,0:T(8,128)S(1)} %get-tuple-element.28.up), channel_id=1, source_target_pairs={{0,1},{1,0},{2,3},{3,2},{4,5},{5,4},{6,7},{7,6},{8,9},{9,8},{10,11... | collective-permute-start | bytes 516104 | tf_op jit(solution)/shard_map/ppermute | solution.py:460
  18.3 2.1 %collective-permute-done.1.below = f32[3,112,128]{2,1,0:T(8,128)S(1)} collective-permute-done((f32[3,112,128]{2,1,0:T(8,128)S(1)}, f32[3,112,128]{2,1,0:T(8,128)S(1)}, u32[]{:S(2)}, u32[]{:S(2)}) %collective-permute-start.1) | collective-permute-done | bytes 172064 | tf_op jit(solution)/shard_map/ppermute | solution.py:459
  20.4 2.5 %collective-permute-done.2.above = f32[3,112,128]{2,1,0:T(8,128)S(1)} collective-permute-done((f32[3,112,128]{2,1,0:T(8,128)S(1)}, f32[3,112,128]{2,1,0:T(8,128)S(1)}, u32[]{:S(2)}, u32[]{:S(2)}) %collective-permute-start.2) | collective-permute-done | bytes 172064 | tf_op jit(solution)/shard_map/ppermute | solution.py:460
  23.0 1.2 %shard_map.88 = (f32[2,112,128]{2,1,0:T(8,128)S(1)}, f32[2,112,128]{2,1,0:T(8,128)S(1)}, f32[2,112,128]{2,1,0:T(8,128)S(1)}) custom-call(f32[3,112,128]{2,1,0:T(8,128)S(1)} %get-tuple-element.27.down, f32[3,112,128]{2,1,0:T(8,128)S(1)} %get-tuple-element.28.up, f32[3,112,128]{2,1,0:T(8,128)S(1)} %collective-permute-done.1.below, ...), custom_call_target="tpu_custom_call" | custom-call | bytes 1048576 | tf_op jit(solution)/shard_map/pallas_call | solution.py:393
  24.2 3.1 %collective-permute-start.3 = (f32[2,112,128]{2,1,0:T(8,128)S(1)}, f32[2,112,128]{2,1,0:T(8,128)S(1)}, u32[]{:S(2)}, u32[]{:S(2)}) collective-permute-start(f32[2,112,128]{2,1,0:T(8,128)S(1)} %get-tuple-element.33.down_two), channel_id=1, source_target_pairs={{0,31},{1,2},{2,1},{3,4},{4,3},{5,6},{6,5},{7,8},{8,7},{9,10},{10,... | collective-permute-start | bytes 344072 | tf_op jit(solution)/shard_map/ppermute | solution.py:465
  27.3 1.9 %collective-permute-start.4 = (f32[2,112,128]{2,1,0:T(8,128)S(1)}, f32[2,112,128]{2,1,0:T(8,128)S(1)}, u32[]{:S(2)}, u32[]{:S(2)}) collective-permute-start(f32[2,112,128]{2,1,0:T(8,128)S(1)} %get-tuple-element.34.up_two), channel_id=1, source_target_pairs={{0,1},{1,0},{2,3},{3,2},{4,5},{5,4},{6,7},{7,6},{8,9},{9,8},{10,11... | collective-permute-start | bytes 344072 | tf_op jit(solution)/shard_map/ppermute | solution.py:466
  29.3 5.2 %collective-permute-done.3.below_two = f32[2,112,128]{2,1,0:T(8,128)S(1)} collective-permute-done((f32[2,112,128]{2,1,0:T(8,128)S(1)}, f32[2,112,128]{2,1,0:T(8,128)S(1)}, u32[]{:S(2)}, u32[]{:S(2)}) %collective-permute-start.3) | collective-permute-done | bytes 114720 | tf_op jit(solution)/shard_map/ppermute | solution.py:465
  34.5 0.0 collective-permute-done.4.above_two
  34.5 1.6 %shard_map.89 = (f32[2,112,128]{2,1,0:T(8,128)S(1)}, f32[2,112,128]{2,1,0:T(8,128)S(1)}, f32[2,4,8,128]{3,2,1,0:T(8,128)S(1)}, f32[16,1,128]{2,1,0:T(1,128)}) custom-call(f32[3,112,128]{2,1,0:T(8,128)S(1)} %get-tuple-element.27.down, f32[3,112,128]{2,1,0:T(8,128)S(1)} %get-tuple-element.28.up, f32[3,112,128]{2,1,0:T(8,128)S(1)} %collective-permute-done.1.below, ...), custom_call_target="tpu_custom_call" | custom-call | bytes 1048576 | tf_op jit(solution)/shard_map/pallas_call | solution.py:393
  36.1 11.6 %all-to-all-start = ((f32[16,1,128]{2,1,0:T(1,128)}), f32[16,1,128]{2,1,0:T(1,128)S(1)}, u32[]{:S(2)}, u32[]{:S(2)}) async-start(f32[16,1,128]{2,1,0:T(1,128)} %get-tuple-element.36), calls=%async_computation | async-start | bytes 16384 | tf_op jit(solution)/shard_map/all_to_all | solution.py:473
  47.7 2.0 %collective-permute-start.5 = (f32[2,4,8,128]{3,2,1,0:T(8,128)S(1)}, f32[2,4,8,128]{3,2,1,0:T(8,128)S(1)}, u32[]{:S(2)}, u32[]{:S(2)}) collective-permute-start(f32[2,4,8,128]{3,2,1,0:T(8,128)S(1)} %get-tuple-element.39), channel_id=1, source_target_pairs={{32,0},{64,32},{96,64},{128,96},{160,128},{192,160},{224,192},{256... | collective-permute-start | bytes 98312 | tf_op jit(solution)/shard_map/ppermute | solution.py:472
  49.8 4.9 %all-to-all-done = f32[16,1,128]{2,1,0:T(1,128)S(1)} async-done(((f32[16,1,128]{2,1,0:T(1,128)}), f32[16,1,128]{2,1,0:T(1,128)S(1)}, u32[]{:S(2)}, u32[]{:S(2)}) %all-to-all-start) | async-done | bytes 8224 | tf_op jit(solution)/shard_map/all_to_all | solution.py:473
  54.7 14.3 %all_to_all.10 = f32[32,1,128]{2,1,0:T(1,128)S(1)} all-to-all(f32[32,1,128]{2,1,0:T(1,128)S(1)} %broadcast_in_dim.2), channel_id=1, replica_groups=mesh['tm'=16,'space'=32] {'space'}, dimensions={0} | all-to-all | bytes 32768 | tf_op jit(solution)/shard_map/all_to_all | solution.py:476
  69.0 0.0 collective-permute-done.5.back
  69.0 0.9 %shard_map.90 = (f32[96,256]{1,0:T(8,128)}, f32[96,256]{1,0:T(8,128)}) custom-call(f32[8,128]{1,0:T(8,128)S(1)} %get-tuple-element.21.flag, f32[1,128]{1,0:T(1,128)S(1)} %bitcast.4, f32[3,112,128]{2,1,0:T(8,128)S(1)} %get-tuple-element.27.down, f32[3,112,128]{2,1,0:T(8,128)S(1)} %get-tuple-element.28.up, f32[2,112,128]{2,1,0:T(8,128)S(1)} %get-tuple-element.32.one, ...), custom_call_target="tpu_custom_call" | custom-call | bytes 1048576 | tf_op jit(solution)/shard_map/pallas_call | solution.py:393
  (4 shorter events, 0.1 us)
Async XLA Ops:
  0.6 0.7 %slice-start = ((f32[96,256]{1,0:T(8,128)}), f32[16,256]{1,0:T(8,128)S(1)}, s32[]{:S(2)}) async-start(f32[96,256]{1,0:T(8,128)} %right_hbm.1), calls=%async_computation.2 | async-start | bytes 32768 | tf_op jit(solution)/shard_map/slice | solution.py:420
  0.6 0.7 %slice-start.1 = ((f32[96,256]{1,0:T(8,128)}), f32[16,256]{1,0:T(8,128)S(1)}, s32[]{:S(2)}) async-start(f32[96,256]{1,0:T(8,128)} %obs_hbm.1), calls=%async_computation.3 | async-start | bytes 32768 | tf_op jit(solution)/shard_map/slice | solution.py:420
  1.4 8.8 %collective-permute-start = (f32[32,256]{1,0:T(8,128)S(1)}, f32[32,256]{1,0:T(8,128)S(1)}, u32[]{:S(2)}, u32[]{:S(2)}) collective-permute-start(f32[32,256]{1,0:T(8,128)S(1)} %pad_maximum_fusion), channel_id=1, source_target_pairs={{0,32},{32,64},{64,96},{96,128},{128,160},{160,192},{192,224},{224... | collective-permute-start | bytes 98312 | tf_op jit(solution)/shard_map/ppermute | solution.py:421
  10.6 9.8 %collective-permute-start.1 = (f32[3,112,128]{2,1,0:T(8,128)S(1)}, f32[3,112,128]{2,1,0:T(8,128)S(1)}, u32[]{:S(2)}, u32[]{:S(2)}) collective-permute-start(f32[3,112,128]{2,1,0:T(8,128)S(1)} %get-tuple-element.27.down), channel_id=1, source_target_pairs={{0,31},{1,2},{2,1},{3,4},{4,3},{5,6},{6,5},{7,8},{8,7},{9,10},{10,... | collective-permute-start | bytes 516104 | tf_op jit(solution)/shard_map/ppermute | solution.py:459
  16.4 6.6 %collective-permute-start.2 = (f32[3,112,128]{2,1,0:T(8,128)S(1)}, f32[3,112,128]{2,1,0:T(8,128)S(1)}, u32[]{:S(2)}, u32[]{:S(2)}) collective-permute-start(f32[3,112,128]{2,1,0:T(8,128)S(1)} %get-tuple-element.28.up), channel_id=1, source_target_pairs={{0,1},{1,0},{2,3},{3,2},{4,5},{5,4},{6,7},{7,6},{8,9},{9,8},{10,11... | collective-permute-start | bytes 516104 | tf_op jit(solution)/shard_map/ppermute | solution.py:460
  24.2 10.3 %collective-permute-start.3 = (f32[2,112,128]{2,1,0:T(8,128)S(1)}, f32[2,112,128]{2,1,0:T(8,128)S(1)}, u32[]{:S(2)}, u32[]{:S(2)}) collective-permute-start(f32[2,112,128]{2,1,0:T(8,128)S(1)} %get-tuple-element.33.down_two), channel_id=1, source_target_pairs={{0,31},{1,2},{2,1},{3,4},{4,3},{5,6},{6,5},{7,8},{8,7},{9,10},{10,... | collective-permute-start | bytes 344072 | tf_op jit(solution)/shard_map/ppermute | solution.py:465
  27.3 7.2 %collective-permute-start.4 = (f32[2,112,128]{2,1,0:T(8,128)S(1)}, f32[2,112,128]{2,1,0:T(8,128)S(1)}, u32[]{:S(2)}, u32[]{:S(2)}) collective-permute-start(f32[2,112,128]{2,1,0:T(8,128)S(1)} %get-tuple-element.34.up_two), channel_id=1, source_target_pairs={{0,1},{1,0},{2,3},{3,2},{4,5},{5,4},{6,7},{7,6},{8,9},{9,8},{10,11... | collective-permute-start | bytes 344072 | tf_op jit(solution)/shard_map/ppermute | solution.py:466
  36.1 18.6 %all-to-all-start = ((f32[16,1,128]{2,1,0:T(1,128)}), f32[16,1,128]{2,1,0:T(1,128)S(1)}, u32[]{:S(2)}, u32[]{:S(2)}) async-start(f32[16,1,128]{2,1,0:T(1,128)} %get-tuple-element.36), calls=%async_computation | async-start | bytes 16384 | tf_op jit(solution)/shard_map/all_to_all | solution.py:473
  47.7 21.3 %collective-permute-start.5 = (f32[2,4,8,128]{3,2,1,0:T(8,128)S(1)}, f32[2,4,8,128]{3,2,1,0:T(8,128)S(1)}, u32[]{:S(2)}, u32[]{:S(2)}) collective-permute-start(f32[2,4,8,128]{3,2,1,0:T(8,128)S(1)} %get-tuple-element.39), channel_id=1, source_target_pairs={{32,0},{64,32},{96,64},{128,96},{160,128},{192,160},{224,192},{256... | collective-permute-start | bytes 98312 | tf_op jit(solution)/shard_map/ppermute | solution.py:472

commit v7 on v5

--- a/solution.py
+++ b/solution.py
@@ -81,7 +81,7 @@
     time_rows, time_total = right.shape[0], band_rows.shape[2]
     extent = time_rows + FRONT
 
-    first = lax.axis_index("tm") * time_rows - FRONT - 2
+    first = lax.axis_index("tm") * time_rows - 2
     tile = (first + time_total) // BLOCK - time_total // BLOCK
     shift = first - tile * BLOCK
     last_tile = time_total // BLOCK - 1
@@ -104,7 +104,7 @@
         rows = [window(band, matrix) for band in range(3)]
         for offset, band, shifted in TERMS:
             line = pltpu.roll(rows[band], (-(2 + shifted)) % BLOCK, 1)
-            lines.append(jnp.where(lane >= offset, line, 0.0) if offset > 0 else line)
+            lines.append(jnp.where(lane < extent + offset, line, 0.0) if offset < 0 else line)
     valid = jnp.where(inside, 1.0, 0.0)
     lines.append(pltpu.roll(valid, BLOCK - 2, 1))
     count = len(lines)
@@ -118,6 +118,8 @@
     entries = lists[0].astype(F32)
     here = lax.broadcasted_iota(jnp.int32, entries.shape, 1) == lax.axis_index("space")
     low = jnp.sum(jnp.where(here, entries, 0.0), axis=1, keepdims=True)
+    turn = lax.axis_index("space") + lax.axis_index("tm")
+    low = jnp.where(turn % 2 == 0, low, 1.0 - low)
     flag = jnp.broadcast_to(low, (8, BLOCK))
     flag_ref[...] = flag
     swapped = jnp.broadcast_to(low, (BLOCK, BLOCK)) > 0.5
@@ -173,17 +175,17 @@
 
 
 def prepare_kernel(
-    right, obs, before, bands, flag, diagonal, local,
+    right, obs, after, bands, flag, diagonal, local,
     precond_ref, obs_ref, down_ref, up_ref,
 ):
     swapped = flag[...] > 0.5
 
     def extended(middle, start):
-        rows = before[start : start + FRONT]
+        rows = after[start : start + FRONT]
         one, two = rows[:, :BLOCK], rows[:, BLOCK:]
         turned = jnp.concatenate([swapped] * (FRONT // 8), axis=0)
         ends = (jnp.where(turned, two, one), jnp.where(turned, one, two))
-        return [jnp.concatenate([ends[k], middle[k]], axis=0) for k in range(2)]
+        return [jnp.concatenate([middle[k], ends[k]], axis=0) for k in range(2)]
 
     rhs, precision = extended(right, 0), extended(obs, FRONT)
     valid = bands[10]
@@ -266,18 +268,18 @@
     olders = [ref[0] for ref in own_two]
     four = full_step(bands, local, into, vectors, nears, obs, inverses, olders)
     extent = bands.shape[1]
-    final = lax.axis_index("tm") == lax.axis_size("tm") - 1
-    counted = lax.broadcasted_iota(jnp.int32, (extent - HALO, BLOCK), 0) < extent - FRONT
-    counted = jnp.where(counted | final, 1.0, 0.0)
+    initial = lax.axis_index("tm") == 0
+    counted = lax.broadcasted_iota(jnp.int32, (extent - HALO, BLOCK), 0) >= HALO
+    counted = jnp.where(counted | initial, 1.0, 0.0)
     sums = [0.0] * 14
     for place in range(2):
         three_ref[place] = vectors[place]
         four_ref[place] = four[place]
         basis = (own[place][0], one[place], olders[place], vectors[place], four[place])
         for k in range(4):
-            back_ref[place, k] = basis[k + 1][HALO:FRONT]
-        basis = [rows[HALO:] for rows in basis]
-        weight = counted * precond[place][HALO:]
+            back_ref[place, k] = basis[k + 1][extent - FRONT : extent - HALO]
+        basis = [rows[: extent - HALO] for rows in basis]
+        weight = counted * precond[place][: extent - HALO]
         index = 0
         for i in range(4):
             weighted = weight * basis[i]
@@ -363,17 +365,17 @@
             direction = combined(state, norm_next / norm_now, direction)
             norm_now = norm_next
     swapped = flag[0:1] > 0.5
-    final = lax.axis_index("tm") == lax.axis_size("tm") - 1
+    initial = lax.axis_index("tm") == 0
     solutions, residuals = [], []
     for place, (ref, ref_two) in enumerate(((down, down_two), (up, up_two))):
         basis = (ref[0], one[place], ref_two[0], three[place], four[place])
         extent = precond.shape[1]
-        start = basis[0][FRONT:]
+        start = basis[0][: extent - FRONT]
         basis = [
             jnp.concatenate(
                 [
-                    rows[FRONT : extent - HALO],
-                    jnp.where(final, rows[extent - HALO :], back[place, k]),
+                    jnp.where(initial, rows[:HALO], back[1 - place, k]),
+                    rows[HALO : extent - FRONT],
                 ],
                 axis=0,
             )
@@ -382,7 +384,7 @@
         basis.insert(0, start)
         solutions.append(added([answer[k] * basis[k] for k in range(4)]))
         left = added([state[k] * basis[k] for k in range(5)])
-        residuals.append(left * precond[place][FRONT:])
+        residuals.append(left * precond[place][: extent - FRONT])
     for ref, pair in ((solution_ref, solutions), (residual_ref, residuals)):
         ref[:, :BLOCK] = jnp.where(swapped, pair[1], pair[0])
         ref[:, BLOCK:] = jnp.where(swapped, pair[0], pair[1])
@@ -416,8 +418,8 @@
     extent = time_rows + FRONT
 
     later, earlier = ring("tm", False)
-    last = jnp.concatenate([right_side[-FRONT:], obs_precision[-FRONT:]], axis=0)
-    before = lax.ppermute(last, "tm", later)
+    first = jnp.concatenate([right_side[:FRONT], obs_precision[:FRONT]], axis=0)
+    after = lax.ppermute(first, "tm", earlier)
 
     wide = 2 * BLOCK
     stored = (
@@ -448,23 +450,32 @@
     triple = (3, extent, BLOCK)
     precond, precision, to_down, to_up = call(
         prepare_kernel, [pair, pair, triple, triple],
-        right, obs, before, bands, flag, diagonal, local,
-    )
-    up, down = ring("space", True)
-    below = lax.ppermute(to_up, "space", up)
-    above = lax.ppermute(to_down, "space", down)
+        right, obs, after, bands, flag, diagonal, local,
+    )
+    parts = lax.axis_size("space")
+    swaps = ([], [])
+    for slab in range(lax.axis_size("tm")):
+        for i in range(parts):
+            outer = (((i + 1) ^ 1) - 1) % parts
+            order = (outer, i ^ 1) if slab % 2 == 0 else (i ^ 1, outer)
+            for pairs, j in zip(swaps, order):
+                pairs.append((slab * parts + i, slab * parts + j))
+    first, second = swaps
+    both = ("tm", "space")
+    below = lax.ppermute(to_down, both, first)
+    above = lax.ppermute(to_up, both, second)
     one, down_two, up_two = call(
         first_kernel, [pair, pair, pair],
         to_down, to_up, below, above, precision, bands, local, into, out,
     )
-    below_two = lax.ppermute(up_two, "space", up)
-    above_two = lax.ppermute(down_two, "space", down)
+    below_two = lax.ppermute(down_two, both, first)
+    above_two = lax.ppermute(up_two, both, second)
     three, four, back, sums = call(
         second_kernel, [pair, pair, (2, 4, HALO, BLOCK), (lax.axis_size("tm"), 1, BLOCK)],
         to_down, to_up, below, above, one, down_two, up_two, below_two, above_two,
         precond, precision, bands, local, into, out,
     )
-    back = lax.ppermute(back, "tm", earlier)
+    back = lax.ppermute(back, "tm", later)
     gathered = lax.all_to_all(sums, "tm", 0, 0)
     sums = jnp.sum(gathered, axis=0)
     sent = jnp.broadcast_to(sums[None], (lax.axis_size("space"), 1, BLOCK))

time: 73.1 us -> 68.3 us (0.934)
  waiting for transfers between devices: 20.8 us -> 12.5 us
  blocking collectives: 11.6 us -> 13.7 us
  starting transfers between devices: 32.5 us -> 33.9 us
    ppermute x6, waiting for transfers between devices: 15.9 us -> 9.11 us  [the longest x1 4.86 us: shards(): above = lax.ppermute(to_up, both, second)]
    ppermute x6, starting transfers between devices: 20.4 us -> 25.3 us  [the longest x1 8.77 us: shards(): after = lax.ppermute(first, 'tm', earlier)]
    all_to_all x1, starting transfers between devices: 12.1 us -> 8.59 us  [shards(): gathered = lax.all_to_all(sums, 'tm', 0, 0)]
    all_to_all x1, blocking collectives: 11.6 us -> 13.7 us  [shards(): gathered = lax.all_to_all(sent, 'space', 0, 0)]
    all_to_all x1, waiting for transfers between devices: 4.93 us -> 3.41 us  [shards(): gathered = lax.all_to_all(sums, 'tm', 0, 0)]
  transfers between devices with their start and end apart: 7 -> 7, of which waited for: 6 -> 3; matrix products, arithmetic and copies ran while one was open for 0% -> 0% of each run, Pallas kernels for 3% -> 3%
where the time goes in v7:
time: 68.3 us; the launch traced here: 67.8 us
  starting transfers between devices  33.9 us (50%)
  blocking collectives  13.7 us (20%)
  waiting for transfers between devices  12.5 us (18%)
  Pallas kernels  6.08 us (9%)
  local copies, waits for them, and re-layouts  0.74 us (1%)
  between operations  0.74 us (1%)
    all_to_all x1, blocking collectives, shards(): gathered = lax.all_to_all(sent, 'space', 0, 0)  13.7 us
    ppermute x1, starting transfers between devices, shards(): after = lax.ppermute(first, 'tm', earlier)  8.77 us
    all_to_all x1, starting transfers between devices, shards(): gathered = lax.all_to_all(sums, 'tm', 0, 0)  8.59 us
    pallas_call x5, Pallas kernels, call(): pl.pallas_call(kernel, out_shape=[shape if isinstance(shape, jax.ShapeDty...  6.08 us
    ppermute x1, waiting for transfers between devices, shards(): above = lax.ppermute(to_up, both, second)  4.86 us
    ppermute x1, starting transfers between devices, shards(): above = lax.ppermute(to_up, both, second)  4.6 us
    ppermute x1, starting transfers between devices, shards(): above_two = lax.ppermute(up_two, both, second)  4.59 us
    ppermute x1, waiting for transfers between devices, shards(): above_two = lax.ppermute(up_two, both, second)  4.25 us
  transfers between devices with their start and end apart: 7, of which 3 were waited for; matrix products, arithmetic and copies ran while one was open for 0% of the time, Pallas kernels for 3%

profile of v7, /device:TPU:1, one launch (start us, length us, event | category | flops | bytes accessed | tf_op | source)
XLA Modules:
  0.0 67.8 jit_solution(3326799916493160968)
XLA Ops:
  0.6 0.0 slice-start
  0.6 0.0 slice-start.1
  0.7 0.7 %slice-done = f32[16,256]{1,0:T(8,128)S(1)} async-done(((f32[96,256]{1,0:T(8,128)}), f32[16,256]{1,0:T(8,128)S(1)}, s32[]{:S(2)}) %slice-start) | async-done | bytes 16408 | tf_op jit(solution)/shard_map/slice | solution.py:421
  1.4 0.0 slice-done.1
  1.4 8.8 %collective-permute-start = (f32[32,256]{1,0:T(8,128)S(1)}, f32[32,256]{1,0:T(8,128)S(1)}, u32[]{:S(2)}, u32[]{:S(2)}) collective-permute-start(f32[32,256]{1,0:T(8,128)S(1)} %pad_maximum_fusion), channel_id=1, source_target_pairs={{32,0},{64,32},{96,64},{128,96},{160,128},{192,160},{224,192},{256... | collective-permute-start | bytes 98312 | tf_op jit(solution)/shard_map/ppermute | solution.py:422
  10.2 1.9 %shard_map.86 = (f32[11,112,128]{2,1,0:T(8,128)S(1)}, f32[8,128]{1,0:T(8,128)S(1)}, f32[8,128]{1,0:T(8,128)S(1)}, bf16[2,256,512]{2,1,0:T(8,128)(2,1)S(1)}, bf16...) custom-call(s32[2,1,32]{2,1,0:T(1,128)} %bitcast.7, ...), custom_call_target="tpu_custom_call" | custom-call | flops 2097152 | bytes 1048576 | tf_op jit(solution)/shard_map/pallas_call | solution.py:394
  12.1 0.0 collective-permute-done.after
  12.1 0.4 shard_map.87
  12.5 1.9 %collective-permute-start.1 = (f32[3,112,128]{2,1,0:T(8,128)S(1)}, f32[3,112,128]{2,1,0:T(8,128)S(1)}, u32[]{:S(2)}, u32[]{:S(2)}) collective-permute-start(f32[3,112,128]{2,1,0:T(8,128)S(1)} %get-tuple-element.27.down), channel_id=1, source_target_pairs={{0,31},{1,2},{2,1},{3,4},{4,3},{5,6},{6,5},{7,8},{8,7},{9,10},{10,... | collective-permute-start | bytes 516104 | tf_op jit(solution)/shard_map/ppermute | solution.py:465
  14.4 4.6 %collective-permute-start.2 = (f32[3,112,128]{2,1,0:T(8,128)S(1)}, f32[3,112,128]{2,1,0:T(8,128)S(1)}, u32[]{:S(2)}, u32[]{:S(2)}) collective-permute-start(f32[3,112,128]{2,1,0:T(8,128)S(1)} %get-tuple-element.28.up), channel_id=1, source_target_pairs={{0,1},{1,0},{2,3},{3,2},{4,5},{5,4},{6,7},{7,6},{8,9},{9,8},{10,11... | collective-permute-start | bytes 516104 | tf_op jit(solution)/shard_map/ppermute | solution.py:466
  19.0 0.0 collective-permute-done.1.below
  19.0 4.9 %collective-permute-done.2.above = f32[3,112,128]{2,1,0:T(8,128)S(1)} collective-permute-done((f32[3,112,128]{2,1,0:T(8,128)S(1)}, f32[3,112,128]{2,1,0:T(8,128)S(1)}, u32[]{:S(2)}, u32[]{:S(2)}) %collective-permute-start.2) | collective-permute-done | bytes 172064 | tf_op jit(solution)/shard_map/ppermute | solution.py:466
  23.9 1.2 %shard_map.88 = (f32[2,112,128]{2,1,0:T(8,128)S(1)}, f32[2,112,128]{2,1,0:T(8,128)S(1)}, f32[2,112,128]{2,1,0:T(8,128)S(1)}) custom-call(f32[3,112,128]{2,1,0:T(8,128)S(1)} %get-tuple-element.27.down, f32[3,112,128]{2,1,0:T(8,128)S(1)} %get-tuple-element.28.up, f32[3,112,128]{2,1,0:T(8,128)S(1)} %collective-permute-done.1.below, ...), custom_call_target="tpu_custom_call" | custom-call | bytes 1048576 | tf_op jit(solution)/shard_map/pallas_call | solution.py:394
  25.1 1.9 %collective-permute-start.3 = (f32[2,112,128]{2,1,0:T(8,128)S(1)}, f32[2,112,128]{2,1,0:T(8,128)S(1)}, u32[]{:S(2)}, u32[]{:S(2)}) collective-permute-start(f32[2,112,128]{2,1,0:T(8,128)S(1)} %get-tuple-element.33.down_two), channel_id=1, source_target_pairs={{0,31},{1,2},{2,1},{3,4},{4,3},{5,6},{6,5},{7,8},{8,7},{9,10},{10,... | collective-permute-start | bytes 344072 | tf_op jit(solution)/shard_map/ppermute | solution.py:471
  27.1 4.6 %collective-permute-start.4 = (f32[2,112,128]{2,1,0:T(8,128)S(1)}, f32[2,112,128]{2,1,0:T(8,128)S(1)}, u32[]{:S(2)}, u32[]{:S(2)}) collective-permute-start(f32[2,112,128]{2,1,0:T(8,128)S(1)} %get-tuple-element.34.up_two), channel_id=1, source_target_pairs={{0,1},{1,0},{2,3},{3,2},{4,5},{5,4},{6,7},{7,6},{8,9},{9,8},{10,11... | collective-permute-start | bytes 344072 | tf_op jit(solution)/shard_map/ppermute | solution.py:472
  31.7 0.0 collective-permute-done.3.below_two
  31.7 4.2 %collective-permute-done.4.above_two = f32[2,112,128]{2,1,0:T(8,128)S(1)} collective-permute-done((f32[2,112,128]{2,1,0:T(8,128)S(1)}, f32[2,112,128]{2,1,0:T(8,128)S(1)}, u32[]{:S(2)}, u32[]{:S(2)}) %collective-permute-start.4) | collective-permute-done | bytes 114720 | tf_op jit(solution)/shard_map/ppermute | solution.py:472
  35.9 1.6 %shard_map.89 = (f32[2,112,128]{2,1,0:T(8,128)S(1)}, f32[2,112,128]{2,1,0:T(8,128)S(1)}, f32[2,4,8,128]{3,2,1,0:T(8,128)S(1)}, f32[16,1,128]{2,1,0:T(1,128)}) custom-call(f32[3,112,128]{2,1,0:T(8,128)S(1)} %get-tuple-element.27.down, f32[3,112,128]{2,1,0:T(8,128)S(1)} %get-tuple-element.28.up, f32[3,112,128]{2,1,0:T(8,128)S(1)} %collective-permute-done.1.below, ...), custom_call_target="tpu_custom_call" | custom-call | bytes 1048576 | tf_op jit(solution)/shard_map/pallas_call | solution.py:394
  37.5 8.6 %all-to-all-start = ((f32[16,1,128]{2,1,0:T(1,128)}), f32[16,1,128]{2,1,0:T(1,128)S(1)}, u32[]{:S(2)}, u32[]{:S(2)}) async-start(f32[16,1,128]{2,1,0:T(1,128)} %get-tuple-element.36), calls=%async_computation | async-start | bytes 16384 | tf_op jit(solution)/shard_map/all_to_all | solution.py:479
  46.1 3.5 %collective-permute-start.5 = (f32[2,4,8,128]{3,2,1,0:T(8,128)S(1)}, f32[2,4,8,128]{3,2,1,0:T(8,128)S(1)}, u32[]{:S(2)}, u32[]{:S(2)}) collective-permute-start(f32[2,4,8,128]{3,2,1,0:T(8,128)S(1)} %get-tuple-element.39), channel_id=1, source_target_pairs={{0,32},{32,64},{64,96},{96,128},{128,160},{160,192},{192,224},{224... | collective-permute-start | bytes 98312 | tf_op jit(solution)/shard_map/ppermute | solution.py:478
  49.7 3.4 %all-to-all-done = f32[16,1,128]{2,1,0:T(1,128)S(1)} async-done(((f32[16,1,128]{2,1,0:T(1,128)}), f32[16,1,128]{2,1,0:T(1,128)S(1)}, u32[]{:S(2)}, u32[]{:S(2)}) %all-to-all-start) | async-done | bytes 8224 | tf_op jit(solution)/shard_map/all_to_all | solution.py:479
  53.1 13.7 %all_to_all.10 = f32[32,1,128]{2,1,0:T(1,128)S(1)} all-to-all(f32[32,1,128]{2,1,0:T(1,128)S(1)} %broadcast_in_dim.2), channel_id=1, replica_groups=mesh['tm'=16,'space'=32] {'space'}, dimensions={0} | all-to-all | bytes 32768 | tf_op jit(solution)/shard_map/all_to_all | solution.py:482
  66.9 0.0 collective-permute-done.5.back
  66.9 0.9 %shard_map.90 = (f32[96,256]{1,0:T(8,128)}, f32[96,256]{1,0:T(8,128)}) custom-call(f32[8,128]{1,0:T(8,128)S(1)} %get-tuple-element.21.flag, f32[1,128]{1,0:T(1,128)S(1)} %bitcast.4, f32[3,112,128]{2,1,0:T(8,128)S(1)} %get-tuple-element.27.down, f32[3,112,128]{2,1,0:T(8,128)S(1)} %get-tuple-element.28.up, f32[2,112,128]{2,1,0:T(8,128)S(1)} %get-tuple-element.32.one, ...), custom_call_target="tpu_custom_call" | custom-call | bytes 1048576 | tf_op jit(solution)/shard_map/pallas_call | solution.py:394
  (4 shorter events, 0.1 us)
Async XLA Ops:
  0.6 0.7 %slice-start = ((f32[96,256]{1,0:T(8,128)}), f32[16,256]{1,0:T(8,128)S(1)}, s32[]{:S(2)}) async-start(f32[96,256]{1,0:T(8,128)} %right_hbm.1), calls=%async_computation.2 | async-start | bytes 32768 | tf_op jit(solution)/shard_map/slice | solution.py:421
  0.6 0.7 %slice-start.1 = ((f32[96,256]{1,0:T(8,128)}), f32[16,256]{1,0:T(8,128)S(1)}, s32[]{:S(2)}) async-start(f32[96,256]{1,0:T(8,128)} %obs_hbm.1), calls=%async_computation.3 | async-start | bytes 32768 | tf_op jit(solution)/shard_map/slice | solution.py:421
  1.4 10.7 %collective-permute-start = (f32[32,256]{1,0:T(8,128)S(1)}, f32[32,256]{1,0:T(8,128)S(1)}, u32[]{:S(2)}, u32[]{:S(2)}) collective-permute-start(f32[32,256]{1,0:T(8,128)S(1)} %pad_maximum_fusion), channel_id=1, source_target_pairs={{32,0},{64,32},{96,64},{128,96},{160,128},{192,160},{224,192},{256... | collective-permute-start | bytes 98312 | tf_op jit(solution)/shard_map/ppermute | solution.py:422
  12.5 6.5 %collective-permute-start.1 = (f32[3,112,128]{2,1,0:T(8,128)S(1)}, f32[3,112,128]{2,1,0:T(8,128)S(1)}, u32[]{:S(2)}, u32[]{:S(2)}) collective-permute-start(f32[3,112,128]{2,1,0:T(8,128)S(1)} %get-tuple-element.27.down), channel_id=1, source_target_pairs={{0,31},{1,2},{2,1},{3,4},{4,3},{5,6},{6,5},{7,8},{8,7},{9,10},{10,... | collective-permute-start | bytes 516104 | tf_op jit(solution)/shard_map/ppermute | solution.py:465
  14.4 9.5 %collective-permute-start.2 = (f32[3,112,128]{2,1,0:T(8,128)S(1)}, f32[3,112,128]{2,1,0:T(8,128)S(1)}, u32[]{:S(2)}, u32[]{:S(2)}) collective-permute-start(f32[3,112,128]{2,1,0:T(8,128)S(1)} %get-tuple-element.28.up), channel_id=1, source_target_pairs={{0,1},{1,0},{2,3},{3,2},{4,5},{5,4},{6,7},{7,6},{8,9},{9,8},{10,11... | collective-permute-start | bytes 516104 | tf_op jit(solution)/shard_map/ppermute | solution.py:466
  25.1 6.5 %collective-permute-start.3 = (f32[2,112,128]{2,1,0:T(8,128)S(1)}, f32[2,112,128]{2,1,0:T(8,128)S(1)}, u32[]{:S(2)}, u32[]{:S(2)}) collective-permute-start(f32[2,112,128]{2,1,0:T(8,128)S(1)} %get-tuple-element.33.down_two), channel_id=1, source_target_pairs={{0,31},{1,2},{2,1},{3,4},{4,3},{5,6},{6,5},{7,8},{8,7},{9,10},{10,... | collective-permute-start | bytes 344072 | tf_op jit(solution)/shard_map/ppermute | solution.py:471
  27.1 8.9 %collective-permute-start.4 = (f32[2,112,128]{2,1,0:T(8,128)S(1)}, f32[2,112,128]{2,1,0:T(8,128)S(1)}, u32[]{:S(2)}, u32[]{:S(2)}) collective-permute-start(f32[2,112,128]{2,1,0:T(8,128)S(1)} %get-tuple-element.34.up_two), channel_id=1, source_target_pairs={{0,1},{1,0},{2,3},{3,2},{4,5},{5,4},{6,7},{7,6},{8,9},{9,8},{10,11... | collective-permute-start | bytes 344072 | tf_op jit(solution)/shard_map/ppermute | solution.py:472
  37.5 15.5 %all-to-all-start = ((f32[16,1,128]{2,1,0:T(1,128)}), f32[16,1,128]{2,1,0:T(1,128)S(1)}, u32[]{:S(2)}, u32[]{:S(2)}) async-start(f32[16,1,128]{2,1,0:T(1,128)} %get-tuple-element.36), calls=%async_computation | async-start | bytes 16384 | tf_op jit(solution)/shard_map/all_to_all | solution.py:479
  46.1 20.8 %collective-permute-start.5 = (f32[2,4,8,128]{3,2,1,0:T(8,128)S(1)}, f32[2,4,8,128]{3,2,1,0:T(8,128)S(1)}, u32[]{:S(2)}, u32[]{:S(2)}) collective-permute-start(f32[2,4,8,128]{3,2,1,0:T(8,128)S(1)} %get-tuple-element.39), channel_id=1, source_target_pairs={{0,32},{32,64},{64,96},{96,128},{128,160},{160,192},{192,224},{224... | collective-permute-start | bytes 98312 | tf_op jit(solution)/shard_map/ppermute | solution.py:478

commit v8 on v7

--- a/solution.py
+++ b/solution.py
@@ -468,8 +468,13 @@
         first_kernel, [pair, pair, pair],
         to_down, to_up, below, above, precision, bands, local, into, out,
     )
-    below_two = lax.ppermute(down_two, both, first)
-    above_two = lax.ppermute(up_two, both, second)
+    even = lax.axis_index("tm") % 2 == 0
+    outer = [(i, (((i + 1) ^ 1) - 1) % parts) for i in range(parts)]
+    inner = [(i, i ^ 1) for i in range(parts)]
+    came_outer = lax.ppermute(jnp.where(even, down_two, up_two), "space", outer)
+    came_inner = lax.ppermute(jnp.where(even, up_two, down_two), "space", inner)
+    below_two = jnp.where(even, came_outer, came_inner)
+    above_two = jnp.where(even, came_inner, came_outer)
     three, four, back, sums = call(
         second_kernel, [pair, pair, (2, 4, HALO, BLOCK), (lax.axis_size("tm"), 1, BLOCK)],
         to_down, to_up, below, above, one, down_two, up_two, below_two, above_two,

time: 68.3 us -> 69.3 us (1.015)
  starting transfers between devices: 33.9 us -> 34.6 us
    all_to_all x1, starting transfers between devices: 8.59 us -> 9.3 us  [shards(): gathered = lax.all_to_all(sums, 'tm', 0, 0)]
where the time goes in v8:
time: 69.3 us; the launch traced here: 68.8 us
  starting transfers between devices  34.6 us (50%)
  blocking collectives  13.7 us (20%)
  waiting for transfers between devices  12.8 us (18%)
  Pallas kernels  6.13 us (9%)
  between operations  0.77 us (1%)
  local copies, waits for them, and re-layouts  0.74 us (1%)
    all_to_all x1, blocking collectives, shards(): gathered = lax.all_to_all(sent, 'space', 0, 0)  13.7 us
    all_to_all x1, starting transfers between devices, shards(): gathered = lax.all_to_all(sums, 'tm', 0, 0)  9.3 us
    ppermute x1, starting transfers between devices, shards(): after = lax.ppermute(first, 'tm', earlier)  8.77 us
    pallas_call x5, Pallas kernels, call(): pl.pallas_call(kernel, out_shape=[shape if isinstance(shape, jax.ShapeDty...  6.13 us
    ppermute x1, waiting for transfers between devices, shards(): above = lax.ppermute(to_up, both, second)  4.84 us
    ppermute x1, starting transfers between devices, shards(): above = lax.ppermute(to_up, both, second)  4.6 us
    ppermute x1, starting transfers between devices, shards(): came_outer = lax.ppermute(jnp.where(even, down_two, up_two), 'space', outer)  4.59 us
    ppermute x1, waiting for transfers between devices, shards(): came_outer = lax.ppermute(jnp.where(even, down_two, up_two), 'space', outer)  4.54 us
  transfers between devices with their start and end apart: 7, of which 3 were waited for; matrix products, arithmetic and copies ran while one was open for 0% of the time, Pallas kernels for 3%

profile of v8, /device:TPU:1, one launch (start us, length us, event | category | flops | bytes accessed | tf_op | source)
XLA Modules:
  0.0 68.8 jit_solution(1527256469132702669)
XLA Ops:
  0.6 0.0 slice-start
  0.6 0.0 slice-start.1
  0.7 0.7 %slice-done = f32[16,256]{1,0:T(8,128)S(1)} async-done(((f32[96,256]{1,0:T(8,128)}), f32[16,256]{1,0:T(8,128)S(1)}, s32[]{:S(2)}) %slice-start) | async-done | bytes 16408 | tf_op jit(solution)/shard_map/slice | solution.py:421
  1.4 0.0 slice-done.1
  1.4 8.8 %collective-permute-start = (f32[32,256]{1,0:T(8,128)S(1)}, f32[32,256]{1,0:T(8,128)S(1)}, u32[]{:S(2)}, u32[]{:S(2)}) collective-permute-start(f32[32,256]{1,0:T(8,128)S(1)} %pad_maximum_fusion), channel_id=1, source_target_pairs={{32,0},{64,32},{96,64},{128,96},{160,128},{192,160},{224,192},{256... | collective-permute-start | bytes 98312 | tf_op jit(solution)/shard_map/ppermute | solution.py:422
  10.2 1.9 %shard_map.86 = (f32[11,112,128]{2,1,0:T(8,128)S(1)}, f32[8,128]{1,0:T(8,128)S(1)}, f32[8,128]{1,0:T(8,128)S(1)}, bf16[2,256,512]{2,1,0:T(8,128)(2,1)S(1)}, bf16...) custom-call(s32[2,1,32]{2,1,0:T(1,128)} %bitcast.7, ...), custom_call_target="tpu_custom_call" | custom-call | flops 2097152 | bytes 1048576 | tf_op jit(solution)/shard_map/pallas_call | solution.py:394
  12.1 0.0 collective-permute-done.after
  12.1 0.4 shard_map.87
  12.5 1.9 %collective-permute-start.1 = (f32[3,112,128]{2,1,0:T(8,128)S(1)}, f32[3,112,128]{2,1,0:T(8,128)S(1)}, u32[]{:S(2)}, u32[]{:S(2)}) collective-permute-start(f32[3,112,128]{2,1,0:T(8,128)S(1)} %get-tuple-element.27.down), channel_id=1, source_target_pairs={{0,31},{1,2},{2,1},{3,4},{4,3},{5,6},{6,5},{7,8},{8,7},{9,10},{10,... | collective-permute-start | bytes 516104 | tf_op jit(solution)/shard_map/ppermute | solution.py:465
  14.4 4.6 %collective-permute-start.2 = (f32[3,112,128]{2,1,0:T(8,128)S(1)}, f32[3,112,128]{2,1,0:T(8,128)S(1)}, u32[]{:S(2)}, u32[]{:S(2)}) collective-permute-start(f32[3,112,128]{2,1,0:T(8,128)S(1)} %get-tuple-element.28.up), channel_id=1, source_target_pairs={{0,1},{1,0},{2,3},{3,2},{4,5},{5,4},{6,7},{7,6},{8,9},{9,8},{10,11... | collective-permute-start | bytes 516104 | tf_op jit(solution)/shard_map/ppermute | solution.py:466
  19.1 0.0 collective-permute-done.1.below
  19.1 4.8 %collective-permute-done.2.above = f32[3,112,128]{2,1,0:T(8,128)S(1)} collective-permute-done((f32[3,112,128]{2,1,0:T(8,128)S(1)}, f32[3,112,128]{2,1,0:T(8,128)S(1)}, u32[]{:S(2)}, u32[]{:S(2)}) %collective-permute-start.2) | collective-permute-done | bytes 172064 | tf_op jit(solution)/shard_map/ppermute | solution.py:466
  23.9 1.2 %shard_map.88 = (f32[2,112,128]{2,1,0:T(8,128)S(1)}, f32[2,112,128]{2,1,0:T(8,128)S(1)}, f32[2,112,128]{2,1,0:T(8,128)S(1)}) custom-call(f32[3,112,128]{2,1,0:T(8,128)S(1)} %get-tuple-element.27.down, f32[3,112,128]{2,1,0:T(8,128)S(1)} %get-tuple-element.28.up, f32[3,112,128]{2,1,0:T(8,128)S(1)} %collective-permute-done.1.below, ...), custom_call_target="tpu_custom_call" | custom-call | bytes 1048576 | tf_op jit(solution)/shard_map/pallas_call | solution.py:394
  25.2 1.9 %collective-permute-start.4 = (f32[2,112,128]{2,1,0:T(8,128)S(1)}, f32[2,112,128]{2,1,0:T(8,128)S(1)}, u32[]{:S(2)}, u32[]{:S(2)}) collective-permute-start(f32[2,112,128]{2,1,0:T(8,128)S(1)} %get-tuple-element.42), channel_id=1, source_target_pairs={{0,1},{1,0},{2,3},{3,2},{4,5},{5,4},{6,7},{7,6},{8,9},{9,8},{10,11... | collective-permute-start | bytes 344072 | tf_op jit(solution)/shard_map/ppermute | solution.py:475
  27.1 4.6 %collective-permute-start.3 = (f32[2,112,128]{2,1,0:T(8,128)S(1)}, f32[2,112,128]{2,1,0:T(8,128)S(1)}, u32[]{:S(2)}, u32[]{:S(2)}) collective-permute-start(f32[2,112,128]{2,1,0:T(8,128)S(1)} %get-tuple-element.43), channel_id=1, source_target_pairs={{0,31},{1,2},{2,1},{3,4},{4,3},{5,6},{6,5},{7,8},{8,7},{9,10},{10,... | collective-permute-start | bytes 344072 | tf_op jit(solution)/shard_map/ppermute | solution.py:474
  31.7 0.0 collective-permute-done.4
  31.7 4.5 %collective-permute-done.3 = f32[2,112,128]{2,1,0:T(8,128)S(1)} collective-permute-done((f32[2,112,128]{2,1,0:T(8,128)S(1)}, f32[2,112,128]{2,1,0:T(8,128)S(1)}, u32[]{:S(2)}, u32[]{:S(2)}) %collective-permute-start.3) | collective-permute-done | bytes 114720 | tf_op jit(solution)/shard_map/ppermute | solution.py:474
  36.3 1.6 %shard_map.89 = (f32[2,112,128]{2,1,0:T(8,128)S(1)}, f32[2,112,128]{2,1,0:T(8,128)S(1)}, f32[2,4,8,128]{3,2,1,0:T(8,128)S(1)}, f32[16,1,128]{2,1,0:T(1,128)}) custom-call(f32[3,112,128]{2,1,0:T(8,128)S(1)} %get-tuple-element.27.down, f32[3,112,128]{2,1,0:T(8,128)S(1)} %get-tuple-element.28.up, f32[3,112,128]{2,1,0:T(8,128)S(1)} %collective-permute-done.1.below, ...), custom_call_target="tpu_custom_call" | custom-call | bytes 1048576 | tf_op jit(solution)/shard_map/pallas_call | solution.py:394
  37.9 9.3 %all-to-all-start = ((f32[16,1,128]{2,1,0:T(1,128)}), f32[16,1,128]{2,1,0:T(1,128)S(1)}, u32[]{:S(2)}, u32[]{:S(2)}) async-start(f32[16,1,128]{2,1,0:T(1,128)} %get-tuple-element.36), calls=%async_computation | async-start | bytes 16384 | tf_op jit(solution)/shard_map/all_to_all | solution.py:484
  47.2 3.5 %collective-permute-start.5 = (f32[2,4,8,128]{3,2,1,0:T(8,128)S(1)}, f32[2,4,8,128]{3,2,1,0:T(8,128)S(1)}, u32[]{:S(2)}, u32[]{:S(2)}) collective-permute-start(f32[2,4,8,128]{3,2,1,0:T(8,128)S(1)} %get-tuple-element.39), channel_id=1, source_target_pairs={{0,32},{32,64},{64,96},{96,128},{128,160},{160,192},{192,224},{224... | collective-permute-start | bytes 98312 | tf_op jit(solution)/shard_map/ppermute | solution.py:483
  50.8 3.4 %all-to-all-done = f32[16,1,128]{2,1,0:T(1,128)S(1)} async-done(((f32[16,1,128]{2,1,0:T(1,128)}), f32[16,1,128]{2,1,0:T(1,128)S(1)}, u32[]{:S(2)}, u32[]{:S(2)}) %all-to-all-start) | async-done | bytes 8224 | tf_op jit(solution)/shard_map/all_to_all | solution.py:484
  54.2 13.7 %all_to_all.10 = f32[32,1,128]{2,1,0:T(1,128)S(1)} all-to-all(f32[32,1,128]{2,1,0:T(1,128)S(1)} %broadcast_in_dim.2), channel_id=1, replica_groups=mesh['tm'=16,'space'=32] {'space'}, dimensions={0} | all-to-all | bytes 32768 | tf_op jit(solution)/shard_map/all_to_all | solution.py:487
  67.9 0.0 collective-permute-done.5.back
  67.9 0.9 %shard_map.90 = (f32[96,256]{1,0:T(8,128)}, f32[96,256]{1,0:T(8,128)}) custom-call(f32[8,128]{1,0:T(8,128)S(1)} %get-tuple-element.21.flag, f32[1,128]{1,0:T(1,128)S(1)} %bitcast.4, f32[3,112,128]{2,1,0:T(8,128)S(1)} %get-tuple-element.27.down, f32[3,112,128]{2,1,0:T(8,128)S(1)} %get-tuple-element.28.up, f32[2,112,128]{2,1,0:T(8,128)S(1)} %get-tuple-element.32.one, ...), custom_call_target="tpu_custom_call" | custom-call | bytes 1048576 | tf_op jit(solution)/shard_map/pallas_call | solution.py:394
  (6 shorter events, 0.1 us)
Async XLA Ops:
  0.6 0.7 %slice-start = ((f32[96,256]{1,0:T(8,128)}), f32[16,256]{1,0:T(8,128)S(1)}, s32[]{:S(2)}) async-start(f32[96,256]{1,0:T(8,128)} %right_hbm.1), calls=%async_computation.2 | async-start | bytes 32768 | tf_op jit(solution)/shard_map/slice | solution.py:421
  0.6 0.7 %slice-start.1 = ((f32[96,256]{1,0:T(8,128)}), f32[16,256]{1,0:T(8,128)S(1)}, s32[]{:S(2)}) async-start(f32[96,256]{1,0:T(8,128)} %obs_hbm.1), calls=%async_computation.3 | async-start | bytes 32768 | tf_op jit(solution)/shard_map/slice | solution.py:421
  1.4 10.7 %collective-permute-start = (f32[32,256]{1,0:T(8,128)S(1)}, f32[32,256]{1,0:T(8,128)S(1)}, u32[]{:S(2)}, u32[]{:S(2)}) collective-permute-start(f32[32,256]{1,0:T(8,128)S(1)} %pad_maximum_fusion), channel_id=1, source_target_pairs={{32,0},{64,32},{96,64},{128,96},{160,128},{192,160},{224,192},{256... | collective-permute-start | bytes 98312 | tf_op jit(solution)/shard_map/ppermute | solution.py:422
  12.5 6.5 %collective-permute-start.1 = (f32[3,112,128]{2,1,0:T(8,128)S(1)}, f32[3,112,128]{2,1,0:T(8,128)S(1)}, u32[]{:S(2)}, u32[]{:S(2)}) collective-permute-start(f32[3,112,128]{2,1,0:T(8,128)S(1)} %get-tuple-element.27.down), channel_id=1, source_target_pairs={{0,31},{1,2},{2,1},{3,4},{4,3},{5,6},{6,5},{7,8},{8,7},{9,10},{10,... | collective-permute-start | bytes 516104 | tf_op jit(solution)/shard_map/ppermute | solution.py:465
  14.4 9.5 %collective-permute-start.2 = (f32[3,112,128]{2,1,0:T(8,128)S(1)}, f32[3,112,128]{2,1,0:T(8,128)S(1)}, u32[]{:S(2)}, u32[]{:S(2)}) collective-permute-start(f32[3,112,128]{2,1,0:T(8,128)S(1)} %get-tuple-element.28.up), channel_id=1, source_target_pairs={{0,1},{1,0},{2,3},{3,2},{4,5},{5,4},{6,7},{7,6},{8,9},{9,8},{10,11... | collective-permute-start | bytes 516104 | tf_op jit(solution)/shard_map/ppermute | solution.py:466
  25.2 6.5 %collective-permute-start.4 = (f32[2,112,128]{2,1,0:T(8,128)S(1)}, f32[2,112,128]{2,1,0:T(8,128)S(1)}, u32[]{:S(2)}, u32[]{:S(2)}) collective-permute-start(f32[2,112,128]{2,1,0:T(8,128)S(1)} %get-tuple-element.42), channel_id=1, source_target_pairs={{0,1},{1,0},{2,3},{3,2},{4,5},{5,4},{6,7},{7,6},{8,9},{9,8},{10,11... | collective-permute-start | bytes 344072 | tf_op jit(solution)/shard_map/ppermute | solution.py:475
  27.1 9.2 %collective-permute-start.3 = (f32[2,112,128]{2,1,0:T(8,128)S(1)}, f32[2,112,128]{2,1,0:T(8,128)S(1)}, u32[]{:S(2)}, u32[]{:S(2)}) collective-permute-start(f32[2,112,128]{2,1,0:T(8,128)S(1)} %get-tuple-element.43), channel_id=1, source_target_pairs={{0,31},{1,2},{2,1},{3,4},{4,3},{5,6},{6,5},{7,8},{8,7},{9,10},{10,... | collective-permute-start | bytes 344072 | tf_op jit(solution)/shard_map/ppermute | solution.py:474
  37.9 16.2 %all-to-all-start = ((f32[16,1,128]{2,1,0:T(1,128)}), f32[16,1,128]{2,1,0:T(1,128)S(1)}, u32[]{:S(2)}, u32[]{:S(2)}) async-start(f32[16,1,128]{2,1,0:T(1,128)} %get-tuple-element.36), calls=%async_computation | async-start | bytes 16384 | tf_op jit(solution)/shard_map/all_to_all | solution.py:484
  47.2 20.7 %collective-permute-start.5 = (f32[2,4,8,128]{3,2,1,0:T(8,128)S(1)}, f32[2,4,8,128]{3,2,1,0:T(8,128)S(1)}, u32[]{:S(2)}, u32[]{:S(2)}) collective-permute-start(f32[2,4,8,128]{3,2,1,0:T(8,128)S(1)} %get-tuple-element.39), channel_id=1, source_target_pairs={{0,32},{32,64},{64,96},{96,128},{128,160},{160,192},{192,224},{224... | collective-permute-start | bytes 98312 | tf_op jit(solution)/shard_map/ppermute | solution.py:483
